TPU v7x, 32 devices: a whole 2x2x4 slice. The times are simulated.
32 devices in a mesh: gz: 16 (over z, y, core), gx: 2 (over x).
Axes of the slice: x: 2, y: 2, z: 4, core: 2. Of those that a mesh axis runs over, the one named last changes fastest.
Arguments:
- electric_x: float32 [128, 128, 128], P('gz', 'gx'), may hold values from -6 to 6
- electric_y: float32 [128, 128, 128], P('gz', 'gx'), may hold values from -6 to 6
- electric_s: float32 [128, 128, 128], P('gz', 'gx'), may hold values from -6 to 6
- magnetic_x: float32 [128, 128, 128], P('gz', 'gx'), may hold values from -6 to 6
- magnetic_y: float32 [128, 128, 128], P('gz', 'gx'), may hold values from -6 to 6
- magnetic_s: float32 [128, 128, 128], P('gz', 'gx'), may hold values from -6 to 6
- bunch_profile: int32 [128, 128, 128], P('gz', 'gx'), may hold values from 0 to 7
- cell_codes: int32 [128, 128, 128], P('gz', 'gx'), may hold values from 0 to 7
- shift_counts: int32 [3], replicated, may hold values from 0 to 1, as said below
Outputs:
- out_electric_x: float32 [128, 128, 128], P('gz', 'gx')
- out_electric_y: float32 [128, 128, 128], P('gz', 'gx')
- out_electric_s: float32 [128, 128, 128], P('gz', 'gx')
- out_magnetic_x: float32 [128, 128, 128], P('gz', 'gx')
- out_magnetic_y: float32 [128, 128, 128], P('gz', 'gx')
- out_magnetic_s: float32 [128, 128, 128], P('gz', 'gx')
Inputs may be any that keep to these rules, and one draw needn't show every extreme that they name: `shift_counts`: each entry is 0 or 1; some entry is 1 and some entry is 0.
All inputs are finite; a program needn't handle non-finite values.
Results may differ from a plain program's by a relative error of at most 0.00002.
Values sent between devices are 32-bit elements; how exact they have to be, the bound alone decides.
No kernel may reach another device: no remote copies, remote signals or barrier semaphores. Data moves between devices by JAX's collectives and lax.ppermute only.
A program may use at most 64 MiB of HBM per device.

v0:
```python
import jax
import jax.numpy as jnp
from jax import lax
from jax.sharding import PartitionSpec as P

STEPS = 3


time_step = 0.5
current_scale = 0.1


def passed_along(block, axis, distance):
    devices = range(lax.axis_size(axis))
    route = [(i - distance, i) for i in devices if i - distance in devices]
    return lax.ppermute(block, axis, route)


def forward_z(values, upper_plane):
    return jnp.concatenate([values[1:], upper_plane[None]], 0) - values


def backward_z(values, lower_plane):
    return values - jnp.concatenate([lower_plane[None], values[:-1]], 0)


def forward_x(values, right_column):
    return jnp.concatenate([values[:, 1:], right_column[:, None]], 1) - values


def backward_x(values, left_column):
    return values - jnp.concatenate([left_column[:, None], values[:, :-1]], 1)


def forward_y(values):
    return jnp.concatenate([values[:, :, 1:], jnp.zeros_like(values[:, :, :1])], 2) - values


def backward_y(values):
    return values - jnp.concatenate([jnp.zeros_like(values[:, :, :1]), values[:, :, :-1]], 2)


def moved_field(values, next_plane, shift_now):
    moved = jnp.concatenate([values[1:], next_plane[None]], 0)
    return jnp.where(shift_now == 1, moved, values)


def coefficients(cell_codes):
    keep = jnp.where(
        cell_codes == 5,
        0.0,
        jnp.where(cell_codes == 6, 0.8 / 1.2, jnp.where(cell_codes == 7, 0.4 / 1.6, 1.0)),
    )
    gain = jnp.where(
        cell_codes == 5,
        0.0,
        jnp.where(
            cell_codes == 6, time_step / 1.2, jnp.where(cell_codes == 7, time_step / 1.6, time_step)
        ),
    )
    return (keep.astype(jnp.float32), gain.astype(jnp.float32))


def on_device(
    electric_x,
    electric_y,
    electric_s,
    magnetic_x,
    magnetic_y,
    magnetic_s,
    bunch_profile,
    cell_codes,
    shift_counts,
):
    width_x = electric_x.shape[1]
    total_x = width_x * lax.axis_size("gx")
    radius = 2 * total_x
    start = lax.axis_index("gx") * width_x
    places = (start + jnp.arange(-1, width_x + 1)).astype(jnp.float32)
    whole_ext = 1.0 + (places - total_x / 2) / radius
    half_ext = 1.0 + (places + 0.5 - total_x / 2) / radius
    scale_whole = whole_ext[1:-1][None, :, None]
    scale_half = half_ext[1:-1][None, :, None]
    whole_right = whole_ext[1:][None, :, None]
    half_left = half_ext[:-1][None, :, None]
    keep, gain = coefficients(cell_codes)
    current = current_scale * bunch_profile.astype(jnp.float32)
    for step_index in range(STEPS):
        shift_now = shift_counts[step_index]
        planes = jnp.stack(
            [
                electric_x[0],
                electric_y[0],
                electric_s[0],
                magnetic_x[0],
                magnetic_y[0],
                magnetic_s[0],
            ]
        )
        above = passed_along(planes, "gz", -1)
        electric_x = moved_field(electric_x, above[0], shift_now)
        electric_y = moved_field(electric_y, above[1], shift_now)
        electric_s = moved_field(electric_s, above[2], shift_now)
        magnetic_x = moved_field(magnetic_x, above[3], shift_now)
        magnetic_y = moved_field(magnetic_y, above[4], shift_now)
        magnetic_s = moved_field(magnetic_s, above[5], shift_now)
        faces_up = passed_along(jnp.stack([electric_x[0], electric_y[0]]), "gz", -1)
        upper_x = faces_up[0]
        upper_y = faces_up[1]
        right = passed_along(jnp.stack([electric_y[:, 0, :], electric_s[:, 0, :]]), "gx", -1)
        weighted_s = whole_right * jnp.concatenate([electric_s, right[1][:, None]], 1)
        magnetic_x = magnetic_x - time_step * (
            forward_y(electric_s) - forward_z(electric_y, upper_y) / scale_whole
        )
        magnetic_y = (
            magnetic_y
            - time_step
            * (forward_z(electric_x, upper_x) - (weighted_s[:, 1:] - weighted_s[:, :-1]))
            / scale_half
        )
        magnetic_s = magnetic_s - time_step * (
            forward_x(electric_y, right[0]) - forward_y(electric_x)
        )
        lower = passed_along(jnp.stack([magnetic_x[-1], magnetic_y[-1]]), "gz", 1)
        left = passed_along(jnp.stack([magnetic_y[:, -1, :], magnetic_s[:, -1, :]]), "gx", 1)
        weighted_m = half_left * jnp.concatenate([left[1][:, None], magnetic_s], 1)
        electric_x = keep * electric_x + gain * (
            backward_y(magnetic_s) - backward_z(magnetic_y, lower[1]) / scale_half
        )
        electric_y = (
            keep * electric_y
            + gain
            * (backward_z(magnetic_x, lower[0]) - (weighted_m[:, 1:] - weighted_m[:, :-1]))
            / scale_whole
        )
        electric_s = keep * electric_s + gain * (
            backward_x(magnetic_y, left[0]) - backward_y(magnetic_x) - current
        )
    return (electric_x, electric_y, electric_s, magnetic_x, magnetic_y, magnetic_s)


def solution(mesh):
    placed = (
        P("gz", "gx", None),
        P("gz", "gx", None),
        P("gz", "gx", None),
        P("gz", "gx", None),
        P("gz", "gx", None),
        P("gz", "gx", None),
        P("gz", "gx", None),
        P("gz", "gx", None),
        P(),
    )
    return jax.shard_map(
        on_device,
        mesh=mesh,
        in_specs=placed,
        out_specs=(
            P("gz", "gx", None),
            P("gz", "gx", None),
            P("gz", "gx", None),
            P("gz", "gx", None),
            P("gz", "gx", None),
            P("gz", "gx", None),
        ),
        check_vma=False,
    )
```

profile of v0, /device:TPU:8, one launch (start us, length us, event | category | flops | bytes accessed | tf_op | source)
XLA Modules:
  0.0 88.6 jit_solution(12271017267750029818)
XLA Ops:
  4.5 2.8 %collective-permute-start = (f32[6,64,128]{2,1,0:T(8,128)S(1)}, f32[6,64,128]{2,1,0:T(8,128)S(1)}, u32[]{:S(2)}, u32[]{:S(2)}) collective-permute-start(f32[6,64,128]{2,1,0:T(8,128)S(1)} %constant_dynamic-update-slice_fusion), channel_id=1, source_target_pairs={{2,0},{4,2},{6,4},{8,6},{10,8},{12,10},{14,12},{16,14},{18,16},{20... | collective-permute-start | bytes 589832 | tf_op jit(solution)/shard_map/ppermute | solution.py:16
  9.2 1.3 %collective-permute-done = f32[6,64,128]{2,1,0:T(8,128)S(1)} collective-permute-done((f32[6,64,128]{2,1,0:T(8,128)S(1)}, f32[6,64,128]{2,1,0:T(8,128)S(1)}, u32[]{:S(2)}, u32[]{:S(2)}) %collective-permute-start) | collective-permute-done | bytes 196640 | tf_op jit(solution)/shard_map/ppermute | solution.py:16
  11.6 1.3 %collective-permute-start.1 = (f32[2,8,128]{2,1,0:T(8,128)S(1)}, f32[2,8,128]{2,1,0:T(8,128)S(1)}, u32[]{:S(2)}, u32[]{:S(2)}) collective-permute-start(f32[2,8,128]{2,1,0:T(8,128)S(1)} %pad_maximum_fusion.6), channel_id=1, source_target_pairs={{1,0},{3,2},{5,4},{7,6},{9,8},{11,10},{13,12},{15,14},{17,16},{19,... | collective-permute-start | bytes 24584 | tf_op jit(solution)/shard_map/ppermute | solution.py:16
  13.2 4.7 %collective-permute-start.2 = (f32[2,64,128]{2,1,0:T(8,128)S(1)}, f32[2,64,128]{2,1,0:T(8,128)S(1)}, u32[]{:S(2)}, u32[]{:S(2)}) collective-permute-start(f32[2,64,128]{2,1,0:T(8,128)S(1)} %pad_maximum_fusion), channel_id=1, source_target_pairs={{2,0},{4,2},{6,4},{8,6},{10,8},{12,10},{14,12},{16,14},{18,16},{20... | collective-permute-start | bytes 196616 | tf_op jit(solution)/shard_map/ppermute | solution.py:16
  18.1 1.7 %collective-permute-done.2 = f32[2,64,128]{2,1,0:T(8,128)S(1)} collective-permute-done((f32[2,64,128]{2,1,0:T(8,128)S(1)}, f32[2,64,128]{2,1,0:T(8,128)S(1)}, u32[]{:S(2)}, u32[]{:S(2)}) %collective-permute-start.2) | collective-permute-done | bytes 65568 | tf_op jit(solution)/shard_map/ppermute | solution.py:16
  21.5 4.3 %collective-permute-start.4 = (f32[2,8,128]{2,1,0:T(8,128)S(1)}, f32[2,8,128]{2,1,0:T(8,128)S(1)}, u32[]{:S(2)}, u32[]{:S(2)}) collective-permute-start(f32[2,8,128]{2,1,0:T(8,128)S(1)} %pad_maximum_fusion.7), channel_id=1, source_target_pairs={{0,1},{2,3},{4,5},{6,7},{8,9},{10,11},{12,13},{14,15},{16,17},{18,... | collective-permute-start | bytes 24584 | tf_op jit(solution)/shard_map/ppermute | solution.py:16
  25.7 1.9 %collective-permute-start.3 = (f32[2,64,128]{2,1,0:T(8,128)S(1)}, f32[2,64,128]{2,1,0:T(8,128)S(1)}, u32[]{:S(2)}, u32[]{:S(2)}) collective-permute-start(f32[2,64,128]{2,1,0:T(8,128)S(1)} %pad_maximum_fusion.1), channel_id=1, source_target_pairs={{0,2},{2,4},{4,6},{6,8},{8,10},{10,12},{12,14},{14,16},{16,18},{18... | collective-permute-start | bytes 196616 | tf_op jit(solution)/shard_map/ppermute | solution.py:16
  27.8 4.4 %collective-permute-done.3 = f32[2,64,128]{2,1,0:T(8,128)S(1)} collective-permute-done((f32[2,64,128]{2,1,0:T(8,128)S(1)}, f32[2,64,128]{2,1,0:T(8,128)S(1)}, u32[]{:S(2)}, u32[]{:S(2)}) %collective-permute-start.3) | collective-permute-done | bytes 65568 | tf_op jit(solution)/shard_map/ppermute | solution.py:16
  33.6 1.9 %collective-permute-start.5 = (f32[6,64,128]{2,1,0:T(8,128)S(1)}, f32[6,64,128]{2,1,0:T(8,128)S(1)}, u32[]{:S(2)}, u32[]{:S(2)}) collective-permute-start(f32[6,64,128]{2,1,0:T(8,128)S(1)} %constant_dynamic-update-slice_fusion.6), channel_id=1, source_target_pairs={{2,0},{4,2},{6,4},{8,6},{10,8},{12,10},{14,12},{16,14},{18,16},{20... | collective-permute-start | bytes 589832 | tf_op jit(solution)/shard_map/ppermute | solution.py:16
  36.3 2.4 %collective-permute-done.5 = f32[6,64,128]{2,1,0:T(8,128)S(1)} collective-permute-done((f32[6,64,128]{2,1,0:T(8,128)S(1)}, f32[6,64,128]{2,1,0:T(8,128)S(1)}, u32[]{:S(2)}, u32[]{:S(2)}) %collective-permute-start.5) | collective-permute-done | bytes 196640 | tf_op jit(solution)/shard_map/ppermute | solution.py:16
  38.9 1.3 %collective-permute-start.6 = (f32[2,8,128]{2,1,0:T(8,128)S(1)}, f32[2,8,128]{2,1,0:T(8,128)S(1)}, u32[]{:S(2)}, u32[]{:S(2)}) collective-permute-start(f32[2,8,128]{2,1,0:T(8,128)S(1)} %pad_maximum_fusion.8), channel_id=1, source_target_pairs={{1,0},{3,2},{5,4},{7,6},{9,8},{11,10},{13,12},{15,14},{17,16},{19,... | collective-permute-start | bytes 24584 | tf_op jit(solution)/shard_map/ppermute | solution.py:16
  41.1 4.7 %collective-permute-start.7 = (f32[2,64,128]{2,1,0:T(8,128)S(1)}, f32[2,64,128]{2,1,0:T(8,128)S(1)}, u32[]{:S(2)}, u32[]{:S(2)}) collective-permute-start(f32[2,64,128]{2,1,0:T(8,128)S(1)} %pad_maximum_fusion.2), channel_id=1, source_target_pairs={{2,0},{4,2},{6,4},{8,6},{10,8},{12,10},{14,12},{16,14},{18,16},{20... | collective-permute-start | bytes 196616 | tf_op jit(solution)/shard_map/ppermute | solution.py:16
  46.0 1.7 %collective-permute-done.7 = f32[2,64,128]{2,1,0:T(8,128)S(1)} collective-permute-done((f32[2,64,128]{2,1,0:T(8,128)S(1)}, f32[2,64,128]{2,1,0:T(8,128)S(1)}, u32[]{:S(2)}, u32[]{:S(2)}) %collective-permute-start.7) | collective-permute-done | bytes 65568 | tf_op jit(solution)/shard_map/ppermute | solution.py:16
  49.2 4.3 %collective-permute-start.9 = (f32[2,8,128]{2,1,0:T(8,128)S(1)}, f32[2,8,128]{2,1,0:T(8,128)S(1)}, u32[]{:S(2)}, u32[]{:S(2)}) collective-permute-start(f32[2,8,128]{2,1,0:T(8,128)S(1)} %pad_maximum_fusion.9), channel_id=1, source_target_pairs={{0,1},{2,3},{4,5},{6,7},{8,9},{10,11},{12,13},{14,15},{16,17},{18,... | collective-permute-start | bytes 24584 | tf_op jit(solution)/shard_map/ppermute | solution.py:16
  53.5 1.9 %collective-permute-start.8 = (f32[2,64,128]{2,1,0:T(8,128)S(1)}, f32[2,64,128]{2,1,0:T(8,128)S(1)}, u32[]{:S(2)}, u32[]{:S(2)}) collective-permute-start(f32[2,64,128]{2,1,0:T(8,128)S(1)} %pad_maximum_fusion.3), channel_id=1, source_target_pairs={{0,2},{2,4},{4,6},{6,8},{8,10},{10,12},{12,14},{14,16},{16,18},{18... | collective-permute-start | bytes 196616 | tf_op jit(solution)/shard_map/ppermute | solution.py:16
  55.6 4.4 %collective-permute-done.8 = f32[2,64,128]{2,1,0:T(8,128)S(1)} collective-permute-done((f32[2,64,128]{2,1,0:T(8,128)S(1)}, f32[2,64,128]{2,1,0:T(8,128)S(1)}, u32[]{:S(2)}, u32[]{:S(2)}) %collective-permute-start.8) | collective-permute-done | bytes 65568 | tf_op jit(solution)/shard_map/ppermute | solution.py:16
  60.6 1.9 %collective-permute-start.10 = (f32[6,64,128]{2,1,0:T(8,128)S(1)}, f32[6,64,128]{2,1,0:T(8,128)S(1)}, u32[]{:S(2)}, u32[]{:S(2)}) collective-permute-start(f32[6,64,128]{2,1,0:T(8,128)S(1)} %constant_dynamic-update-slice_fusion.12), channel_id=1, source_target_pairs={{2,0},{4,2},{6,4},{8,6},{10,8},{12,10},{14,12},{16,14},{18,16},{20... | collective-permute-start | bytes 589832 | tf_op jit(solution)/shard_map/ppermute | solution.py:16
  63.3 2.4 %collective-permute-done.10 = f32[6,64,128]{2,1,0:T(8,128)S(1)} collective-permute-done((f32[6,64,128]{2,1,0:T(8,128)S(1)}, f32[6,64,128]{2,1,0:T(8,128)S(1)}, u32[]{:S(2)}, u32[]{:S(2)}) %collective-permute-start.10) | collective-permute-done | bytes 196640 | tf_op jit(solution)/shard_map/ppermute | solution.py:16
  66.9 1.3 %collective-permute-start.11 = (f32[2,8,128]{2,1,0:T(8,128)S(1)}, f32[2,8,128]{2,1,0:T(8,128)S(1)}, u32[]{:S(2)}, u32[]{:S(2)}) collective-permute-start(f32[2,8,128]{2,1,0:T(8,128)S(1)} %pad_maximum_fusion.10), channel_id=1, source_target_pairs={{1,0},{3,2},{5,4},{7,6},{9,8},{11,10},{13,12},{15,14},{17,16},{19,... | collective-permute-start | bytes 24584 | tf_op jit(solution)/shard_map/ppermute | solution.py:16
  68.5 4.7 %collective-permute-start.12 = (f32[2,64,128]{2,1,0:T(8,128)S(1)}, f32[2,64,128]{2,1,0:T(8,128)S(1)}, u32[]{:S(2)}, u32[]{:S(2)}) collective-permute-start(f32[2,64,128]{2,1,0:T(8,128)S(1)} %pad_maximum_fusion.4), channel_id=1, source_target_pairs={{2,0},{4,2},{6,4},{8,6},{10,8},{12,10},{14,12},{16,14},{18,16},{20... | collective-permute-start | bytes 196616 | tf_op jit(solution)/shard_map/ppermute | solution.py:16
  73.4 1.7 %collective-permute-done.12 = f32[2,64,128]{2,1,0:T(8,128)S(1)} collective-permute-done((f32[2,64,128]{2,1,0:T(8,128)S(1)}, f32[2,64,128]{2,1,0:T(8,128)S(1)}, u32[]{:S(2)}, u32[]{:S(2)}) %collective-permute-start.12) | collective-permute-done | bytes 65568 | tf_op jit(solution)/shard_map/ppermute | solution.py:16
  75.5 4.3 %collective-permute-start.14 = (f32[2,8,128]{2,1,0:T(8,128)S(1)}, f32[2,8,128]{2,1,0:T(8,128)S(1)}, u32[]{:S(2)}, u32[]{:S(2)}) collective-permute-start(f32[2,8,128]{2,1,0:T(8,128)S(1)} %pad_maximum_fusion.11), channel_id=1, source_target_pairs={{0,1},{2,3},{4,5},{6,7},{8,9},{10,11},{12,13},{14,15},{16,17},{18,... | collective-permute-start | bytes 24584 | tf_op jit(solution)/shard_map/ppermute | solution.py:16
  80.1 1.9 %collective-permute-start.13 = (f32[2,64,128]{2,1,0:T(8,128)S(1)}, f32[2,64,128]{2,1,0:T(8,128)S(1)}, u32[]{:S(2)}, u32[]{:S(2)}) collective-permute-start(f32[2,64,128]{2,1,0:T(8,128)S(1)} %pad_maximum_fusion.5), channel_id=1, source_target_pairs={{0,2},{2,4},{4,6},{6,8},{8,10},{10,12},{12,14},{14,16},{16,18},{18... | collective-permute-start | bytes 196616 | tf_op jit(solution)/shard_map/ppermute | solution.py:16
  82.1 4.4 %collective-permute-done.13 = f32[2,64,128]{2,1,0:T(8,128)S(1)} collective-permute-done((f32[2,64,128]{2,1,0:T(8,128)S(1)}, f32[2,64,128]{2,1,0:T(8,128)S(1)}, u32[]{:S(2)}, u32[]{:S(2)}) %collective-permute-start.13) | collective-permute-done | bytes 65568 | tf_op jit(solution)/shard_map/ppermute | solution.py:16
  (192 shorter events, 17.0 us)
Async XLA Ops:
  0.6 3.9 %copy-start.14 = (f32[8,64,128]{2,1,0:T(8,128)S(1)}, f32[8,64,128]{2,1,0:T(8,128)}, u32[]{:S(2)}) copy-start(f32[8,64,128]{2,1,0:T(8,128)} %param.14) | copy-start | bytes 786436
  4.5 5.9 %collective-permute-start = (f32[6,64,128]{2,1,0:T(8,128)S(1)}, f32[6,64,128]{2,1,0:T(8,128)S(1)}, u32[]{:S(2)}, u32[]{:S(2)}) collective-permute-start(f32[6,64,128]{2,1,0:T(8,128)S(1)} %constant_dynamic-update-slice_fusion), channel_id=1, source_target_pairs={{2,0},{4,2},{6,4},{8,6},{10,8},{12,10},{14,12},{16,14},{18,16},{20... | collective-permute-start | bytes 589832 | tf_op jit(solution)/shard_map/ppermute | solution.py:16
  7.3 3.2 %copy-start.16 = (f32[8,64,128]{2,1,0:T(8,128)S(1)}, f32[8,64,128]{2,1,0:T(8,128)}, u32[]{:S(2)}) copy-start(f32[8,64,128]{2,1,0:T(8,128)} %param.10) | copy-start | bytes 786436
  7.5 3.0 %slice-start.8 = ((f32[8,64,128]{2,1,0:T(8,128)}), f32[7,64,128]{2,1,0:T(8,128)S(1)}, s32[]{:S(2)}) async-start(f32[8,64,128]{2,1,0:T(8,128)} %param.10), calls=%async_computation.8 | async-start | bytes 458752 | tf_op jit(solution)/shard_map/slice | solution.py:44
  7.5 3.0 %slice-start.7 = ((f32[8,64,128]{2,1,0:T(8,128)}), f32[7,64,128]{2,1,0:T(8,128)S(1)}, s32[]{:S(2)}) async-start(f32[8,64,128]{2,1,0:T(8,128)} %param.9), calls=%async_computation.7 | async-start | bytes 458752 | tf_op jit(solution)/shard_map/slice | solution.py:44
  11.6 6.4 %collective-permute-start.1 = (f32[2,8,128]{2,1,0:T(8,128)S(1)}, f32[2,8,128]{2,1,0:T(8,128)S(1)}, u32[]{:S(2)}, u32[]{:S(2)}) collective-permute-start(f32[2,8,128]{2,1,0:T(8,128)S(1)} %pad_maximum_fusion.6), channel_id=1, source_target_pairs={{1,0},{3,2},{5,4},{7,6},{9,8},{11,10},{13,12},{15,14},{17,16},{19,... | collective-permute-start | bytes 24584 | tf_op jit(solution)/shard_map/ppermute | solution.py:16
  13.2 6.6 %collective-permute-start.2 = (f32[2,64,128]{2,1,0:T(8,128)S(1)}, f32[2,64,128]{2,1,0:T(8,128)S(1)}, u32[]{:S(2)}, u32[]{:S(2)}) collective-permute-start(f32[2,64,128]{2,1,0:T(8,128)S(1)} %pad_maximum_fusion), channel_id=1, source_target_pairs={{2,0},{4,2},{6,4},{8,6},{10,8},{12,10},{14,12},{16,14},{18,16},{20... | collective-permute-start | bytes 196616 | tf_op jit(solution)/shard_map/ppermute | solution.py:16
  21.5 6.2 %collective-permute-start.4 = (f32[2,8,128]{2,1,0:T(8,128)S(1)}, f32[2,8,128]{2,1,0:T(8,128)S(1)}, u32[]{:S(2)}, u32[]{:S(2)}) collective-permute-start(f32[2,8,128]{2,1,0:T(8,128)S(1)} %pad_maximum_fusion.7), channel_id=1, source_target_pairs={{0,1},{2,3},{4,5},{6,7},{8,9},{10,11},{12,13},{14,15},{16,17},{18,... | collective-permute-start | bytes 24584 | tf_op jit(solution)/shard_map/ppermute | solution.py:16
  25.7 6.5 %collective-permute-start.3 = (f32[2,64,128]{2,1,0:T(8,128)S(1)}, f32[2,64,128]{2,1,0:T(8,128)S(1)}, u32[]{:S(2)}, u32[]{:S(2)}) collective-permute-start(f32[2,64,128]{2,1,0:T(8,128)S(1)} %pad_maximum_fusion.1), channel_id=1, source_target_pairs={{0,2},{2,4},{4,6},{6,8},{8,10},{10,12},{12,14},{14,16},{16,18},{18... | collective-permute-start | bytes 196616 | tf_op jit(solution)/shard_map/ppermute | solution.py:16
  27.7 4.5 %copy-start.18 = (s32[8,64,128]{2,1,0:T(8,128)S(1)}, s32[8,64,128]{2,1,0:T(8,128)}, u32[]{:S(2)}) copy-start(s32[8,64,128]{2,1,0:T(8,128)} %param.16) | copy-start | bytes 786436
  33.6 5.1 %collective-permute-start.5 = (f32[6,64,128]{2,1,0:T(8,128)S(1)}, f32[6,64,128]{2,1,0:T(8,128)S(1)}, u32[]{:S(2)}, u32[]{:S(2)}) collective-permute-start(f32[6,64,128]{2,1,0:T(8,128)S(1)} %constant_dynamic-update-slice_fusion.6), channel_id=1, source_target_pairs={{2,0},{4,2},{6,4},{8,6},{10,8},{12,10},{14,12},{16,14},{18,16},{20... | collective-permute-start | bytes 589832 | tf_op jit(solution)/shard_map/ppermute | solution.py:16
  38.9 6.9 %collective-permute-start.6 = (f32[2,8,128]{2,1,0:T(8,128)S(1)}, f32[2,8,128]{2,1,0:T(8,128)S(1)}, u32[]{:S(2)}, u32[]{:S(2)}) collective-permute-start(f32[2,8,128]{2,1,0:T(8,128)S(1)} %pad_maximum_fusion.8), channel_id=1, source_target_pairs={{1,0},{3,2},{5,4},{7,6},{9,8},{11,10},{13,12},{15,14},{17,16},{19,... | collective-permute-start | bytes 24584 | tf_op jit(solution)/shard_map/ppermute | solution.py:16
  41.1 6.6 %collective-permute-start.7 = (f32[2,64,128]{2,1,0:T(8,128)S(1)}, f32[2,64,128]{2,1,0:T(8,128)S(1)}, u32[]{:S(2)}, u32[]{:S(2)}) collective-permute-start(f32[2,64,128]{2,1,0:T(8,128)S(1)} %pad_maximum_fusion.2), channel_id=1, source_target_pairs={{2,0},{4,2},{6,4},{8,6},{10,8},{12,10},{14,12},{16,14},{18,16},{20... | collective-permute-start | bytes 196616 | tf_op jit(solution)/shard_map/ppermute | solution.py:16
  49.2 6.2 %collective-permute-start.9 = (f32[2,8,128]{2,1,0:T(8,128)S(1)}, f32[2,8,128]{2,1,0:T(8,128)S(1)}, u32[]{:S(2)}, u32[]{:S(2)}) collective-permute-start(f32[2,8,128]{2,1,0:T(8,128)S(1)} %pad_maximum_fusion.9), channel_id=1, source_target_pairs={{0,1},{2,3},{4,5},{6,7},{8,9},{10,11},{12,13},{14,15},{16,17},{18,... | collective-permute-start | bytes 24584 | tf_op jit(solution)/shard_map/ppermute | solution.py:16
  53.5 6.5 %collective-permute-start.8 = (f32[2,64,128]{2,1,0:T(8,128)S(1)}, f32[2,64,128]{2,1,0:T(8,128)S(1)}, u32[]{:S(2)}, u32[]{:S(2)}) collective-permute-start(f32[2,64,128]{2,1,0:T(8,128)S(1)} %pad_maximum_fusion.3), channel_id=1, source_target_pairs={{0,2},{2,4},{4,6},{6,8},{8,10},{10,12},{12,14},{14,16},{16,18},{18... | collective-permute-start | bytes 196616 | tf_op jit(solution)/shard_map/ppermute | solution.py:16
  60.2 3.0 %copy-start.9 = (f32[8,64,128]{2,1,0:T(8,128)}, f32[8,64,128]{2,1,0:T(8,128)S(1)}, u32[]{:S(2)}) copy-start(f32[8,64,128]{2,1,0:T(8,128)S(1)} %fusion.49) | copy-start | bytes 786436
  60.6 5.1 %collective-permute-start.10 = (f32[6,64,128]{2,1,0:T(8,128)S(1)}, f32[6,64,128]{2,1,0:T(8,128)S(1)}, u32[]{:S(2)}, u32[]{:S(2)}) collective-permute-start(f32[6,64,128]{2,1,0:T(8,128)S(1)} %constant_dynamic-update-slice_fusion.12), channel_id=1, source_target_pairs={{2,0},{4,2},{6,4},{8,6},{10,8},{12,10},{14,12},{16,14},{18,16},{20... | collective-permute-start | bytes 589832 | tf_op jit(solution)/shard_map/ppermute | solution.py:16
  66.9 6.4 %collective-permute-start.11 = (f32[2,8,128]{2,1,0:T(8,128)S(1)}, f32[2,8,128]{2,1,0:T(8,128)S(1)}, u32[]{:S(2)}, u32[]{:S(2)}) collective-permute-start(f32[2,8,128]{2,1,0:T(8,128)S(1)} %pad_maximum_fusion.10), channel_id=1, source_target_pairs={{1,0},{3,2},{5,4},{7,6},{9,8},{11,10},{13,12},{15,14},{17,16},{19,... | collective-permute-start | bytes 24584 | tf_op jit(solution)/shard_map/ppermute | solution.py:16
  68.5 6.6 %collective-permute-start.12 = (f32[2,64,128]{2,1,0:T(8,128)S(1)}, f32[2,64,128]{2,1,0:T(8,128)S(1)}, u32[]{:S(2)}, u32[]{:S(2)}) collective-permute-start(f32[2,64,128]{2,1,0:T(8,128)S(1)} %pad_maximum_fusion.4), channel_id=1, source_target_pairs={{2,0},{4,2},{6,4},{8,6},{10,8},{12,10},{14,12},{16,14},{18,16},{20... | collective-permute-start | bytes 196616 | tf_op jit(solution)/shard_map/ppermute | solution.py:16
  75.4 11.1 %copy-start.7 = (f32[8,64,128]{2,1,0:T(8,128)}, f32[8,64,128]{2,1,0:T(8,128)S(1)}, u32[]{:S(2)}) copy-start(f32[8,64,128]{2,1,0:T(8,128)S(1)} %get-tuple-element.16) | copy-start | bytes 786436
  75.5 12.0 %copy-start.4 = (f32[8,64,128]{2,1,0:T(8,128)}, f32[8,64,128]{2,1,0:T(8,128)S(1)}, u32[]{:S(2)}) copy-start(f32[8,64,128]{2,1,0:T(8,128)S(1)} %get-tuple-element.17) | copy-start | bytes 786436
  75.5 6.5 %collective-permute-start.14 = (f32[2,8,128]{2,1,0:T(8,128)S(1)}, f32[2,8,128]{2,1,0:T(8,128)S(1)}, u32[]{:S(2)}, u32[]{:S(2)}) collective-permute-start(f32[2,8,128]{2,1,0:T(8,128)S(1)} %pad_maximum_fusion.11), channel_id=1, source_target_pairs={{0,1},{2,3},{4,5},{6,7},{8,9},{10,11},{12,13},{14,15},{16,17},{18,... | collective-permute-start | bytes 24584 | tf_op jit(solution)/shard_map/ppermute | solution.py:16
  80.0 7.5 %copy-start.8 = (f32[8,64,128]{2,1,0:T(8,128)}, f32[8,64,128]{2,1,0:T(8,128)S(1)}, u32[]{:S(2)}) copy-start(f32[8,64,128]{2,1,0:T(8,128)S(1)} %fusion.57) | copy-start | bytes 786436
  80.1 6.5 %collective-permute-start.13 = (f32[2,64,128]{2,1,0:T(8,128)S(1)}, f32[2,64,128]{2,1,0:T(8,128)S(1)}, u32[]{:S(2)}, u32[]{:S(2)}) collective-permute-start(f32[2,64,128]{2,1,0:T(8,128)S(1)} %pad_maximum_fusion.5), channel_id=1, source_target_pairs={{0,2},{2,4},{4,6},{6,8},{8,10},{10,12},{12,14},{14,16},{16,18},{18... | collective-permute-start | bytes 196616 | tf_op jit(solution)/shard_map/ppermute | solution.py:16
  (21 other events, 29.3 us)
where the time goes:
time: 89.5 us; the launch traced here: 88.6 us
  starting transfers between devices  43.2 us (48%)
  waiting for transfers between devices  24.7 us (28%)
  local copies, waits for them, and re-layouts  11.4 us (13%)
  other arithmetic  5.54 us (6%)
  between operations  3.83 us (4%)
    ppermute x15, starting transfers between devices, passed_along(): return lax.ppermute(block, axis, route)  43.2 us
    ppermute x15, waiting for transfers between devices, passed_along(): return lax.ppermute(block, axis, route)  24.7 us
    unnamed x55, local copies, waits for them, and re-layouts  8.77 us
  transfers between devices with their start and end apart: 15, of which 9 were waited for; matrix products, arithmetic and copies ran while one was open for 3% of the time, Pallas kernels for 0%

commit v1 on v0

v1 whole, which is shorter than its diff:
```python
import functools

import jax
import jax.numpy as jnp
from jax import lax
from jax.experimental import pallas as pl
from jax.experimental.pallas import tpu as pltpu
from jax.sharding import PartitionSpec as P

STEPS = 3
TILE = 8
HALF = 4
TIME_STEP = 0.5
CURRENT_SCALE = 0.1
VMEM = pl.BlockSpec(memory_space=pltpu.VMEM)
ANY = pl.BlockSpec(memory_space=pl.ANY)
SMEM = pl.BlockSpec(memory_space=pltpu.SMEM)
CODES, BUNCH = 6, 7


def down_counts(moves):
    return (moves + 3, moves + 3) + (moves + 2,) * 5 + (moves + 1,)


def up_counts(moves):
    below = 3 - moves
    return (below,) * 5 + (below - 1, below, below)


def offsets(counts):
    starts = [0]
    for count in counts:
        starts.append(starts[-1] + count)
    return starts


def pack_kernel(moves, sides, *refs):
    fields, bunch, codes = refs[:6], refs[6], refs[7]
    outs = refs[8 : 8 + 2 + 3 * len(sides)]
    down_int, up_int, side_int, sems = refs[8 + 2 + 3 * len(sides) :]
    down, up = outs[:2]
    planes, width = codes.shape[:2]
    downs, ups = down_counts(moves), up_counts(moves)
    down_at, up_at = offsets(downs), offsets(ups)
    arrays = list(fields) + [codes, bunch]
    copies = []

    def copy(source, target):
        item = pltpu.make_async_copy(source, target, sems.at[len(copies)])
        item.start()
        copies.append(item)

    gx = lax.axis_index("gx")
    for a, array in enumerate(arrays):
        whole = a < 6
        if downs[a]:
            goal = down.at[pl.ds(down_at[a], downs[a])] if whole else down_int.at[a - 6, pl.ds(0, downs[a])]
            copy(array.at[pl.ds(0, downs[a])], goal)
        if ups[a]:
            goal = up.at[pl.ds(up_at[a], ups[a])] if whole else up_int.at[a - 6, pl.ds(0, ups[a])]
            copy(array.at[pl.ds(planes - ups[a], ups[a])], goal)
        for n, side in enumerate(sides):
            if side == "swap":
                row = pl.multiple_of(jnp.where(gx == 0, width - TILE, 0), TILE)
            else:
                row = width - TILE if side == "right" else 0
            goal = outs[2 + 3 * n].at[pl.ds(a * planes, planes)] if whole else side_int.at[n, a - 6]
            copy(array.at[:, pl.ds(row, TILE)], goal)
    for item in copies:
        item.wait()
    for a in (CODES, BUNCH):
        if downs[a]:
            down[pl.ds(down_at[a], downs[a])] = down_int[a - 6, pl.ds(0, downs[a])].astype(jnp.float32)
        if ups[a]:
            up[pl.ds(up_at[a], ups[a])] = up_int[a - 6, pl.ds(0, ups[a])].astype(jnp.float32)
    for n in range(len(sides)):
        block, block_down, block_up = outs[2 + 3 * n : 5 + 3 * n]
        for a in (CODES, BUNCH):
            block[pl.ds(a * planes, planes)] = side_int[n, a - 6].astype(jnp.float32)
        for a in range(8):
            if downs[a]:
                block_down[pl.ds(down_at[a], downs[a])] = block[pl.ds(a * planes, downs[a])]
            if ups[a]:
                block_up[pl.ds(up_at[a], ups[a])] = block[pl.ds((a + 1) * planes - ups[a], ups[a])]


def pack(moves, sides, arrays):
    planes, width, depth = arrays[0].shape
    n_down, n_up = sum(down_counts(moves)), sum(up_counts(moves))
    f32 = lambda *shape: jax.ShapeDtypeStruct(shape, jnp.float32)
    shapes = [f32(n_down, width, depth), f32(n_up, width, depth)]
    for _ in sides:
        shapes += [f32(8 * planes, TILE, depth), f32(n_down, TILE, depth), f32(n_up, TILE, depth)]
    return pl.pallas_call(
        functools.partial(pack_kernel, moves, sides),
        out_shape=shapes,
        in_specs=[ANY] * 8,
        out_specs=[VMEM] * len(shapes),
        scratch_shapes=[
            pltpu.VMEM((2, moves + 2, width, depth), jnp.int32),
            pltpu.VMEM((2, 3 - moves, width, depth), jnp.int32),
            pltpu.VMEM((len(sides), 2, planes, TILE, depth), jnp.int32),
            pltpu.SemaphoreType.DMA((8 * (2 + len(sides)),)),
        ],
        compiler_params=pltpu.CompilerParams(vmem_limit_bytes=24 * 2**20),
        name="pack",
    )(*arrays)


def coefficients(code):
    kind = code.dtype.type
    five, six, seven = code == kind(5), code == kind(6), code == kind(7)
    keep = jnp.where(five, 0.0, jnp.where(six, 0.8 / 1.2, jnp.where(seven, 0.4 / 1.6, 1.0)))
    gain = jnp.where(
        five,
        0.0,
        jnp.where(six, TIME_STEP / 1.2, jnp.where(seven, TIME_STEP / 1.6, TIME_STEP)),
    )
    return keep, gain


def steps_kernel(moves, moved, *refs):
    local, bunch, codes = refs[:6], refs[6], refs[7]
    down, up, side, side_down, side_up = refs[8:13]
    outs = refs[13:19]
    ext, keep, gain, current, rows = refs[19:]
    planes, width, depth = codes.shape
    tall = width + TILE
    gz, gx = lax.axis_index("gz"), lax.axis_index("gx")
    first = gz == 0
    last = gz == lax.axis_size("gz") - 1
    total = width * lax.axis_size("gx")
    start = gx * width
    downs, ups = down_counts(moves), up_counts(moves)
    down_at, up_at = offsets(downs), offsets(ups)
    base = 3 - moves

    row = lax.broadcasted_iota(jnp.int32, (tall, depth), 0)
    place = start + jnp.where(row < width + HALF, row, row - tall)
    inside = (place >= 0) & (place < total)
    place = place.astype(jnp.float32)
    whole = 1.0 + (place - total / 2) / (2 * total)
    half = 1.0 + (place + 0.5 - total / 2) / (2 * total)
    step = jnp.where(inside, TIME_STEP, 0.0)
    for n, value in enumerate((whole, half, 1.0 / whole, 1.0 / half, step, step / whole, step / half)):
        rows[n] = value
    ghost_in = inside[width:]

    own = pl.ds(0, width)
    edge = pl.ds(width, TILE)

    def spread(a, store):
        n_down, n_up = downs[a], ups[a]
        local_ref = (list(local) + [codes, bunch])[a]
        store(base, planes, own, local_ref[...], None)
        store(base, planes, edge, side[pl.ds(a * planes, planes)], ghost_in)
        if n_down:
            store(base + planes, n_down, own, down[pl.ds(down_at[a], n_down)], None)
            store(base + planes, n_down, edge, side_down[pl.ds(down_at[a], n_down)], ghost_in)
        if n_up:
            store(base - n_up, n_up, own, up[pl.ds(up_at[a], n_up)], None)
            store(base - n_up, n_up, edge, side_up[pl.ds(up_at[a], n_up)], ghost_in)

    for a in range(6):

        def store_field(at, count, where, value, mask):
            if mask is not None:
                value = jnp.where(mask[None], value, 0.0)
            ext[a, pl.ds(at, count), where] = value

        spread(a, store_field)

    def store_codes(at, count, where, value, mask):
        kept, gained = coefficients(value)
        if mask is not None:
            kept, gained = jnp.where(mask[None], kept, 0.0), jnp.where(mask[None], gained, 0.0)
        keep[pl.ds(at, count), where] = kept
        gain[pl.ds(at, count), where] = gained

    def store_bunch(at, count, where, value, mask):
        current[pl.ds(at, count), where] = CURRENT_SCALE * value.astype(jnp.float32)

    spread(CODES, store_codes)
    spread(BUNCH, store_bunch)

    lane = lax.broadcasted_iota(jnp.int32, (tall, depth), 1)
    not_last, not_first = lane < depth - 1, lane > 0

    def forward_y(v):
        return jnp.where(not_last, pltpu.roll(v, depth - 1, 1), 0.0) - v

    def backward_y(v):
        return v - jnp.where(not_first, pltpu.roll(v, 1, 1), 0.0)

    def forward_x(v):
        return pltpu.roll(v, tall - 1, 0) - v

    def backward_x(v):
        return v - pltpu.roll(v, 1, 0)

    def magnetic(e):
        ex, ey, es = ext[0, e], ext[1, e], ext[2, e]
        bx = ext[3, e] - (rows[4] * forward_y(es) - rows[5] * (ext[1, e + 1] - ey))
        by = ext[4, e] - rows[6] * ((ext[0, e + 1] - ex) - forward_x(rows[0] * es))
        bs = ext[5, e] - rows[4] * (forward_x(ey) - forward_y(ex))
        return ex, ey, es, bx, by, bs

    moved_now = 0
    for t in range(STEPS):
        moved_now = moved_now + moved[t]
        begin = jnp.where(first, base + moved_now, t + 1)
        end = jnp.where(last, jnp.minimum(planes + 4 - t, planes + 2 + moved_now - moves), planes + 4 - t) + 1
        _, _, _, bx, by, _ = magnetic(t)
        ext[3, t], ext[4, t] = bx, by

        @pl.when(first)
        def _():
            ext[3, begin - 1] = jnp.zeros((tall, depth), jnp.float32)
            ext[4, begin - 1] = jnp.zeros((tall, depth), jnp.float32)

        def plane(e, carry):
            ex, ey, es, bx, by, bs = magnetic(e)
            kept, gained = keep[e - moved_now], gain[e - moved_now]
            ex = kept * ex + gained * (backward_y(bs) - rows[3] * (by - ext[4, e - 1]))
            ey = kept * ey + gained * (rows[2] * ((bx - ext[3, e - 1]) - backward_x(rows[1] * bs)))
            es = kept * es + gained * (backward_x(by) - backward_y(bx) - current[e - moved_now])
            for a, value in enumerate((ex, ey, es, bx, by, bs)):
                if t < STEPS - 1:
                    ext[a, e] = value
                else:
                    outs[a][e - 3] = value[:width]
                    if a in (3, 4):
                        ext[a, e] = value
            return carry

        lax.fori_loop(begin, end, plane, 0)


def advance(moves, moved, arrays, ghosts):
    planes, width, depth = arrays[0].shape
    tall = width + TILE
    block = jax.ShapeDtypeStruct((planes, width, depth), jnp.float32)
    return pl.pallas_call(
        lambda moved, *refs: steps_kernel(moves, moved, *refs),
        out_shape=[block] * 6,
        in_specs=[SMEM] + [VMEM] * 13,
        out_specs=[VMEM] * 6,
        scratch_shapes=[
            pltpu.VMEM((6, planes + 6, tall, depth), jnp.float32),
            pltpu.VMEM((planes + 5, tall, depth), jnp.float32),
            pltpu.VMEM((planes + 5, tall, depth), jnp.float32),
            pltpu.VMEM((planes + 5, tall, depth), jnp.float32),
            pltpu.VMEM((7, tall, depth), jnp.float32),
        ],
        compiler_params=pltpu.CompilerParams(vmem_limit_bytes=32 * 2**20),
        name="steps",
    )(moved, *arrays, *ghosts)


def exchange(moves, sides, packed):
    size_z, size_x = lax.axis_size("gz"), lax.axis_size("gx")

    def passed(block, dz, side):
        steps_x = {"swap": (1, -1), "right": (1,), "left": (-1,), None: (0,)}[side]
        route = [
            (z * size_x + x, (z + dz) * size_x + x + dx)
            for z in range(size_z)
            for x in range(size_x)
            for dx in steps_x
            if 0 <= z + dz < size_z and 0 <= x + dx < size_x
        ]
        return lax.ppermute(block, ("gz", "gx"), route)

    down, up = passed(packed[0], -1, None), passed(packed[1], 1, None)
    found = []
    for n, side in enumerate(sides):
        block, block_down, block_up = packed[2 + 3 * n : 5 + 3 * n]
        found.append((passed(block, 0, side), passed(block_down, -1, side), passed(block_up, 1, side)))
    if len(sides) == 2:
        from_left, from_right = found
        row = lax.broadcasted_iota(jnp.int32, (1, TILE, 1), 1)
        merged = [jnp.where(row < HALF, r, l) for l, r in zip(from_left, from_right)]
    else:
        merged = list(found[0])
    return [down, up] + merged


def on_device(*args):
    arrays, moved = args[:8], args[8]
    sides = ("swap",) if lax.axis_size("gx") == 2 else ("right", "left")

    def run(moves, arrays, moved):
        packed = pack(moves, sides, arrays)
        ghosts = exchange(moves, sides, packed)
        return tuple(advance(moves, moved, arrays, ghosts))

    return lax.cond(
        jnp.sum(moved) == 2,
        functools.partial(run, 2),
        functools.partial(run, 1),
        arrays,
        moved,
    )


def solution(mesh):
    block = P("gz", "gx", None)
    return jax.shard_map(
        on_device,
        mesh=mesh,
        in_specs=(block,) * 8 + (P(),),
        out_specs=(block,) * 6,
        check_vma=False,
    )
```

time: 89.5 us -> 34.1 us (0.38)
  the two profiles are of different devices: /device:TPU:8 before, /device:TPU:1 now
where the time goes in v1:
time: 34.1 us; the launch traced here: 33.9 us
  starting transfers between devices  14.5 us (43%)
  Pallas kernels  9.35 us (27%)
  waiting for transfers between devices  7.25 us (21%)
  other arithmetic  1.29 us (4%)
  between operations  1.28 us (4%)
    ppermute x5, starting transfers between devices, passed(): return lax.ppermute(block, ('gz', 'gx'), route)  14.5 us
    pallas_call x1, Pallas kernels, advance(): pl.pallas_call(lambda moved, *refs: steps_kernel(moves, moved, *refs), ou...  7.55 us
    ppermute x5, waiting for transfers between devices, passed(): return lax.ppermute(block, ('gz', 'gx'), route)  7.25 us
    pallas_call x1, Pallas kernels, pack(): pl.pallas_call(functools.partial(pack_kernel, moves, sides), out_shape=sh...  1.8 us
    reduce_sum x1, other arithmetic, on_device(): jnp.sum(moved) == 2  1.29 us
  transfers between devices with their start and end apart: 5, of which 3 were waited for; matrix products, arithmetic and copies ran while one was open for 0% of the time, Pallas kernels for 0%

profile of v1, /device:TPU:1, one launch (start us, length us, event | category | flops | bytes accessed | tf_op | source)
XLA Modules:
  0.0 33.9 jit_solution(11116646664067460419)
XLA Ops:
  0.6 1.3 %reduce_sum.9 = s32[]{:T(128)} reduce(s32[3]{0:T(128)} %param.19, s32[]{:T(128)} %constant.0.clone.1), dimensions={0}, to_apply=%region_0.0 | reduce | flops 2 | bytes 20 | tf_op jit(solution)/shard_map/reduce_sum | solution.py:298
  2.6 31.3 %conditional.1 = ((f32[8,64,128]{2,1,0:T(8,128)}, f32[8,64,128]{2,1,0:T(8,128)}, f32[8,64,128]{2,1,0:T(8,128)}, f32[8,64,128]{2,1,0:T(8,128)}, f32[8,64,128]{2,1,0:T(8,128)}, /*index=5*/f32[8,64,128]{2,1,0:T(8,128)})) conditional(s32[]{:T(128)} %convert_element_type.3, (f32[8,64,128]{2,1,0:T(8,128)}, f32[8,64,128]{2,1,0:T(8,128)}, ...), branch_computations={%region_1.0_spmd, %region_2.0_spmd} | conditional | bytes 15335932 | solution.py:297
  2.6 0.0 copy-start.1
  2.6 0.0 copy-start.3
  2.6 0.0 copy-start.5
  2.6 0.0 copy-start.7
  2.6 0.0 copy-start.9
  2.7 0.0 copy-start.11
  2.7 0.0 copy-start.13
  2.7 0.0 copy-start.15
  2.7 0.0 copy-start.17
  2.7 1.8 %pack.3 = (f32[33,64,128]{2,1,0:T(8,128)S(1)}, f32[7,64,128]{2,1,0:T(8,128)S(1)}, f32[64,8,128]{2,1,0:T(8,128)S(1)}, f32[33,8,128]{2,1,0:T(8,128)S(1)}, f32[7,8,128]{2,1,0:T(8,128)S(1)}) custom-call(f32[8,64,128]{2,1,0:T(8,128)} %get-tuple-element.51.refs_0_, f32[8,64,128]{2,1,0:T(8,128)} %get-tuple-element.52.refs_1_, ...), custom_call_target="tpu_custom_call" | custom-call | tf_op jit(solution)/shard_map/cond/branch_1_fun/pack/pallas_call | solution.py:94
  4.5 2.0 %collective-permute-start.5 = (f32[33,64,128]{2,1,0:T(8,128)S(1)}, f32[33,64,128]{2,1,0:T(8,128)S(1)}, u32[]{:S(2)}, u32[]{:S(2)}) collective-permute-start(f32[33,64,128]{2,1,0:T(8,128)S(1)} %get-tuple-element.59), channel_id=1, source_target_pairs={{2,0},{3,1},{4,2},{5,3},{6,4},{7,5},{8,6},{9,7},{10,8},{11,9},{12,... | collective-permute-start | bytes 3244040 | tf_op jit(solution)/shard_map/cond/branch_1_fun/ppermute | solution.py:272
  6.5 2.7 %collective-permute-start.7 = (f32[64,8,128]{2,1,0:T(8,128)S(1)}, f32[64,8,128]{2,1,0:T(8,128)S(1)}, u32[]{:S(2)}, u32[]{:S(2)}) collective-permute-start(f32[64,8,128]{2,1,0:T(8,128)S(1)} %get-tuple-element.61), channel_id=1, source_target_pairs={{0,1},{1,0},{2,3},{3,2},{4,5},{5,4},{6,7},{7,6},{8,9},{9,8},{10,11... | collective-permute-start | bytes 786440 | tf_op jit(solution)/shard_map/cond/branch_1_fun/ppermute | solution.py:272
  9.2 3.3 %collective-permute-start.6 = (f32[7,64,128]{2,1,0:T(8,128)S(1)}, f32[7,64,128]{2,1,0:T(8,128)S(1)}, u32[]{:S(2)}, u32[]{:S(2)}) collective-permute-start(f32[7,64,128]{2,1,0:T(8,128)S(1)} %get-tuple-element.60), channel_id=1, source_target_pairs={{0,2},{1,3},{2,4},{3,5},{4,6},{5,7},{6,8},{7,9},{8,10},{9,11},{10,... | collective-permute-start | bytes 688136 | tf_op jit(solution)/shard_map/cond/branch_1_fun/ppermute | solution.py:272
  12.5 1.9 %collective-permute-start.8 = (f32[33,8,128]{2,1,0:T(8,128)S(1)}, f32[33,8,128]{2,1,0:T(8,128)S(1)}, u32[]{:S(2)}, u32[]{:S(2)}) collective-permute-start(f32[33,8,128]{2,1,0:T(8,128)S(1)} %get-tuple-element.62), channel_id=1, source_target_pairs={{2,1},{3,0},{4,3},{5,2},{6,5},{7,4},{8,7},{9,6},{10,9},{11,8},{12,... | collective-permute-start | bytes 405512 | tf_op jit(solution)/shard_map/cond/branch_1_fun/ppermute | solution.py:272
  14.5 4.5 %collective-permute-start.9 = (f32[7,8,128]{2,1,0:T(8,128)S(1)}, f32[7,8,128]{2,1,0:T(8,128)S(1)}, u32[]{:S(2)}, u32[]{:S(2)}) collective-permute-start(f32[7,8,128]{2,1,0:T(8,128)S(1)} %get-tuple-element.63), channel_id=1, source_target_pairs={{0,3},{1,2},{2,5},{3,4},{4,7},{5,6},{6,9},{7,8},{8,11},{9,10},{10,... | collective-permute-start | bytes 86024 | tf_op jit(solution)/shard_map/cond/branch_1_fun/ppermute | solution.py:272
  19.0 1.0 %collective-permute-done.9.refs_12_ = f32[7,8,128]{2,1,0:T(8,128)S(1)} collective-permute-done((f32[7,8,128]{2,1,0:T(8,128)S(1)}, f32[7,8,128]{2,1,0:T(8,128)S(1)}, u32[]{:S(2)}, u32[]{:S(2)}) %collective-permute-start.9) | collective-permute-done | bytes 28704 | tf_op jit(solution)/shard_map/cond/branch_1_fun/ppermute | solution.py:272
  20.0 0.4 %collective-permute-done.8.refs_11_ = f32[33,8,128]{2,1,0:T(8,128)S(1)} collective-permute-done((f32[33,8,128]{2,1,0:T(8,128)S(1)}, f32[33,8,128]{2,1,0:T(8,128)S(1)}, u32[]{:S(2)}, u32[]{:S(2)}) %collective-permute-start.8) | collective-permute-done | bytes 135200 | tf_op jit(solution)/shard_map/cond/branch_1_fun/ppermute | solution.py:272
  20.4 5.9 %collective-permute-done.6.refs_9_ = f32[7,64,128]{2,1,0:T(8,128)S(1)} collective-permute-done((f32[7,64,128]{2,1,0:T(8,128)S(1)}, f32[7,64,128]{2,1,0:T(8,128)S(1)}, u32[]{:S(2)}, u32[]{:S(2)}) %collective-permute-start.6) | collective-permute-done | bytes 229408 | tf_op jit(solution)/shard_map/cond/branch_1_fun/ppermute | solution.py:272
  26.3 0.0 collective-permute-done.7.refs_10_
  26.3 0.0 collective-permute-done.5.refs_8_
  26.3 0.0 copy-done.1
  26.4 7.5 %steps.3 = (f32[8,64,128]{2,1,0:T(8,128)}, f32[8,64,128]{2,1,0:T(8,128)}, f32[8,64,128]{2,1,0:T(8,128)}, f32[8,64,128]{2,1,0:T(8,128)}, f32[8,64,128]{2,1,0:T(8,128)}, /*index=5*/f32[8,64,128]{2,1,0:T(8,128)}) custom-call(s32[3]{0:T(128)S(1)} %copy-done.17, f32[8,64,128]{2,1,0:T(8,128)S(1)} %copy-done.1, f32[8,64,128]{2,1,0:T(8,128)S(1)} %copy-done.3, ...), custom_call_target="tpu_custom_call" | custom-call | tf_op jit(solution)/shard_map/cond/branch_1_fun/steps/pallas_call | solution.py:243
  (8 shorter events, 0.0 us)
Async XLA Ops:
  2.6 23.7 %copy-start.1 = (f32[8,64,128]{2,1,0:T(8,128)S(1)}, f32[8,64,128]{2,1,0:T(8,128)}, u32[]{:S(2)}) copy-start(f32[8,64,128]{2,1,0:T(8,128)} %get-tuple-element.51.refs_0_) | copy-start | bytes 786436 | tf_op jit(solution)/shard_map/cond
  2.6 23.7 %copy-start.3 = (f32[8,64,128]{2,1,0:T(8,128)S(1)}, f32[8,64,128]{2,1,0:T(8,128)}, u32[]{:S(2)}) copy-start(f32[8,64,128]{2,1,0:T(8,128)} %get-tuple-element.52.refs_1_) | copy-start | bytes 786436 | tf_op jit(solution)/shard_map/cond
  2.6 23.7 %copy-start.5 = (f32[8,64,128]{2,1,0:T(8,128)S(1)}, f32[8,64,128]{2,1,0:T(8,128)}, u32[]{:S(2)}) copy-start(f32[8,64,128]{2,1,0:T(8,128)} %get-tuple-element.53.refs_2_) | copy-start | bytes 786436 | tf_op jit(solution)/shard_map/cond
  2.6 23.7 %copy-start.7 = (f32[8,64,128]{2,1,0:T(8,128)S(1)}, f32[8,64,128]{2,1,0:T(8,128)}, u32[]{:S(2)}) copy-start(f32[8,64,128]{2,1,0:T(8,128)} %get-tuple-element.54.refs_3_) | copy-start | bytes 786436 | tf_op jit(solution)/shard_map/cond
  2.6 23.7 %copy-start.9 = (f32[8,64,128]{2,1,0:T(8,128)S(1)}, f32[8,64,128]{2,1,0:T(8,128)}, u32[]{:S(2)}) copy-start(f32[8,64,128]{2,1,0:T(8,128)} %get-tuple-element.55.refs_4_) | copy-start | bytes 786436 | tf_op jit(solution)/shard_map/cond
  2.7 23.7 %copy-start.11 = (f32[8,64,128]{2,1,0:T(8,128)S(1)}, f32[8,64,128]{2,1,0:T(8,128)}, u32[]{:S(2)}) copy-start(f32[8,64,128]{2,1,0:T(8,128)} %get-tuple-element.56.refs_5_) | copy-start | bytes 786436 | tf_op jit(solution)/shard_map/cond
  2.7 23.7 %copy-start.13 = (s32[8,64,128]{2,1,0:T(8,128)S(1)}, s32[8,64,128]{2,1,0:T(8,128)}, u32[]{:S(2)}) copy-start(s32[8,64,128]{2,1,0:T(8,128)} %get-tuple-element.57.refs_6_) | copy-start | bytes 786436 | tf_op jit(solution)/shard_map/cond
  2.7 23.7 %copy-start.15 = (s32[8,64,128]{2,1,0:T(8,128)S(1)}, s32[8,64,128]{2,1,0:T(8,128)}, u32[]{:S(2)}) copy-start(s32[8,64,128]{2,1,0:T(8,128)} %get-tuple-element.58.refs_7_) | copy-start | bytes 786436 | tf_op jit(solution)/shard_map/cond
  2.7 23.6 %copy-start.17 = (s32[3]{0:T(128)S(1)}, s32[3]{0:T(128)}, u32[]{:S(2)}) copy-start(s32[3]{0:T(128)} %get-tuple-element.50.moved) | copy-start | bytes 40 | tf_op jit(solution)/shard_map/cond
  4.5 21.8 %collective-permute-start.5 = (f32[33,64,128]{2,1,0:T(8,128)S(1)}, f32[33,64,128]{2,1,0:T(8,128)S(1)}, u32[]{:S(2)}, u32[]{:S(2)}) collective-permute-start(f32[33,64,128]{2,1,0:T(8,128)S(1)} %get-tuple-element.59), channel_id=1, source_target_pairs={{2,0},{3,1},{4,2},{5,3},{6,4},{7,5},{8,6},{9,7},{10,8},{11,9},{12,... | collective-permute-start | bytes 3244040 | tf_op jit(solution)/shard_map/cond/branch_1_fun/ppermute | solution.py:272
  6.5 19.8 %collective-permute-start.7 = (f32[64,8,128]{2,1,0:T(8,128)S(1)}, f32[64,8,128]{2,1,0:T(8,128)S(1)}, u32[]{:S(2)}, u32[]{:S(2)}) collective-permute-start(f32[64,8,128]{2,1,0:T(8,128)S(1)} %get-tuple-element.61), channel_id=1, source_target_pairs={{0,1},{1,0},{2,3},{3,2},{4,5},{5,4},{6,7},{7,6},{8,9},{9,8},{10,11... | collective-permute-start | bytes 786440 | tf_op jit(solution)/shard_map/cond/branch_1_fun/ppermute | solution.py:272
  9.2 17.0 %collective-permute-start.6 = (f32[7,64,128]{2,1,0:T(8,128)S(1)}, f32[7,64,128]{2,1,0:T(8,128)S(1)}, u32[]{:S(2)}, u32[]{:S(2)}) collective-permute-start(f32[7,64,128]{2,1,0:T(8,128)S(1)} %get-tuple-element.60), channel_id=1, source_target_pairs={{0,2},{1,3},{2,4},{3,5},{4,6},{5,7},{6,8},{7,9},{8,10},{9,11},{10,... | collective-permute-start | bytes 688136 | tf_op jit(solution)/shard_map/cond/branch_1_fun/ppermute | solution.py:272
  12.5 7.9 %collective-permute-start.8 = (f32[33,8,128]{2,1,0:T(8,128)S(1)}, f32[33,8,128]{2,1,0:T(8,128)S(1)}, u32[]{:S(2)}, u32[]{:S(2)}) collective-permute-start(f32[33,8,128]{2,1,0:T(8,128)S(1)} %get-tuple-element.62), channel_id=1, source_target_pairs={{2,1},{3,0},{4,3},{5,2},{6,5},{7,4},{8,7},{9,6},{10,9},{11,8},{12,... | collective-permute-start | bytes 405512 | tf_op jit(solution)/shard_map/cond/branch_1_fun/ppermute | solution.py:272
  14.5 5.5 %collective-permute-start.9 = (f32[7,8,128]{2,1,0:T(8,128)S(1)}, f32[7,8,128]{2,1,0:T(8,128)S(1)}, u32[]{:S(2)}, u32[]{:S(2)}) collective-permute-start(f32[7,8,128]{2,1,0:T(8,128)S(1)} %get-tuple-element.63), channel_id=1, source_target_pairs={{0,3},{1,2},{2,5},{3,4},{4,7},{5,6},{6,9},{7,8},{8,11},{9,10},{10,... | collective-permute-start | bytes 86024 | tf_op jit(solution)/shard_map/cond/branch_1_fun/ppermute | solution.py:272

commit v2 on v1

v2 whole, which is shorter than its diff:
```python
import functools

import jax
import jax.numpy as jnp
from jax import lax
from jax.experimental import pallas as pl
from jax.experimental.pallas import tpu as pltpu
from jax.sharding import PartitionSpec as P

STEPS = 3
TILE = 8
HALF = 4
TIME_STEP = 0.5
CURRENT_SCALE = 0.1
VMEM = pl.BlockSpec(memory_space=pltpu.VMEM)
SMEM = pl.BlockSpec(memory_space=pltpu.SMEM)
ANY = pl.BlockSpec(memory_space=pl.ANY)
EX, EY, ES, BX, BY, BS, CODES, BUNCH = range(8)
CASES = ((1, 1), (1, 0), (2, 1), (2, 0))


def down_counts(case):
    moves, now = case
    later = moves - now
    return (moves + 2,) * 6 + (later + 2, later + 1)


def up_counts(case):
    moves, now = case
    below = 3 - moves
    later = moves - now
    return (below - 1, below - 1, below, below, below, below - 1, 2 - later, 2 - later)


def offsets(counts):
    starts = [0]
    for count in counts:
        starts.append(starts[-1] + count)
    return starts


def half_up(count):
    return (count + 1) // 2


def column_scales(place, total):
    place = place.astype(jnp.float32)
    whole = 1.0 + (place - total / 2) / (2 * total)
    half = 1.0 + (place + 0.5 - total / 2) / (2 * total)
    return whole, half


def turned(tiles):
    return pltpu.roll(tiles, HALF, 1)


def pack_kernel(sides, *refs):
    sources, moved = refs[:8], refs[8]
    own = refs[9:17]
    which = refs[17]
    across = refs[18 : 18 + len(sides)]
    sent = refs[18 + len(sides) : -3]
    moved_here, sems, moved_sem = refs[-3:]
    per_case = 2 + 2 * len(sides)
    planes, width, depth = own[0].shape
    gx = lax.axis_index("gx")
    total = width * lax.axis_size("gx")

    get_moved = pltpu.make_async_copy(moved, moved_here, moved_sem)
    get_moved.start()
    copies = [pltpu.make_async_copy(sources[a], own[a], sems.at[a]) for a in range(8)]
    for item in copies:
        item.start()
    get_moved.wait()
    now = moved_here[0]
    later = moved_here[1] + moved_here[2]
    case_index = jnp.where(now + later == 1, 1 - now, 3 - now)
    which[0] = case_index

    row = lax.broadcasted_iota(jnp.int32, (width, depth), 0)
    whole, half = column_scales(gx * width + row, total)
    step_whole, step_half = TIME_STEP / whole, TIME_STEP / half
    low = lax.broadcasted_iota(jnp.int32, (1, TILE, depth), 1) < HALF

    def edge_of(side):
        if side == "swap":
            return pl.multiple_of(jnp.where(gx == 0, width - TILE, 0), TILE), gx == 0
        return (width - TILE, True) if side == "right" else (0, False)

    def paired(first, second, high):
        if high is True:
            return jnp.where(low, turned(first), second)
        if high is False:
            return jnp.where(low, first, turned(second))
        return jnp.where(
            low,
            jnp.where(high, turned(first), first),
            jnp.where(high, second, turned(second)),
        )

    for item in copies:
        item.wait()

    for n, side in enumerate(sides):
        at, high = edge_of(side)
        for a in range(4):
            first = own[a][:, pl.ds(at, TILE)]
            second = own[a + 4][:, pl.ds(at, TILE)].astype(jnp.float32)
            across[n][pl.ds(a * planes, planes)] = paired(first, second, high)

    for c, case in enumerate(CASES):
        down, up = sent[c * per_case : c * per_case + 2]
        corners = sent[c * per_case + 2 : (c + 1) * per_case]
        downs, ups = down_counts(case), up_counts(case)
        down_at, up_at = offsets(downs), offsets(ups)
        moves = case[0]

        @pl.when(case_index == c)
        def _():
            for a in range(8):
                if downs[a]:
                    down[pl.ds(down_at[a], downs[a])] = own[a][: downs[a]].astype(jnp.float32)
                if ups[a]:
                    up[pl.ds(up_at[a], ups[a])] = own[a][planes - ups[a] :].astype(jnp.float32)
            far = moves + 2
            down[down_at[BX] + far - 1] = own[BX][far - 1] + step_whole * own[EY][far]
            down[down_at[BY] + far - 1] = own[BY][far - 1] - step_half * own[EX][far]
            far = planes - (3 - moves)
            up[up_at[BX]] = own[BX][far] - step_whole * own[EY][far]
            up[up_at[BY]] = own[BY][far] + step_half * own[EX][far]
            for n, side in enumerate(sides):
                at, high = edge_of(side)
                for block, corner, count in (
                    (down, corners[2 * n], down_at[-1]),
                    (up, corners[2 * n + 1], up_at[-1]),
                ):
                    middle = half_up(count)
                    rest = count - middle
                    first = block[pl.ds(0, middle), pl.ds(at, TILE)]
                    second = block[pl.ds(middle, rest), pl.ds(at, TILE)]
                    corner[pl.ds(0, rest)] = paired(first[:rest], second, high)
                    if rest < middle:
                        corner[pl.ds(rest, 1)] = paired(first[rest:], first[rest:], high)


def pack(sides, arrays, moved):
    planes, width, depth = arrays[0].shape
    vmem = lambda *shape: pltpu.VMEM(shape, jnp.float32)
    shapes = [pltpu.VMEM(a.shape, a.dtype) for a in arrays] + [pltpu.SMEM((1,), jnp.int32)]
    shapes += [vmem(4 * planes, TILE, depth)] * len(sides)
    for case in CASES:
        n_down, n_up = sum(down_counts(case)), sum(up_counts(case))
        shapes += [vmem(n_down, width, depth), vmem(n_up, width, depth)]
        shapes += [vmem(half_up(n_down), TILE, depth), vmem(half_up(n_up), TILE, depth)] * len(sides)
    found = pl.pallas_call(
        functools.partial(pack_kernel, sides),
        out_shape=shapes,
        in_specs=[ANY] * 9,
        out_specs=[VMEM] * 8 + [SMEM] + [VMEM] * (len(shapes) - 9),
        scratch_shapes=[
            pltpu.SMEM((STEPS,), jnp.int32),
            pltpu.SemaphoreType.DMA((8,)),
            pltpu.SemaphoreType.DMA,
        ],
        compiler_params=pltpu.CompilerParams(vmem_limit_bytes=32 * 2**20),
        name="pack",
    )(*arrays, moved)
    own, which, rest = found[:8], found[8], found[9:]
    across, sent = rest[: len(sides)], rest[len(sides) :]
    per_case = 2 + 2 * len(sides)
    return own, which, across, [sent[c * per_case : (c + 1) * per_case] for c in range(len(CASES))]


def coefficients(code):
    kind = code.dtype.type
    five, six, seven = code == kind(5), code == kind(6), code == kind(7)
    keep = jnp.where(five, 0.0, jnp.where(six, 0.8 / 1.2, jnp.where(seven, 0.4 / 1.6, 1.0)))
    gain = jnp.where(
        five,
        0.0,
        jnp.where(six, TIME_STEP / 1.2, jnp.where(seven, TIME_STEP / 1.6, TIME_STEP)),
    )
    return keep, gain


def ghost_inside(width, depth):
    gx = lax.axis_index("gx")
    row = lax.broadcasted_iota(jnp.int32, (1, TILE, depth), 1)
    right = gx < lax.axis_size("gx") - 1
    return jnp.where(row < HALF, right.astype(jnp.int32), (gx > 0).astype(jnp.int32)) == 1


def prepare_kernel(moves, *refs):
    own, (ext, keep, gain, current, rows) = refs[:8], refs[8:]
    planes, width, depth = own[0].shape
    tall = width + TILE
    base = 3 - moves
    total = width * lax.axis_size("gx")

    row = lax.broadcasted_iota(jnp.int32, (tall, depth), 0)
    place = lax.axis_index("gx") * width + jnp.where(row < width + HALF, row, row - tall)
    inside = (place >= 0) & (place < total)
    whole, half = column_scales(place, total)
    step = jnp.where(inside, TIME_STEP, 0.0)
    for n, value in enumerate((whole, half, 1.0 / whole, 1.0 / half, step, step / whole, step / half)):
        rows[n] = value
    here, mine = pl.ds(base, planes), pl.ds(0, width)
    for a in range(6):
        ext[a, here, mine] = own[a][...]
    keep[here, mine], gain[here, mine] = coefficients(own[CODES][...])
    current[here, mine] = CURRENT_SCALE * own[BUNCH][...].astype(jnp.float32)
    for a in (EX, EY):
        ext[a, 0] = jnp.zeros((tall, depth), jnp.float32)
        ext[a, planes + 5] = jnp.zeros((tall, depth), jnp.float32)


def prepare(moves, own):
    planes, width, depth = own[0].shape
    tall = width + TILE
    vmem = lambda *shape: pltpu.VMEM(shape, jnp.float32)
    cells = vmem(planes + 5, tall, depth)
    return pl.pallas_call(
        functools.partial(prepare_kernel, moves),
        out_shape=[vmem(6, planes + 6, tall, depth), cells, cells, cells, vmem(7, tall, depth)],
        in_specs=[VMEM] * 8,
        out_specs=[VMEM] * 5,
        compiler_params=pltpu.CompilerParams(vmem_limit_bytes=32 * 2**20),
        cost_estimate=pl.CostEstimate(flops=10**7, bytes_accessed=10**7, transcendentals=0),
        name="prepare",
    )(*own)


def steps_kernel(case, n_sides, moved, *refs):
    rows = refs[4]
    down, up = refs[5:7]
    beside = [refs[7 + 3 * n : 10 + 3 * n] for n in range(n_sides)]
    outs = refs[7 + 3 * n_sides : 13 + 3 * n_sides]
    ext, keep, gain, current = refs[13 + 3 * n_sides : 17 + 3 * n_sides]
    final, sems = refs[17 + 3 * n_sides :]
    moves = case[0]
    base = 3 - moves
    _, planes, width, depth = final.shape
    tall = width + TILE
    gz, gx = lax.axis_index("gz"), lax.axis_index("gx")
    first = gz == 0
    last = gz == lax.axis_size("gz") - 1
    downs, ups = down_counts(case), up_counts(case)
    down_at, up_at = offsets(downs), offsets(ups)
    ghost_in = ghost_inside(width, depth)
    low = lax.broadcasted_iota(jnp.int32, (1, TILE, depth), 1) < HALF

    def spread_tiles(kind, at, count, upper):
        tiles = [side[kind][pl.ds(at, count)] for side in beside]
        if n_sides == 1:
            same = (gx > 0) if upper else (gx == 0)
            found = jnp.where(same, tiles[0], turned(tiles[0]))
        else:
            from_left, from_right = tiles
            if upper:
                from_right = turned(from_right)
            else:
                from_left = turned(from_left)
            found = jnp.where(low, from_right, from_left)
        return jnp.where(ghost_in, found, 0.0)

    def pieces(kind, at, count, middle):
        cut = min(max(middle - at, 0), count)
        if cut:
            yield 0, cut, spread_tiles(kind, at, cut, False)
        if cut < count:
            yield cut, count - cut, spread_tiles(kind, at + cut - middle, count - cut, True)

    def put(a, at, count, where, value):
        span = pl.ds(at, count)
        if a < 6:
            ext[a, span, where] = value
        elif a == CODES:
            kept, gained = coefficients(value)
            if where.start:
                kept, gained = jnp.where(ghost_in, kept, 0.0), jnp.where(ghost_in, gained, 0.0)
            keep[span, where] = kept
            gain[span, where] = gained
        else:
            current[span, where] = CURRENT_SCALE * value

    mine, edge = pl.ds(0, width), pl.ds(width, TILE)
    for a in range(8):
        for at, count, value in pieces(0, a * planes, planes, 4 * planes):
            put(a, base + at, count, edge, value)
        for block, kind, counts, starts, to in (
            (down, 1, downs, down_at, base + planes),
            (up, 2, ups, up_at, base - ups[a]),
        ):
            if counts[a]:
                put(a, to, counts[a], mine, block[pl.ds(starts[a], counts[a])])
                for at, count, value in pieces(kind, starts[a], counts[a], half_up(starts[-1])):
                    put(a, to + at, count, edge, value)

    lane = lax.broadcasted_iota(jnp.int32, (tall, depth), 1)
    not_last, not_first = lane < depth - 1, lane > 0

    def forward_y(v):
        return jnp.where(not_last, pltpu.roll(v, depth - 1, 1), 0.0) - v

    def backward_y(v):
        return v - jnp.where(not_first, pltpu.roll(v, 1, 1), 0.0)

    def forward_x(v):
        return pltpu.roll(v, tall - 1, 0) - v

    def backward_x(v):
        return v - pltpu.roll(v, 1, 0)

    def magnetic(e):
        ex, ey, es = ext[EX, e], ext[EY, e], ext[ES, e]
        bx = ext[BX, e] - (rows[4] * forward_y(es) - rows[5] * (ext[EY, e + 1] - ey))
        by = ext[BY, e] - rows[6] * ((ext[EX, e + 1] - ex) - forward_x(rows[0] * es))
        bs = ext[BS, e] - rows[4] * (forward_x(ey) - forward_y(ex))
        return ex, ey, es, bx, by, bs

    def out_copy(a, plane):
        return pltpu.make_async_copy(final.at[a, plane], outs[a].at[plane], sems.at[a, plane])

    moved_now = 0
    for t in range(STEPS):
        moved_now = moved_now + moved[t]
        begin = jnp.where(first, base + moved_now, t + 1)
        end = jnp.where(last, jnp.minimum(planes + 4 - t, planes + 2 + moved_now - moves), planes + 4 - t) + 1
        _, _, _, bx, by, _ = magnetic(t)
        ext[BX, t], ext[BY, t] = bx, by

        @pl.when(first)
        def _():
            ext[BX, begin - 1] = jnp.zeros((tall, depth), jnp.float32)
            ext[BY, begin - 1] = jnp.zeros((tall, depth), jnp.float32)

        def plane(e, carry):
            ex, ey, es, bx, by, bs = magnetic(e)
            kept, gained = keep[e - moved_now], gain[e - moved_now]
            ex = kept * ex + gained * (backward_y(bs) - rows[3] * (by - ext[BY, e - 1]))
            ey = kept * ey + gained * (rows[2] * ((bx - ext[BX, e - 1]) - backward_x(rows[1] * bs)))
            es = kept * es + gained * (backward_x(by) - backward_y(bx) - current[e - moved_now])
            for a, value in enumerate((ex, ey, es, bx, by, bs)):
                if t < STEPS - 1:
                    ext[a, e] = value
                else:
                    final[a, e - 3] = value[:width]
                    if a in (BX, BY):
                        ext[a, e] = value
            if t == STEPS - 1:
                for a in range(6):
                    out_copy(a, e - 3).start()
            return carry

        lax.fori_loop(begin, end, plane, 0)

    def finish(plane, carry):
        for a in range(6):
            out_copy(a, plane).wait()
        return carry

    lax.fori_loop(0, planes, finish, 0)


def advance(case, moved, shape, ready, ghosts):
    planes, width, depth = shape
    block = jax.ShapeDtypeStruct(shape, jnp.float32)
    n_in = 6 + len(ghosts)
    like = lambda x: pltpu.VMEM(x.shape, x.dtype)
    found = pl.pallas_call(
        functools.partial(steps_kernel, case, (len(ghosts) - 2) // 3),
        out_shape=[block] * 6 + [like(x) for x in ready[:4]],
        in_specs=[SMEM] + [VMEM] * (n_in - 1),
        out_specs=[ANY] * 6 + [VMEM] * 4,
        input_output_aliases={1: 6, 2: 7, 3: 8, 4: 9},
        scratch_shapes=[
            pltpu.VMEM((6, planes, width, depth), jnp.float32),
            pltpu.SemaphoreType.DMA((6, planes)),
        ],
        compiler_params=pltpu.CompilerParams(vmem_limit_bytes=32 * 2**20),
        name="steps",
    )(moved, *ready, *ghosts)
    return tuple(found[:6])


def passed(block, dz, side):
    size_z, size_x = lax.axis_size("gz"), lax.axis_size("gx")
    steps_x = {"swap": (1, -1), "right": (1,), "left": (-1,), None: (0,)}[side]
    route = [
        (z * size_x + x, (z + dz) * size_x + x + dx)
        for z in range(size_z)
        for x in range(size_x)
        for dx in steps_x
        if 0 <= z + dz < size_z and 0 <= x + dx < size_x
    ]
    return lax.ppermute(block, ("gz", "gx"), route)


def on_device(*args):
    arrays, moved = args[:8], args[8]
    arrays = arrays[:6] + (arrays[7], arrays[6])
    sides = ("swap",) if lax.axis_size("gx") == 2 else ("right", "left")
    own, which, across, sent = pack(sides, arrays, moved)

    def run(c, own, across, sent, moved):
        case = CASES[c]
        blocks = sent[c]
        ghosts = [passed(blocks[0], -1, None), passed(blocks[1], 1, None)]
        for n, side in enumerate(sides):
            ghosts.append(passed(across[n], 0, side))
            ghosts.append(passed(blocks[2 + 2 * n], -1, side))
            ghosts.append(passed(blocks[3 + 2 * n], 1, side))
        ready = prepare(case[0], own)
        return advance(case, moved, own[0].shape, ready, ghosts)

    return lax.switch(
        which[0],
        [functools.partial(run, c) for c in range(len(CASES))],
        own,
        across,
        sent,
        moved,
    )


def solution(mesh):
    block = P("gz", "gx", None)
    return jax.shard_map(
        on_device,
        mesh=mesh,
        in_specs=(block,) * 8 + (P(),),
        out_specs=(block,) * 6,
        check_vma=False,
    )
```

time: 34.1 us -> 35.7 us (1.047)
  local copies, waits for them, and re-layouts: 0.06 us -> 7.59 us
  waiting for transfers between devices: 7.25 us -> 4.2 us
  other arithmetic: 1.29 us -> 0 us
  Pallas kernels: 9.35 us -> 8.48 us
  between operations: 1.28 us -> 0.66 us
    unnamed x0 -> x16, local copies, waits for them, and re-layouts: none -> 7.59 us
    ppermute x5, waiting for transfers between devices: 7.25 us -> 4.2 us  [passed(): return lax.ppermute(block, ('gz', 'gx'), route)]
    reduce_sum x1 -> x0, other arithmetic: 1.29 us -> none  [on_device(): jnp.sum(moved) == 2]
    pallas_call x2 -> x3, Pallas kernels: 9.35 us -> 8.48 us  [the longest x1 7.31 us: advance(): pl.pallas_call(functools.partial(steps_kernel, case, (len(ghosts) - 2) //...]
  transfers between devices with their start and end apart: 5 -> 5, of which waited for: 3 -> 2; matrix products, arithmetic and copies ran while one was open for 0% -> 0% of each run, Pallas kernels for 0% -> 1%
where the time goes in v2:
time: 35.7 us; the launch traced here: 35.2 us
  starting transfers between devices  14.2 us (40%)
  Pallas kernels  8.48 us (24%)
  local copies, waits for them, and re-layouts  7.59 us (21%)
  waiting for transfers between devices  4.2 us (12%)
  between operations  0.66 us (2%)
    ppermute x5, starting transfers between devices, passed(): return lax.ppermute(block, ('gz', 'gx'), route)  14.2 us
    unnamed x16, local copies, waits for them, and re-layouts  7.59 us
    pallas_call x1, Pallas kernels, advance(): pl.pallas_call(functools.partial(steps_kernel, case, (len(ghosts) - 2) //...  7.31 us
    ppermute x5, waiting for transfers between devices, passed(): return lax.ppermute(block, ('gz', 'gx'), route)  4.2 us
    pallas_call x1, Pallas kernels, pack(): pl.pallas_call(functools.partial(pack_kernel, sides), out_shape=shapes, i...  0.92 us
  transfers between devices with their start and end apart: 5, of which 2 were waited for; matrix products, arithmetic and copies ran while one was open for 0% of the time, Pallas kernels for 1%

profile of v2, /device:TPU:1, one launch (start us, length us, event | category | flops | bytes accessed | tf_op | source)
XLA Modules:
  0.0 35.2 jit_solution(905959664436635487)
XLA Ops:
  0.6 0.0 copy-start
  0.6 0.9 %copy-done = f32[8,64,128]{2,1,0:T(8,128)S(1)} copy-done((f32[8,64,128]{2,1,0:T(8,128)S(1)}, f32[8,64,128]{2,1,0:T(8,128)}, u32[]{:S(2)}) %copy-start) | copy-done | bytes 262168
  1.6 0.0 copy-start.1
  1.6 0.9 %copy-done.1 = f32[8,64,128]{2,1,0:T(8,128)S(1)} copy-done((f32[8,64,128]{2,1,0:T(8,128)S(1)}, f32[8,64,128]{2,1,0:T(8,128)}, u32[]{:S(2)}) %copy-start.1) | copy-done | bytes 262168
  2.5 0.9 %copy-done.2 = f32[8,64,128]{2,1,0:T(8,128)S(1)} copy-done((f32[8,64,128]{2,1,0:T(8,128)S(1)}, f32[8,64,128]{2,1,0:T(8,128)}, u32[]{:S(2)}) %copy-start.2) | copy-done | bytes 262168
  3.5 0.9 %copy-done.3 = f32[8,64,128]{2,1,0:T(8,128)S(1)} copy-done((f32[8,64,128]{2,1,0:T(8,128)S(1)}, f32[8,64,128]{2,1,0:T(8,128)}, u32[]{:S(2)}) %copy-start.3) | copy-done | bytes 262168
  4.4 0.9 %copy-done.4 = f32[8,64,128]{2,1,0:T(8,128)S(1)} copy-done((f32[8,64,128]{2,1,0:T(8,128)S(1)}, f32[8,64,128]{2,1,0:T(8,128)}, u32[]{:S(2)}) %copy-start.4) | copy-done | bytes 262168
  5.4 0.9 %copy-done.5 = f32[8,64,128]{2,1,0:T(8,128)S(1)} copy-done((f32[8,64,128]{2,1,0:T(8,128)S(1)}, f32[8,64,128]{2,1,0:T(8,128)}, u32[]{:S(2)}) %copy-start.5) | copy-done | bytes 262168
  6.3 0.9 %copy-done.6 = s32[8,64,128]{2,1,0:T(8,128)S(1)} copy-done((s32[8,64,128]{2,1,0:T(8,128)S(1)}, s32[8,64,128]{2,1,0:T(8,128)}, u32[]{:S(2)}) %copy-start.6) | copy-done | bytes 262168
  7.3 0.9 %copy-done.7 = s32[8,64,128]{2,1,0:T(8,128)S(1)} copy-done((s32[8,64,128]{2,1,0:T(8,128)S(1)}, s32[8,64,128]{2,1,0:T(8,128)}, u32[]{:S(2)}) %copy-start.7) | copy-done | bytes 262168
  8.2 0.9 %pack.1 = (f32[8,64,128]{2,1,0:T(8,128)S(1)}, f32[8,64,128]{2,1,0:T(8,128)S(1)}, f32[8,64,128]{2,1,0:T(8,128)S(1)}, f32[8,64,128]{2,1,0:T(8,128)S(1)}, f32[8,64,...) custom-call(f32[8,64,128]{2,1,0:T(8,128)S(1)} %copy-done, ...), custom_call_target="tpu_custom_call" | custom-call | tf_op jit(solution)/shard_map/pack/pallas_call | solution.py:155
  9.2 26.0 %conditional.1 = (f32[8,64,128]{2,1,0:T(8,128)}, f32[8,64,128]{2,1,0:T(8,128)}, f32[8,64,128]{2,1,0:T(8,128)}, f32[8,64,128]{2,1,0:T(8,128)}, f32[8,64,128]{2,1,0:T(8,128)}, /*index=5*/f32[8,64,128]{2,1,0:T(8,128)}) conditional(s32[]{:T(128)} %bitcast, (f32[8,64,128]{2,1,0:T(8,128)S(1)}, f32[8,64,128]{2,1,0:T(8,128)S(1)}, ...), branch_computations={%region_0.0_spmd, %region_1.0_spmd, %region_2.0_spmd, %region_3.0_... | conditional | flops 10000000 | bytes 15275896 | solution.py:416
  9.2 2.0 %collective-permute-start.5 = (f32[23,64,128]{2,1,0:T(8,128)S(1)}, f32[23,64,128]{2,1,0:T(8,128)S(1)}, u32[]{:S(2)}, u32[]{:S(2)}) collective-permute-start(f32[23,64,128]{2,1,0:T(8,128)S(1)} %get-tuple-element.151), channel_id=1, source_target_pairs={{2,0},{3,1},{4,2},{5,3},{6,4},{7,5},{8,6},{9,7},{10,8},{11,9},{12,... | collective-permute-start | bytes 2261000 | tf_op jit(solution)/shard_map/cond/branch_1_fun/ppermute | solution.py:396
  11.2 4.5 %collective-permute-start.6 = (f32[11,64,128]{2,1,0:T(8,128)S(1)}, f32[11,64,128]{2,1,0:T(8,128)S(1)}, u32[]{:S(2)}, u32[]{:S(2)}) collective-permute-start(f32[11,64,128]{2,1,0:T(8,128)S(1)} %get-tuple-element.152), channel_id=1, source_target_pairs={{0,2},{1,3},{2,4},{3,5},{4,6},{5,7},{6,8},{7,9},{8,10},{9,11},{10,... | collective-permute-start | bytes 1081352 | tf_op jit(solution)/shard_map/cond/branch_1_fun/ppermute | solution.py:396
  15.7 1.3 %collective-permute-start.7 = (f32[32,8,128]{2,1,0:T(8,128)S(1)}, f32[32,8,128]{2,1,0:T(8,128)S(1)}, u32[]{:S(2)}, u32[]{:S(2)}) collective-permute-start(f32[32,8,128]{2,1,0:T(8,128)S(1)} %get-tuple-element.153), channel_id=1, source_target_pairs={{0,1},{1,0},{2,3},{3,2},{4,5},{5,4},{6,7},{7,6},{8,9},{9,8},{10,11... | collective-permute-start | bytes 393224 | tf_op jit(solution)/shard_map/cond/branch_1_fun/ppermute | solution.py:396
  16.9 1.9 %collective-permute-start.8 = (f32[12,8,128]{2,1,0:T(8,128)S(1)}, f32[12,8,128]{2,1,0:T(8,128)S(1)}, u32[]{:S(2)}, u32[]{:S(2)}) collective-permute-start(f32[12,8,128]{2,1,0:T(8,128)S(1)} %get-tuple-element.154), channel_id=1, source_target_pairs={{2,1},{3,0},{4,3},{5,2},{6,5},{7,4},{8,7},{9,6},{10,9},{11,8},{12,... | collective-permute-start | bytes 147464 | tf_op jit(solution)/shard_map/cond/branch_1_fun/ppermute | solution.py:396
  18.9 4.5 %collective-permute-start.9 = (f32[6,8,128]{2,1,0:T(8,128)S(1)}, f32[6,8,128]{2,1,0:T(8,128)S(1)}, u32[]{:S(2)}, u32[]{:S(2)}) collective-permute-start(f32[6,8,128]{2,1,0:T(8,128)S(1)} %get-tuple-element.155), channel_id=1, source_target_pairs={{0,3},{1,2},{2,5},{3,4},{4,7},{5,6},{6,9},{7,8},{8,11},{9,10},{10,... | collective-permute-start | bytes 73736 | tf_op jit(solution)/shard_map/cond/branch_1_fun/ppermute | solution.py:396
  23.4 0.2 prepare.5
  23.7 0.7 %collective-permute-done.9.refs_9_ = f32[6,8,128]{2,1,0:T(8,128)S(1)} collective-permute-done((f32[6,8,128]{2,1,0:T(8,128)S(1)}, f32[6,8,128]{2,1,0:T(8,128)S(1)}, u32[]{:S(2)}, u32[]{:S(2)}) %collective-permute-start.9) | collective-permute-done | bytes 24608 | tf_op jit(solution)/shard_map/cond/branch_1_fun/ppermute | solution.py:396
  24.3 0.0 collective-permute-done.8.refs_8_
  24.3 0.0 collective-permute-done.7.refs_7_
  24.3 3.5 %collective-permute-done.6.refs_6_ = f32[11,64,128]{2,1,0:T(8,128)S(1)} collective-permute-done((f32[11,64,128]{2,1,0:T(8,128)S(1)}, f32[11,64,128]{2,1,0:T(8,128)S(1)}, u32[]{:S(2)}, u32[]{:S(2)}) %collective-permute-start.6) | collective-permute-done | bytes 360480 | tf_op jit(solution)/shard_map/cond/branch_1_fun/ppermute | solution.py:396
  27.9 0.0 collective-permute-done.5.refs_5_
  27.9 7.3 %steps.5 = (f32[8,64,128]{2,1,0:T(8,128)}, f32[8,64,128]{2,1,0:T(8,128)}, f32[8,64,128]{2,1,0:T(8,128)}, f32[8,64,128]{2,1,0:T(8,128)}, f32[8,64,128]{2,1,0:T(8,...) custom-call(s32[3]{0:T(128)} %get-tuple-element.137.moved, ...), custom_call_target="tpu_custom_call", output_to_operand_aliasing={{6}: (1, {}), {7}: (2, {}), {8}: (3, {}), {9}: (4, {})} | custom-call | tf_op jit(solution)/shard_map/cond/branch_1_fun/steps/pallas_call | solution.py:370
  (6 shorter events, 0.0 us)
Async XLA Ops:
  0.6 1.0 %copy-start = (f32[8,64,128]{2,1,0:T(8,128)S(1)}, f32[8,64,128]{2,1,0:T(8,128)}, u32[]{:S(2)}) copy-start(f32[8,64,128]{2,1,0:T(8,128)} %refs_0_.1) | copy-start | bytes 786436
  1.6 0.9 %copy-start.1 = (f32[8,64,128]{2,1,0:T(8,128)S(1)}, f32[8,64,128]{2,1,0:T(8,128)}, u32[]{:S(2)}) copy-start(f32[8,64,128]{2,1,0:T(8,128)} %refs_1_.1) | copy-start | bytes 786436
  2.5 0.9 %copy-start.2 = (f32[8,64,128]{2,1,0:T(8,128)S(1)}, f32[8,64,128]{2,1,0:T(8,128)}, u32[]{:S(2)}) copy-start(f32[8,64,128]{2,1,0:T(8,128)} %refs_2_.1) | copy-start | bytes 786436
  3.5 0.9 %copy-start.3 = (f32[8,64,128]{2,1,0:T(8,128)S(1)}, f32[8,64,128]{2,1,0:T(8,128)}, u32[]{:S(2)}) copy-start(f32[8,64,128]{2,1,0:T(8,128)} %refs_3_.1) | copy-start | bytes 786436
  4.4 0.9 %copy-start.4 = (f32[8,64,128]{2,1,0:T(8,128)S(1)}, f32[8,64,128]{2,1,0:T(8,128)}, u32[]{:S(2)}) copy-start(f32[8,64,128]{2,1,0:T(8,128)} %refs_4_.1) | copy-start | bytes 786436
  5.4 0.9 %copy-start.5 = (f32[8,64,128]{2,1,0:T(8,128)S(1)}, f32[8,64,128]{2,1,0:T(8,128)}, u32[]{:S(2)}) copy-start(f32[8,64,128]{2,1,0:T(8,128)} %refs_5_.1) | copy-start | bytes 786436
  6.3 0.9 %copy-start.6 = (s32[8,64,128]{2,1,0:T(8,128)S(1)}, s32[8,64,128]{2,1,0:T(8,128)}, u32[]{:S(2)}) copy-start(s32[8,64,128]{2,1,0:T(8,128)} %refs_6_.1) | copy-start | bytes 786436
  7.3 0.9 %copy-start.7 = (s32[8,64,128]{2,1,0:T(8,128)S(1)}, s32[8,64,128]{2,1,0:T(8,128)}, u32[]{:S(2)}) copy-start(s32[8,64,128]{2,1,0:T(8,128)} %refs_7_.1) | copy-start | bytes 786436
  9.2 18.7 %collective-permute-start.5 = (f32[23,64,128]{2,1,0:T(8,128)S(1)}, f32[23,64,128]{2,1,0:T(8,128)S(1)}, u32[]{:S(2)}, u32[]{:S(2)}) collective-permute-start(f32[23,64,128]{2,1,0:T(8,128)S(1)} %get-tuple-element.151), channel_id=1, source_target_pairs={{2,0},{3,1},{4,2},{5,3},{6,4},{7,5},{8,6},{9,7},{10,8},{11,9},{12,... | collective-permute-start | bytes 2261000 | tf_op jit(solution)/shard_map/cond/branch_1_fun/ppermute | solution.py:396
  11.2 16.7 %collective-permute-start.6 = (f32[11,64,128]{2,1,0:T(8,128)S(1)}, f32[11,64,128]{2,1,0:T(8,128)S(1)}, u32[]{:S(2)}, u32[]{:S(2)}) collective-permute-start(f32[11,64,128]{2,1,0:T(8,128)S(1)} %get-tuple-element.152), channel_id=1, source_target_pairs={{0,2},{1,3},{2,4},{3,5},{4,6},{5,7},{6,8},{7,9},{8,10},{9,11},{10,... | collective-permute-start | bytes 1081352 | tf_op jit(solution)/shard_map/cond/branch_1_fun/ppermute | solution.py:396
  15.7 8.7 %collective-permute-start.7 = (f32[32,8,128]{2,1,0:T(8,128)S(1)}, f32[32,8,128]{2,1,0:T(8,128)S(1)}, u32[]{:S(2)}, u32[]{:S(2)}) collective-permute-start(f32[32,8,128]{2,1,0:T(8,128)S(1)} %get-tuple-element.153), channel_id=1, source_target_pairs={{0,1},{1,0},{2,3},{3,2},{4,5},{5,4},{6,7},{7,6},{8,9},{9,8},{10,11... | collective-permute-start | bytes 393224 | tf_op jit(solution)/shard_map/cond/branch_1_fun/ppermute | solution.py:396
  16.9 7.4 %collective-permute-start.8 = (f32[12,8,128]{2,1,0:T(8,128)S(1)}, f32[12,8,128]{2,1,0:T(8,128)S(1)}, u32[]{:S(2)}, u32[]{:S(2)}) collective-permute-start(f32[12,8,128]{2,1,0:T(8,128)S(1)} %get-tuple-element.154), channel_id=1, source_target_pairs={{2,1},{3,0},{4,3},{5,2},{6,5},{7,4},{8,7},{9,6},{10,9},{11,8},{12,... | collective-permute-start | bytes 147464 | tf_op jit(solution)/shard_map/cond/branch_1_fun/ppermute | solution.py:396
  18.9 5.5 %collective-permute-start.9 = (f32[6,8,128]{2,1,0:T(8,128)S(1)}, f32[6,8,128]{2,1,0:T(8,128)S(1)}, u32[]{:S(2)}, u32[]{:S(2)}) collective-permute-start(f32[6,8,128]{2,1,0:T(8,128)S(1)} %get-tuple-element.155), channel_id=1, source_target_pairs={{0,3},{1,2},{2,5},{3,4},{4,7},{5,6},{6,9},{7,8},{8,11},{9,10},{10,... | collective-permute-start | bytes 73736 | tf_op jit(solution)/shard_map/cond/branch_1_fun/ppermute | solution.py:396

commit v3 on v2

--- a/solution.py
+++ b/solution.py
@@ -10,6 +10,7 @@
 STEPS = 3
 TILE = 8
 HALF = 4
+GROUP = 4
 TIME_STEP = 0.5
 CURRENT_SCALE = 0.1
 VMEM = pl.BlockSpec(memory_space=pltpu.VMEM)
@@ -164,7 +165,7 @@
         ],
         compiler_params=pltpu.CompilerParams(vmem_limit_bytes=32 * 2**20),
         name="pack",
-    )(*arrays, moved)
+    )(*(pltpu.with_memory_space_constraint(a, pltpu.HBM) for a in (*arrays, moved)))
     own, which, rest = found[:8], found[8], found[9:]
     across, sent = rest[: len(sides)], rest[len(sides) :]
     per_case = 2 + 2 * len(sides)
@@ -191,7 +192,7 @@
 
 
 def prepare_kernel(moves, *refs):
-    own, (ext, keep, gain, current, rows) = refs[:8], refs[8:]
+    own, ext, (keep, gain, current, rows) = refs[:8], refs[8:14], refs[14:]
     planes, width, depth = own[0].shape
     tall = width + TILE
     base = 3 - moves
@@ -206,12 +207,12 @@
         rows[n] = value
     here, mine = pl.ds(base, planes), pl.ds(0, width)
     for a in range(6):
-        ext[a, here, mine] = own[a][...]
+        ext[a][here, mine] = own[a][...]
     keep[here, mine], gain[here, mine] = coefficients(own[CODES][...])
     current[here, mine] = CURRENT_SCALE * own[BUNCH][...].astype(jnp.float32)
     for a in (EX, EY):
-        ext[a, 0] = jnp.zeros((tall, depth), jnp.float32)
-        ext[a, planes + 5] = jnp.zeros((tall, depth), jnp.float32)
+        ext[a][0] = jnp.zeros((tall, depth), jnp.float32)
+        ext[a][planes + 5] = jnp.zeros((tall, depth), jnp.float32)
 
 
 def prepare(moves, own):
@@ -221,9 +222,9 @@
     cells = vmem(planes + 5, tall, depth)
     return pl.pallas_call(
         functools.partial(prepare_kernel, moves),
-        out_shape=[vmem(6, planes + 6, tall, depth), cells, cells, cells, vmem(7, tall, depth)],
+        out_shape=[vmem(planes + 6, tall, depth)] * 6 + [cells] * 3 + [vmem(7, tall, depth)],
         in_specs=[VMEM] * 8,
-        out_specs=[VMEM] * 5,
+        out_specs=[VMEM] * 10,
         compiler_params=pltpu.CompilerParams(vmem_limit_bytes=32 * 2**20),
         cost_estimate=pl.CostEstimate(flops=10**7, bytes_accessed=10**7, transcendentals=0),
         name="prepare",
@@ -231,12 +232,12 @@
 
 
 def steps_kernel(case, n_sides, moved, *refs):
-    rows = refs[4]
-    down, up = refs[5:7]
-    beside = [refs[7 + 3 * n : 10 + 3 * n] for n in range(n_sides)]
-    outs = refs[7 + 3 * n_sides : 13 + 3 * n_sides]
-    ext, keep, gain, current = refs[13 + 3 * n_sides : 17 + 3 * n_sides]
-    final, sems = refs[17 + 3 * n_sides :]
+    rows = refs[9]
+    down, up = refs[10:12]
+    beside = [refs[12 + 3 * n : 15 + 3 * n] for n in range(n_sides)]
+    at = 12 + 3 * n_sides
+    outs, ext = refs[at : at + 6], refs[at + 6 : at + 12]
+    keep, gain, current, final, sems = refs[at + 12 :]
     moves = case[0]
     base = 3 - moves
     _, planes, width, depth = final.shape
@@ -273,7 +274,7 @@
     def put(a, at, count, where, value):
         span = pl.ds(at, count)
         if a < 6:
-            ext[a, span, where] = value
+            ext[a][span, where] = value
         elif a == CODES:
             kept, gained = coefficients(value)
             if where.start:
@@ -300,59 +301,76 @@
     not_last, not_first = lane < depth - 1, lane > 0
 
     def forward_y(v):
-        return jnp.where(not_last, pltpu.roll(v, depth - 1, 1), 0.0) - v
+        return jnp.where(not_last, pltpu.roll(v, depth - 1, 2), 0.0) - v
 
     def backward_y(v):
-        return v - jnp.where(not_first, pltpu.roll(v, 1, 1), 0.0)
+        return v - jnp.where(not_first, pltpu.roll(v, 1, 2), 0.0)
 
     def forward_x(v):
-        return pltpu.roll(v, tall - 1, 0) - v
+        return pltpu.roll(v, tall - 1, 1) - v
 
     def backward_x(v):
-        return v - pltpu.roll(v, 1, 0)
-
-    def magnetic(e):
-        ex, ey, es = ext[EX, e], ext[EY, e], ext[ES, e]
-        bx = ext[BX, e] - (rows[4] * forward_y(es) - rows[5] * (ext[EY, e + 1] - ey))
-        by = ext[BY, e] - rows[6] * ((ext[EX, e + 1] - ex) - forward_x(rows[0] * es))
-        bs = ext[BS, e] - rows[4] * (forward_x(ey) - forward_y(ex))
-        return ex, ey, es, bx, by, bs
+        return v - pltpu.roll(v, 1, 1)
 
     def out_copy(a, plane):
         return pltpu.make_async_copy(final.at[a, plane], outs[a].at[plane], sems.at[a, plane])
+
+    def in_groups(start, count, body):
+        whole = count // GROUP
+        if whole:
+
+            @pl.loop(0, whole)
+            def _(i):
+                body(start + i * GROUP, GROUP)
+
+        if count % GROUP:
+            body(start + whole * GROUP, count % GROUP)
 
     moved_now = 0
     for t in range(STEPS):
         moved_now = moved_now + moved[t]
-        begin = jnp.where(first, base + moved_now, t + 1)
-        end = jnp.where(last, jnp.minimum(planes + 4 - t, planes + 2 + moved_now - moves), planes + 4 - t) + 1
-        _, _, _, bx, by, _ = magnetic(t)
-        ext[BX, t], ext[BY, t] = bx, by
+        done = t == STEPS - 1
+
+        def magnetic(e, count):
+            here, above = pl.ds(e, count), pl.ds(e + 1, count)
+            ex, ey, es = ext[EX][here], ext[EY][here], ext[ES][here]
+            bx = ext[BX][here] - (rows[4] * forward_y(es) - rows[5] * (ext[EY][above] - ey))
+            by = ext[BY][here] - rows[6] * ((ext[EX][above] - ex) - forward_x(rows[0] * es))
+            bs = ext[BS][here] - rows[4] * (forward_x(ey) - forward_y(ex))
+            ext[BX][here], ext[BY][here], ext[BS][here] = bx, by, bs
+
+        def electric(e, count):
+            here, below, cells = pl.ds(e, count), pl.ds(e - 1, count), pl.ds(e - moved_now, count)
+            bx, by, bs = ext[BX][here], ext[BY][here], ext[BS][here]
+            kept, gained = keep[cells], gain[cells]
+            ex = kept * ext[EX][here] + gained * (backward_y(bs) - rows[3] * (by - ext[BY][below]))
+            ey = kept * ext[EY][here] + gained * (
+                rows[2] * ((bx - ext[BX][below]) - backward_x(rows[1] * bs))
+            )
+            es = kept * ext[ES][here] + gained * (backward_x(by) - backward_y(bx) - current[cells])
+            if not done:
+                ext[EX][here], ext[EY][here], ext[ES][here] = ex, ey, es
+                return
+            for a, value in enumerate((ex, ey, es, bx, by, bs)):
+                final[a, pl.ds(e - 3, count)] = value[:, :width]
+                for n in range(count):
+                    out_copy(a, e - 3 + n).start()
+
+        in_groups(t, planes + 5 - 2 * t, magnetic)
 
         @pl.when(first)
         def _():
-            ext[BX, begin - 1] = jnp.zeros((tall, depth), jnp.float32)
-            ext[BY, begin - 1] = jnp.zeros((tall, depth), jnp.float32)
-
-        def plane(e, carry):
-            ex, ey, es, bx, by, bs = magnetic(e)
-            kept, gained = keep[e - moved_now], gain[e - moved_now]
-            ex = kept * ex + gained * (backward_y(bs) - rows[3] * (by - ext[BY, e - 1]))
-            ey = kept * ey + gained * (rows[2] * ((bx - ext[BX, e - 1]) - backward_x(rows[1] * bs)))
-            es = kept * es + gained * (backward_x(by) - backward_y(bx) - current[e - moved_now])
-            for a, value in enumerate((ex, ey, es, bx, by, bs)):
-                if t < STEPS - 1:
-                    ext[a, e] = value
-                else:
-                    final[a, e - 3] = value[:width]
-                    if a in (BX, BY):
-                        ext[a, e] = value
-            if t == STEPS - 1:
-                for a in range(6):
-                    out_copy(a, e - 3).start()
-            return carry
-
-        lax.fori_loop(begin, end, plane, 0)
+            for a in (BX, BY):
+                ext[a][base + moved_now - 1] = jnp.zeros((tall, depth), jnp.float32)
+
+        in_groups(t + 1, planes + 4 - 2 * t, electric)
+
+        if not done:
+
+            @pl.when(last)
+            def _():
+                for a in (EX, EY, ES):
+                    ext[a][planes + base + moved_now] = jnp.zeros((tall, depth), jnp.float32)
 
     def finish(plane, carry):
         for a in range(6):
@@ -365,14 +383,14 @@
 def advance(case, moved, shape, ready, ghosts):
     planes, width, depth = shape
     block = jax.ShapeDtypeStruct(shape, jnp.float32)
-    n_in = 6 + len(ghosts)
+    n_in = 11 + len(ghosts)
     like = lambda x: pltpu.VMEM(x.shape, x.dtype)
     found = pl.pallas_call(
         functools.partial(steps_kernel, case, (len(ghosts) - 2) // 3),
-        out_shape=[block] * 6 + [like(x) for x in ready[:4]],
+        out_shape=[block] * 6 + [like(x) for x in ready[:9]],
         in_specs=[SMEM] + [VMEM] * (n_in - 1),
-        out_specs=[ANY] * 6 + [VMEM] * 4,
-        input_output_aliases={1: 6, 2: 7, 3: 8, 4: 9},
+        out_specs=[ANY] * 6 + [VMEM] * 9,
+        input_output_aliases={1 + n: 6 + n for n in range(9)},
         scratch_shapes=[
             pltpu.VMEM((6, planes, width, depth), jnp.float32),
             pltpu.SemaphoreType.DMA((6, planes)),

time: 35.7 us -> 27.1 us (0.76)
  the two profiles are of different devices: /device:TPU:1 before, /device:TPU:6 now
where the time goes in v3:
time: 27.1 us; the launch traced here: 26.7 us
  starting transfers between devices  11.8 us (44%)
  Pallas kernels  7.16 us (26%)
  waiting for transfers between devices  6.43 us (24%)
  between operations  0.66 us (2%)
  local copies, waits for them, and re-layouts  0.65 us (2%)
    ppermute x5, starting transfers between devices, passed(): return lax.ppermute(block, ('gz', 'gx'), route)  11.8 us
    ppermute x5, waiting for transfers between devices, passed(): return lax.ppermute(block, ('gz', 'gx'), route)  6.43 us
    pallas_call x1, Pallas kernels, advance(): pl.pallas_call(functools.partial(steps_kernel, case, (len(ghosts) - 2) //...  5.15 us
    pallas_call x1, Pallas kernels, pack(): pl.pallas_call(functools.partial(pack_kernel, sides), out_shape=shapes, i...  1.77 us
    unnamed x2, local copies, waits for them, and re-layouts  0.65 us
  transfers between devices with their start and end apart: 5, of which 2 were waited for; matrix products, arithmetic and copies ran while one was open for 0% of the time, Pallas kernels for 1%

profile of v3, /device:TPU:6, one launch (start us, length us, event | category | flops | bytes accessed | tf_op | source)
XLA Modules:
  0.0 26.7 jit_solution(5092834373564693232)
XLA Ops:
  0.6 1.8 %pack.1 = (f32[8,64,128]{2,1,0:T(8,128)S(1)}, f32[8,64,128]{2,1,0:T(8,128)S(1)}, f32[8,64,128]{2,1,0:T(8,128)S(1)}, f32[8,64,128]{2,1,0:T(8,128)S(1)}, f32[8,64,...) custom-call(f32[8,64,128]{2,1,0:T(8,128)} %refs_0_.1, ...), custom_call_target="tpu_custom_call" | custom-call | tf_op jit(solution)/shard_map/pack/pallas_call | solution.py:156
  2.4 0.0 copy-start
  2.4 0.6 %copy-done = s32[3]{0:T(128)S(1)} copy-done((s32[3]{0:T(128)S(1)}, s32[3]{0:T(128)}, u32[]{:S(2)}) %copy-start) | copy-done | bytes 36
  3.1 23.7 %conditional.1 = (f32[8,64,128]{2,1,0:T(8,128)}, f32[8,64,128]{2,1,0:T(8,128)}, f32[8,64,128]{2,1,0:T(8,128)}, f32[8,64,128]{2,1,0:T(8,128)}, f32[8,64,128]{2,1,0:T(8,128)}, /*index=5*/f32[8,64,128]{2,1,0:T(8,128)}) conditional(s32[]{:T(128)} %bitcast, (f32[8,64,128]{2,1,0:T(8,128)S(1)}, f32[8,64,128]{2,1,0:T(8,128)S(1)}, ...), branch_computations={%region_0.0_spmd, %region_1.0_spmd, %region_2.0_spmd, %region_3.0_... | conditional | flops 10000000 | bytes 15275896 | solution.py:434
  3.1 1.9 %collective-permute-start.15 = (f32[31,64,128]{2,1,0:T(8,128)S(1)}, f32[31,64,128]{2,1,0:T(8,128)S(1)}, u32[]{:S(2)}, u32[]{:S(2)}) collective-permute-start(f32[31,64,128]{2,1,0:T(8,128)S(1)} %get-tuple-element.221), channel_id=1, source_target_pairs={{2,0},{3,1},{4,2},{5,3},{6,4},{7,5},{8,6},{9,7},{10,8},{11,9},{12,... | collective-permute-start | bytes 3047432 | tf_op jit(solution)/shard_map/cond/branch_3_fun/ppermute | solution.py:414
  5.0 0.6 %collective-permute-start.17 = (f32[32,8,128]{2,1,0:T(8,128)S(1)}, f32[32,8,128]{2,1,0:T(8,128)S(1)}, u32[]{:S(2)}, u32[]{:S(2)}) collective-permute-start(f32[32,8,128]{2,1,0:T(8,128)S(1)} %get-tuple-element.223), channel_id=1, source_target_pairs={{0,1},{1,0},{2,3},{3,2},{4,5},{5,4},{6,7},{7,6},{8,9},{9,8},{10,11... | collective-permute-start | bytes 393224 | tf_op jit(solution)/shard_map/cond/branch_3_fun/ppermute | solution.py:414
  5.6 2.1 %collective-permute-start.16 = (f32[3,64,128]{2,1,0:T(8,128)S(1)}, f32[3,64,128]{2,1,0:T(8,128)S(1)}, u32[]{:S(2)}, u32[]{:S(2)}) collective-permute-start(f32[3,64,128]{2,1,0:T(8,128)S(1)} %get-tuple-element.222), channel_id=1, source_target_pairs={{0,2},{1,3},{2,4},{3,5},{4,6},{5,7},{6,8},{7,9},{8,10},{9,11},{10,... | collective-permute-start | bytes 294920 | tf_op jit(solution)/shard_map/cond/branch_3_fun/ppermute | solution.py:414
  7.7 4.4 %collective-permute-start.18 = (f32[16,8,128]{2,1,0:T(8,128)S(1)}, f32[16,8,128]{2,1,0:T(8,128)S(1)}, u32[]{:S(2)}, u32[]{:S(2)}) collective-permute-start(f32[16,8,128]{2,1,0:T(8,128)S(1)} %get-tuple-element.224), channel_id=1, source_target_pairs={{2,1},{3,0},{4,3},{5,2},{6,5},{7,4},{8,7},{9,6},{10,9},{11,8},{12,... | collective-permute-start | bytes 196616 | tf_op jit(solution)/shard_map/cond/branch_3_fun/ppermute | solution.py:414
  12.1 2.8 %collective-permute-start.19 = (f32[2,8,128]{2,1,0:T(8,128)S(1)}, f32[2,8,128]{2,1,0:T(8,128)S(1)}, u32[]{:S(2)}, u32[]{:S(2)}) collective-permute-start(f32[2,8,128]{2,1,0:T(8,128)S(1)} %get-tuple-element.225), channel_id=1, source_target_pairs={{0,3},{1,2},{2,5},{3,4},{4,7},{5,6},{6,9},{7,8},{8,11},{9,10},{10,... | collective-permute-start | bytes 24584 | tf_op jit(solution)/shard_map/cond/branch_3_fun/ppermute | solution.py:414
  14.9 0.2 prepare.7
  15.2 2.9 %collective-permute-done.19.refs_14_ = f32[2,8,128]{2,1,0:T(8,128)S(1)} collective-permute-done((f32[2,8,128]{2,1,0:T(8,128)S(1)}, f32[2,8,128]{2,1,0:T(8,128)S(1)}, u32[]{:S(2)}, u32[]{:S(2)}) %collective-permute-start.19) | collective-permute-done | bytes 8224 | tf_op jit(solution)/shard_map/cond/branch_3_fun/ppermute | solution.py:414
  18.1 0.0 collective-permute-done.18.refs_13_
  18.1 3.5 %collective-permute-done.16.refs_11_ = f32[3,64,128]{2,1,0:T(8,128)S(1)} collective-permute-done((f32[3,64,128]{2,1,0:T(8,128)S(1)}, f32[3,64,128]{2,1,0:T(8,128)S(1)}, u32[]{:S(2)}, u32[]{:S(2)}) %collective-permute-start.16) | collective-permute-done | bytes 98336 | tf_op jit(solution)/shard_map/cond/branch_3_fun/ppermute | solution.py:414
  21.6 0.0 collective-permute-done.17.refs_12_
  21.6 0.0 collective-permute-done.15.refs_10_
  21.6 5.2 %steps.7 = (f32[8,64,128]{2,1,0:T(8,128)}, f32[8,64,128]{2,1,0:T(8,128)}, f32[8,64,128]{2,1,0:T(8,128)}, f32[8,64,128]{2,1,0:T(8,128)}, f32[8,64,128]{2,1,0:T(8,...) custom-call(s32[3]{0:T(128)S(1)} %get-tuple-element.202.moved, ...), custom_call_target="tpu_custom_call", output_to_operand_aliasing={{6}: (1, {}), {7}: (2, {}), {8}: (3, {}), {9}: (4, {}), {10... | custom-call | tf_op jit(solution)/shard_map/cond/branch_3_fun/steps/pallas_call | solution.py:388
Async XLA Ops:
  2.4 0.7 %copy-start = (s32[3]{0:T(128)S(1)}, s32[3]{0:T(128)}, u32[]{:S(2)}) copy-start(s32[3]{0:T(128)} %refs_8_.1) | copy-start | bytes 40
  3.1 18.5 %collective-permute-start.15 = (f32[31,64,128]{2,1,0:T(8,128)S(1)}, f32[31,64,128]{2,1,0:T(8,128)S(1)}, u32[]{:S(2)}, u32[]{:S(2)}) collective-permute-start(f32[31,64,128]{2,1,0:T(8,128)S(1)} %get-tuple-element.221), channel_id=1, source_target_pairs={{2,0},{3,1},{4,2},{5,3},{6,4},{7,5},{8,6},{9,7},{10,8},{11,9},{12,... | collective-permute-start | bytes 3047432 | tf_op jit(solution)/shard_map/cond/branch_3_fun/ppermute | solution.py:414
  5.0 16.6 %collective-permute-start.17 = (f32[32,8,128]{2,1,0:T(8,128)S(1)}, f32[32,8,128]{2,1,0:T(8,128)S(1)}, u32[]{:S(2)}, u32[]{:S(2)}) collective-permute-start(f32[32,8,128]{2,1,0:T(8,128)S(1)} %get-tuple-element.223), channel_id=1, source_target_pairs={{0,1},{1,0},{2,3},{3,2},{4,5},{5,4},{6,7},{7,6},{8,9},{9,8},{10,11... | collective-permute-start | bytes 393224 | tf_op jit(solution)/shard_map/cond/branch_3_fun/ppermute | solution.py:414
  5.6 16.0 %collective-permute-start.16 = (f32[3,64,128]{2,1,0:T(8,128)S(1)}, f32[3,64,128]{2,1,0:T(8,128)S(1)}, u32[]{:S(2)}, u32[]{:S(2)}) collective-permute-start(f32[3,64,128]{2,1,0:T(8,128)S(1)} %get-tuple-element.222), channel_id=1, source_target_pairs={{0,2},{1,3},{2,4},{3,5},{4,6},{5,7},{6,8},{7,9},{8,10},{9,11},{10,... | collective-permute-start | bytes 294920 | tf_op jit(solution)/shard_map/cond/branch_3_fun/ppermute | solution.py:414
  7.7 10.4 %collective-permute-start.18 = (f32[16,8,128]{2,1,0:T(8,128)S(1)}, f32[16,8,128]{2,1,0:T(8,128)S(1)}, u32[]{:S(2)}, u32[]{:S(2)}) collective-permute-start(f32[16,8,128]{2,1,0:T(8,128)S(1)} %get-tuple-element.224), channel_id=1, source_target_pairs={{2,1},{3,0},{4,3},{5,2},{6,5},{7,4},{8,7},{9,6},{10,9},{11,8},{12,... | collective-permute-start | bytes 196616 | tf_op jit(solution)/shard_map/cond/branch_3_fun/ppermute | solution.py:414
  12.1 6.0 %collective-permute-start.19 = (f32[2,8,128]{2,1,0:T(8,128)S(1)}, f32[2,8,128]{2,1,0:T(8,128)S(1)}, u32[]{:S(2)}, u32[]{:S(2)}) collective-permute-start(f32[2,8,128]{2,1,0:T(8,128)S(1)} %get-tuple-element.225), channel_id=1, source_target_pairs={{0,3},{1,2},{2,5},{3,4},{4,7},{5,6},{6,9},{7,8},{8,11},{9,10},{10,... | collective-permute-start | bytes 24584 | tf_op jit(solution)/shard_map/cond/branch_3_fun/ppermute | solution.py:414

commit v4 on v3

v4 whole, which is shorter than its diff:
```python
import functools

import jax
import jax.numpy as jnp
from jax import lax
from jax.experimental import pallas as pl
from jax.experimental.pallas import tpu as pltpu
from jax.sharding import PartitionSpec as P

STEPS = 3
TILE = 8
HALF = 4
GROUP = 4
TIME_STEP = 0.5
CURRENT_SCALE = 0.1
VMEM = pl.BlockSpec(memory_space=pltpu.VMEM)
SMEM = pl.BlockSpec(memory_space=pltpu.SMEM)
ANY = pl.BlockSpec(memory_space=pl.ANY)
EX, EY, ES, BX, BY, BS, CODES, BUNCH = range(8)
CASES = ((1, 1), (1, 0), (2, 1), (2, 0))


def down_counts(case):
    moves, now = case
    later = moves - now
    return (moves + 2,) * 6 + (later + 2, later + 1)


def up_counts(case):
    moves, now = case
    below = 3 - moves
    later = moves - now
    return (below - 1, below - 1, below, below, below, below - 1, 2 - later, 2 - later)


def offsets(counts):
    starts = [0]
    for count in counts:
        starts.append(starts[-1] + count)
    return starts


def half_up(count):
    return (count + 1) // 2


def column_scales(place, total):
    place = place.astype(jnp.float32)
    whole = 1.0 + (place - total / 2) / (2 * total)
    half = 1.0 + (place + 0.5 - total / 2) / (2 * total)
    return whole, half


def turned(tiles):
    return pltpu.roll(tiles, HALF, 1)


def pack_kernel(sides, *refs):
    sources, moved = refs[:8], refs[8]
    own = refs[9:17]
    which, moved_here = refs[17:19]
    across = refs[19 : 19 + len(sides)]
    sent = refs[19 + len(sides) : -2]
    sems, moved_sem = refs[-2:]
    per_case = 2 + 2 * len(sides)
    planes, width, depth = own[0].shape
    gx = lax.axis_index("gx")
    total = width * lax.axis_size("gx")

    get_moved = pltpu.make_async_copy(moved, moved_here, moved_sem)
    get_moved.start()
    copies = [pltpu.make_async_copy(sources[a], own[a], sems.at[a]) for a in range(8)]
    for item in copies:
        item.start()
    get_moved.wait()
    now = moved_here[0]
    later = moved_here[1] + moved_here[2]
    case_index = jnp.where(now + later == 1, 1 - now, 3 - now)
    which[0] = case_index

    row = lax.broadcasted_iota(jnp.int32, (width, depth), 0)
    whole, half = column_scales(gx * width + row, total)
    step_whole, step_half = TIME_STEP / whole, TIME_STEP / half
    low = lax.broadcasted_iota(jnp.int32, (1, TILE, depth), 1) < HALF

    def edge_of(side):
        if side == "swap":
            return pl.multiple_of(jnp.where(gx == 0, width - TILE, 0), TILE), gx == 0
        return (width - TILE, True) if side == "right" else (0, False)

    def paired(first, second, high):
        if high is True:
            return jnp.where(low, turned(first), second)
        if high is False:
            return jnp.where(low, first, turned(second))
        return jnp.where(
            low,
            jnp.where(high, turned(first), first),
            jnp.where(high, second, turned(second)),
        )

    for item in copies:
        item.wait()

    for n, side in enumerate(sides):
        at, high = edge_of(side)
        for a in range(4):
            first = own[a][:, pl.ds(at, TILE)]
            second = own[a + 4][:, pl.ds(at, TILE)].astype(jnp.float32)
            across[n][pl.ds(a * planes, planes)] = paired(first, second, high)

    for c, case in enumerate(CASES):
        down, up = sent[c * per_case : c * per_case + 2]
        corners = sent[c * per_case + 2 : (c + 1) * per_case]
        downs, ups = down_counts(case), up_counts(case)
        down_at, up_at = offsets(downs), offsets(ups)
        moves = case[0]

        @pl.when(case_index == c)
        def _():
            for a in range(8):
                if downs[a]:
                    down[pl.ds(down_at[a], downs[a])] = own[a][: downs[a]].astype(jnp.float32)
                if ups[a]:
                    up[pl.ds(up_at[a], ups[a])] = own[a][planes - ups[a] :].astype(jnp.float32)
            far = moves + 2
            down[down_at[BX] + far - 1] = own[BX][far - 1] + step_whole * own[EY][far]
            down[down_at[BY] + far - 1] = own[BY][far - 1] - step_half * own[EX][far]
            far = planes - (3 - moves)
            up[up_at[BX]] = own[BX][far] - step_whole * own[EY][far]
            up[up_at[BY]] = own[BY][far] + step_half * own[EX][far]
            for n, side in enumerate(sides):
                at, high = edge_of(side)
                for block, corner, count in (
                    (down, corners[2 * n], down_at[-1]),
                    (up, corners[2 * n + 1], up_at[-1]),
                ):
                    middle = half_up(count)
                    rest = count - middle
                    first = block[pl.ds(0, middle), pl.ds(at, TILE)]
                    second = block[pl.ds(middle, rest), pl.ds(at, TILE)]
                    corner[pl.ds(0, rest)] = paired(first[:rest], second, high)
                    if rest < middle:
                        corner[pl.ds(rest, 1)] = paired(first[rest:], first[rest:], high)


def pack(sides, arrays, moved):
    planes, width, depth = arrays[0].shape
    vmem = lambda *shape: pltpu.VMEM(shape, jnp.float32)
    shapes = [pltpu.VMEM(a.shape, a.dtype) for a in arrays] + [pltpu.SMEM((1,), jnp.int32), pltpu.SMEM((STEPS,), jnp.int32)]
    shapes += [vmem(4 * planes, TILE, depth)] * len(sides)
    for case in CASES:
        n_down, n_up = sum(down_counts(case)), sum(up_counts(case))
        shapes += [vmem(n_down, width, depth), vmem(n_up, width, depth)]
        shapes += [vmem(half_up(n_down), TILE, depth), vmem(half_up(n_up), TILE, depth)] * len(sides)
    found = pl.pallas_call(
        functools.partial(pack_kernel, sides),
        out_shape=shapes,
        in_specs=[ANY] * 9,
        out_specs=[VMEM] * 8 + [SMEM] * 2 + [VMEM] * (len(shapes) - 10),
        scratch_shapes=[
            pltpu.SemaphoreType.DMA((8,)),
            pltpu.SemaphoreType.DMA,
        ],
        compiler_params=pltpu.CompilerParams(vmem_limit_bytes=32 * 2**20),
        name="pack",
    )(*(pltpu.with_memory_space_constraint(a, pltpu.HBM) for a in (*arrays, moved)))
    own, which, moved_here, rest = found[:8], found[8], found[9], found[10:]
    across, sent = rest[: len(sides)], rest[len(sides) :]
    per_case = 2 + 2 * len(sides)
    return own, which, moved_here, across, [sent[c * per_case : (c + 1) * per_case] for c in range(len(CASES))]


def coefficients(code):
    kind = code.dtype.type
    five, six, seven = code == kind(5), code == kind(6), code == kind(7)
    keep = jnp.where(five, 0.0, jnp.where(six, 0.8 / 1.2, jnp.where(seven, 0.4 / 1.6, 1.0)))
    gain = jnp.where(
        five,
        0.0,
        jnp.where(six, TIME_STEP / 1.2, jnp.where(seven, TIME_STEP / 1.6, TIME_STEP)),
    )
    return keep, gain


def ghost_inside(width, depth):
    gx = lax.axis_index("gx")
    row = lax.broadcasted_iota(jnp.int32, (1, TILE, depth), 1)
    right = gx < lax.axis_size("gx") - 1
    return jnp.where(row < HALF, right.astype(jnp.int32), (gx > 0).astype(jnp.int32)) == 1


def spread_tiles(beside, upper, depth):
    gx = lax.axis_index("gx")
    if len(beside) == 1:
        same = (gx > 0) if upper else (gx == 0)
        found = jnp.where(same, beside[0], turned(beside[0]))
    else:
        from_left, from_right = beside
        if upper:
            from_right = turned(from_right)
        else:
            from_left = turned(from_left)
        low = lax.broadcasted_iota(jnp.int32, (1, TILE, depth), 1) < HALF
        found = jnp.where(low, from_right, from_left)
    return found


def pieces(beside, at, count, middle):
    depth = beside[0].shape[-1]
    cut = min(max(middle - at, 0), count)
    if cut:
        yield 0, cut, spread_tiles([side[pl.ds(at, cut)] for side in beside], False, depth)
    if cut < count:
        span = pl.ds(at + cut - middle, count - cut)
        yield cut, count - cut, spread_tiles([side[span] for side in beside], True, depth)


class Cells:
    def __init__(self, refs, width):
        self.ext, (self.keep, self.gain, self.current, self.rows) = refs[:6], refs[6:]
        self.width = width
        self.tall, self.depth = self.keep.shape[1:]
        self.ghost_in = ghost_inside(width, self.depth)
        lane = lax.broadcasted_iota(jnp.int32, (self.tall, self.depth), 1)
        self.not_last, self.not_first = lane < self.depth - 1, lane > 0

    def put(self, a, at, count, value, ghost):
        here = pl.ds(at, count)
        where = pl.ds(self.width, TILE) if ghost else pl.ds(0, self.width)
        mask = (lambda v: jnp.where(self.ghost_in, v, 0.0)) if ghost else (lambda v: v)
        if a < 6:
            self.ext[a][here, where] = mask(value)
        elif a == CODES:
            kept, gained = coefficients(value)
            self.keep[here, where], self.gain[here, where] = mask(kept), mask(gained)
        else:
            self.current[here, where] = CURRENT_SCALE * mask(value.astype(jnp.float32))

    def forward_y(self, v):
        return jnp.where(self.not_last, pltpu.roll(v, self.depth - 1, 2), 0.0) - v

    def backward_y(self, v):
        return v - jnp.where(self.not_first, pltpu.roll(v, 1, 2), 0.0)

    def forward_x(self, v):
        return pltpu.roll(v, self.tall - 1, 1) - v

    def backward_x(self, v):
        return v - pltpu.roll(v, 1, 1)

    def magnetic(self, e, count):
        ext, rows = self.ext, self.rows
        here, above = pl.ds(e, count), pl.ds(e + 1, count)
        ex, ey, es = ext[EX][here], ext[EY][here], ext[ES][here]
        bx = ext[BX][here] - (rows[4] * self.forward_y(es) - rows[5] * (ext[EY][above] - ey))
        by = ext[BY][here] - rows[6] * ((ext[EX][above] - ex) - self.forward_x(rows[0] * es))
        bs = ext[BS][here] - rows[4] * (self.forward_x(ey) - self.forward_y(ex))
        ext[BX][here], ext[BY][here], ext[BS][here] = bx, by, bs

    def electric(self, e, count, moved_now):
        ext, rows = self.ext, self.rows
        here, below, cells = pl.ds(e, count), pl.ds(e - 1, count), pl.ds(e - moved_now, count)
        bx, by, bs = ext[BX][here], ext[BY][here], ext[BS][here]
        kept, gained = self.keep[cells], self.gain[cells]
        ex = kept * ext[EX][here] + gained * (self.backward_y(bs) - rows[3] * (by - ext[BY][below]))
        ey = kept * ext[EY][here] + gained * (
            rows[2] * ((bx - ext[BX][below]) - self.backward_x(rows[1] * bs))
        )
        es = kept * ext[ES][here] + gained * (
            self.backward_x(by) - self.backward_y(bx) - self.current[cells]
        )
        ext[EX][here], ext[EY][here], ext[ES][here] = ex, ey, es

    def leave(self, plane):
        for a in (BX, BY):
            self.ext[a][plane] = jnp.zeros((self.tall, self.depth), jnp.float32)


def in_groups(start, count, body):
    whole = max(count, 0) // GROUP
    if whole:

        @pl.loop(0, whole)
        def _(i):
            body(start + i * GROUP, GROUP)

    if count > 0 and count % GROUP:
        body(start + whole * GROUP, count % GROUP)


def prepare_kernel(moves, n_sides, moved, *refs):
    own, beside = refs[:8], refs[8 : 8 + n_sides]
    planes, width, depth = own[0].shape
    cells = Cells(refs[8 + n_sides :], width)
    tall, rows = cells.tall, cells.rows
    base = 3 - moves
    top = base + planes - 1
    total = width * lax.axis_size("gx")

    row = lax.broadcasted_iota(jnp.int32, (tall, depth), 0)
    place = lax.axis_index("gx") * width + jnp.where(row < width + HALF, row, row - tall)
    inside = (place >= 0) & (place < total)
    whole, half = column_scales(place, total)
    step = jnp.where(inside, TIME_STEP, 0.0)
    for n, value in enumerate((whole, half, 1.0 / whole, 1.0 / half, step, step / whole, step / half)):
        rows[n] = value
    for a in range(8):
        cells.put(a, base, planes, own[a][...], False)
        for at, count, value in pieces(beside, a * planes, planes, 4 * planes):
            cells.put(a, base + at, count, value, True)
    for a in (EX, EY):
        cells.ext[a][0] = jnp.zeros((tall, depth), jnp.float32)
        cells.ext[a][planes + 5] = jnp.zeros((tall, depth), jnp.float32)

    moved_now = 0
    for t in range(STEPS):
        moved_now = moved_now + moved[t]
        in_groups(base + t, planes - 1 - 2 * t, cells.magnetic)

        @pl.when((lax.axis_index("gz") == 0) & (moved_now == t + 1))
        def _():
            cells.leave(base + t)

        in_groups(base + t + 1, planes - 2 - 2 * t, lambda e, n: cells.electric(e, n, moved_now))


def prepare(moves, moved, own, beside):
    planes, width, depth = own[0].shape
    tall = width + TILE
    vmem = lambda *shape: pltpu.VMEM(shape, jnp.float32)
    shapes = [vmem(planes + 6, tall, depth)] * 6 + [vmem(planes + 5, tall, depth)] * 3
    shapes += [vmem(7, tall, depth)]
    return pl.pallas_call(
        functools.partial(prepare_kernel, moves, len(beside)),
        out_shape=shapes,
        in_specs=[SMEM] + [VMEM] * (8 + len(beside)),
        out_specs=[VMEM] * len(shapes),
        compiler_params=pltpu.CompilerParams(vmem_limit_bytes=32 * 2**20),
        cost_estimate=pl.CostEstimate(flops=10**7, bytes_accessed=10**7, transcendentals=0),
        name="prepare",
    )(moved, *own, *beside)


def steps_kernel(case, n_sides, planes, width, moved, *refs):
    rows, (down, up) = refs[9], refs[10:12]
    side_down, side_up = refs[12 : 12 + n_sides], refs[12 + n_sides : 12 + 2 * n_sides]
    at = 12 + 2 * n_sides
    outs = refs[at : at + 6]
    cells = Cells((*refs[at + 6 : at + 15], rows), width)
    sems = refs[at + 15]
    ext = cells.ext
    moves = case[0]
    base = 3 - moves
    top = base + planes - 1
    first = lax.axis_index("gz") == 0
    last = lax.axis_index("gz") == lax.axis_size("gz") - 1
    downs, ups = down_counts(case), up_counts(case)
    down_at, up_at = offsets(downs), offsets(ups)
    copies = []

    def send(a, start, end):
        if end > start:
            item = pltpu.make_async_copy(
                ext[a].at[pl.ds(start, end - start), pl.ds(0, width)],
                outs[a].at[pl.ds(start - 3, end - start)],
                sems.at[len(copies)],
            )
            item.start()
            copies.append(item)

    for a in range(6):
        send(a, base + (2 if a >= BX else 3), top - 2)

    for block, sides, counts, starts, is_down in (
        (down, side_down, downs, down_at, True),
        (up, side_up, ups, up_at, False),
    ):
        for a in range(8):
            if counts[a]:
                to = top + 1 if is_down else base - counts[a]
                cells.put(a, to, counts[a], block[pl.ds(starts[a], counts[a])], False)
                for at, count, value in pieces(sides, starts[a], counts[a], half_up(starts[-1])):
                    cells.put(a, to + at, count, value, True)

    moved_now = 0
    for t in range(STEPS):
        moved_now = moved_now + moved[t]
        cells.magnetic(t, base)
        cells.magnetic(top - t, moves + 3)

        @pl.when(first)
        def _():
            cells.leave(base + moved_now - 1)

        if t == STEPS - 1:
            for a in (BX, BY, BS):
                send(a, 3, base + 2)
                send(a, top - 2, planes + 3)
        cells.electric(t + 1, base, moved_now)
        if t == STEPS - 1:
            for a in (EX, EY, ES):
                send(a, 3, base + 3)
        cells.electric(top - t, moves + 3, moved_now)
        if t == STEPS - 1:
            for a in (EX, EY, ES):
                send(a, top - 2, planes + 3)
        else:

            @pl.when(last)
            def _():
                for a in (EX, EY, ES):
                    ext[a][top + 1 + moved_now] = jnp.zeros((cells.tall, cells.depth), jnp.float32)

    for item in copies:
        item.wait()


def advance(case, moved, shape, ready, ghosts):
    planes, width, depth = shape
    block = jax.ShapeDtypeStruct(shape, jnp.float32)
    n_in = 11 + len(ghosts)
    found = pl.pallas_call(
        functools.partial(steps_kernel, case, (len(ghosts) - 2) // 2, planes, width),
        out_shape=[block] * 6 + [pltpu.VMEM(x.shape, x.dtype) for x in ready[:9]],
        in_specs=[SMEM] + [VMEM] * (n_in - 1),
        out_specs=[ANY] * 6 + [VMEM] * 9,
        input_output_aliases={1 + n: 6 + n for n in range(9)},
        scratch_shapes=[pltpu.SemaphoreType.DMA((18,))],
        compiler_params=pltpu.CompilerParams(vmem_limit_bytes=32 * 2**20),
        name="steps",
    )(moved, *ready, *ghosts)
    return tuple(found[:6])


def passed(block, dz, side):
    size_z, size_x = lax.axis_size("gz"), lax.axis_size("gx")
    steps_x = {"swap": (1, -1), "right": (1,), "left": (-1,), None: (0,)}[side]
    route = [
        (z * size_x + x, (z + dz) * size_x + x + dx)
        for z in range(size_z)
        for x in range(size_x)
        for dx in steps_x
        if 0 <= z + dz < size_z and 0 <= x + dx < size_x
    ]
    return lax.ppermute(block, ("gz", "gx"), route)


def on_device(*args):
    arrays, moved = args[:8], args[8]
    arrays = arrays[:6] + (arrays[7], arrays[6])
    sides = ("swap",) if lax.axis_size("gx") == 2 else ("right", "left")
    own, which, moved, across, sent = pack(sides, arrays, moved)

    def run(c, own, across, sent, moved):
        case, blocks = CASES[c], sent[c]
        down, up = passed(blocks[0], -1, None), passed(blocks[1], 1, None)
        beside = [passed(across[n], 0, side) for n, side in enumerate(sides)]
        side_down = [passed(blocks[2 + 2 * n], -1, side) for n, side in enumerate(sides)]
        side_up = [passed(blocks[3 + 2 * n], 1, side) for n, side in enumerate(sides)]
        ready = prepare(case[0], moved, own, beside)
        return advance(case, moved, own[0].shape, ready, [down, up] + side_down + side_up)

    return lax.switch(
        which[0],
        [functools.partial(run, c) for c in range(len(CASES))],
        own,
        across,
        sent,
        moved,
    )


def solution(mesh):
    block = P("gz", "gx", None)
    return jax.shard_map(
        on_device,
        mesh=mesh,
        in_specs=(block,) * 8 + (P(),),
        out_specs=(block,) * 6,
        check_vma=False,
    )
```

time: 27.1 us -> 24.4 us (0.900)
  the two profiles are of different devices: /device:TPU:6 before, /device:TPU:1 now
where the time goes in v4:
time: 24.4 us; the launch traced here: 24.2 us
  starting transfers between devices  14.2 us (58%)
  Pallas kernels  6.02 us (25%)
  waiting for transfers between devices  2.83 us (12%)
  between operations  0.83 us (3%)
  loops' own time  0.32 us (1%)
    ppermute x5, starting transfers between devices, passed(): return lax.ppermute(block, ('gz', 'gx'), route)  14.2 us
    ppermute x5, waiting for transfers between devices, passed(): return lax.ppermute(block, ('gz', 'gx'), route)  2.83 us
    pallas_call x1, Pallas kernels, advance(): pl.pallas_call(functools.partial(steps_kernel, case, (len(ghosts) - 2) //...  2.66 us
    pallas_call x1, Pallas kernels, pack(): pl.pallas_call(functools.partial(pack_kernel, sides), out_shape=shapes, i...  1.76 us
    pallas_call x1, Pallas kernels, prepare(): pl.pallas_call(functools.partial(prepare_kernel, moves, len(beside)), out...  1.6 us
  transfers between devices with their start and end apart: 5, of which 1 were waited for; matrix products, arithmetic and copies ran while one was open for 0% of the time, Pallas kernels for 7%

profile of v4, /device:TPU:1, one launch (start us, length us, event | category | flops | bytes accessed | tf_op | source)
XLA Modules:
  0.0 24.2 jit_solution(7050114474880047686)
XLA Ops:
  0.6 1.8 %pack.1 = (f32[8,64,128]{2,1,0:T(8,128)S(1)}, f32[8,64,128]{2,1,0:T(8,128)S(1)}, f32[8,64,128]{2,1,0:T(8,128)S(1)}, f32[8,64,128]{2,1,0:T(8,128)S(1)}, f32[8,64,...) custom-call(f32[8,64,128]{2,1,0:T(8,128)} %refs_0_.1, ...), custom_call_target="tpu_custom_call" | custom-call | tf_op jit(solution)/shard_map/pack/pallas_call | solution.py:156
  2.4 21.6 %conditional.1 = (f32[8,64,128]{2,1,0:T(8,128)}, f32[8,64,128]{2,1,0:T(8,128)}, f32[8,64,128]{2,1,0:T(8,128)}, f32[8,64,128]{2,1,0:T(8,128)}, f32[8,64,128]{2,1,0:T(8,128)}, /*index=5*/f32[8,64,128]{2,1,0:T(8,128)}) conditional(s32[]{:T(128)} %bitcast, (f32[32,8,128]{2,1,0:T(8,128)S(1)}, s32[3]{0:T(128)S(4)}, ...), branch_computations={%region_0.0_spmd, %region_1.0_spmd, %region_2.0_spmd, %region_3.0_... | conditional | flops 10000000 | bytes 15275896 | solution.py:464
  2.4 2.0 %collective-permute-start.6 = (f32[23,64,128]{2,1,0:T(8,128)S(1)}, f32[23,64,128]{2,1,0:T(8,128)S(1)}, u32[]{:S(2)}, u32[]{:S(2)}) collective-permute-start(f32[23,64,128]{2,1,0:T(8,128)S(1)} %get-tuple-element.162), channel_id=1, source_target_pairs={{2,0},{3,1},{4,2},{5,3},{6,4},{7,5},{8,6},{9,7},{10,8},{11,9},{12,... | collective-permute-start | bytes 2261000 | tf_op jit(solution)/shard_map/cond/branch_1_fun/ppermute | solution.py:446
  4.4 4.5 %collective-permute-start.7 = (f32[11,64,128]{2,1,0:T(8,128)S(1)}, f32[11,64,128]{2,1,0:T(8,128)S(1)}, u32[]{:S(2)}, u32[]{:S(2)}) collective-permute-start(f32[11,64,128]{2,1,0:T(8,128)S(1)} %get-tuple-element.163), channel_id=1, source_target_pairs={{0,2},{1,3},{2,4},{3,5},{4,6},{5,7},{6,8},{7,9},{8,10},{9,11},{10,... | collective-permute-start | bytes 1081352 | tf_op jit(solution)/shard_map/cond/branch_1_fun/ppermute | solution.py:446
  8.9 1.3 %collective-permute-start.5 = (f32[32,8,128]{2,1,0:T(8,128)S(1)}, f32[32,8,128]{2,1,0:T(8,128)S(1)}, u32[]{:S(2)}, u32[]{:S(2)}) collective-permute-start(f32[32,8,128]{2,1,0:T(8,128)S(1)} %get-tuple-element.151), channel_id=1, source_target_pairs={{0,1},{1,0},{2,3},{3,2},{4,5},{5,4},{6,7},{7,6},{8,9},{9,8},{10,11... | collective-permute-start | bytes 393224 | tf_op jit(solution)/shard_map/cond/branch_1_fun/ppermute | solution.py:446
  10.2 1.9 %collective-permute-start.8 = (f32[12,8,128]{2,1,0:T(8,128)S(1)}, f32[12,8,128]{2,1,0:T(8,128)S(1)}, u32[]{:S(2)}, u32[]{:S(2)}) collective-permute-start(f32[12,8,128]{2,1,0:T(8,128)S(1)} %get-tuple-element.164), channel_id=1, source_target_pairs={{2,1},{3,0},{4,3},{5,2},{6,5},{7,4},{8,7},{9,6},{10,9},{11,8},{12,... | collective-permute-start | bytes 147464 | tf_op jit(solution)/shard_map/cond/branch_1_fun/ppermute | solution.py:446
  12.1 4.5 %collective-permute-start.9 = (f32[6,8,128]{2,1,0:T(8,128)S(1)}, f32[6,8,128]{2,1,0:T(8,128)S(1)}, u32[]{:S(2)}, u32[]{:S(2)}) collective-permute-start(f32[6,8,128]{2,1,0:T(8,128)S(1)} %get-tuple-element.165), channel_id=1, source_target_pairs={{0,3},{1,2},{2,5},{3,4},{4,7},{5,6},{6,9},{7,8},{8,11},{9,10},{10,... | collective-permute-start | bytes 73736 | tf_op jit(solution)/shard_map/cond/branch_1_fun/ppermute | solution.py:446
  16.6 0.0 collective-permute-done.5.refs_8_
  16.7 1.6 %prepare.5 = (f32[14,72,128]{2,1,0:T(8,128)S(1)}, f32[14,72,128]{2,1,0:T(8,128)S(1)}, f32[14,72,128]{2,1,0:T(8,128)S(1)}, f32[14,72,128]{2,1,0:T(8,128)S(1)}, f3...) custom-call(s32[3]{0:T(128)S(4)} %get-tuple-element.142.moved, ...), custom_call_target="tpu_custom_call" | custom-call | flops 10000000 | bytes 10000000 | tf_op jit(solution)/shard_map/cond/branch_1_fun/prepare/pallas_call | solution.py:334
  18.3 0.0 collective-permute-done.9.refs_13_
  18.3 0.0 collective-permute-done.8.refs_12_
  18.3 2.8 %collective-permute-done.7.refs_11_ = f32[11,64,128]{2,1,0:T(8,128)S(1)} collective-permute-done((f32[11,64,128]{2,1,0:T(8,128)S(1)}, f32[11,64,128]{2,1,0:T(8,128)S(1)}, u32[]{:S(2)}, u32[]{:S(2)}) %collective-permute-start.7) | collective-permute-done | bytes 360480 | tf_op jit(solution)/shard_map/cond/branch_1_fun/ppermute | solution.py:446
  21.1 0.0 collective-permute-done.6.refs_10_
  21.1 2.7 %steps.5 = (f32[8,64,128]{2,1,0:T(8,128)}, f32[8,64,128]{2,1,0:T(8,128)}, f32[8,64,128]{2,1,0:T(8,128)}, f32[8,64,128]{2,1,0:T(8,128)}, f32[8,64,128]{2,1,0:T(8,...) custom-call(s32[3]{0:T(128)S(4)} %get-tuple-element.142.moved, ...), custom_call_target="tpu_custom_call", output_to_operand_aliasing={{6}: (1, {}), {7}: (2, {}), {8}: (3, {}), {9}: (4, {}), {10... | custom-call | tf_op jit(solution)/shard_map/cond/branch_1_fun/steps/pallas_call | solution.py:423
Async XLA Ops:
  2.4 18.7 %collective-permute-start.6 = (f32[23,64,128]{2,1,0:T(8,128)S(1)}, f32[23,64,128]{2,1,0:T(8,128)S(1)}, u32[]{:S(2)}, u32[]{:S(2)}) collective-permute-start(f32[23,64,128]{2,1,0:T(8,128)S(1)} %get-tuple-element.162), channel_id=1, source_target_pairs={{2,0},{3,1},{4,2},{5,3},{6,4},{7,5},{8,6},{9,7},{10,8},{11,9},{12,... | collective-permute-start | bytes 2261000 | tf_op jit(solution)/shard_map/cond/branch_1_fun/ppermute | solution.py:446
  4.4 16.7 %collective-permute-start.7 = (f32[11,64,128]{2,1,0:T(8,128)S(1)}, f32[11,64,128]{2,1,0:T(8,128)S(1)}, u32[]{:S(2)}, u32[]{:S(2)}) collective-permute-start(f32[11,64,128]{2,1,0:T(8,128)S(1)} %get-tuple-element.163), channel_id=1, source_target_pairs={{0,2},{1,3},{2,4},{3,5},{4,6},{5,7},{6,8},{7,9},{8,10},{9,11},{10,... | collective-permute-start | bytes 1081352 | tf_op jit(solution)/shard_map/cond/branch_1_fun/ppermute | solution.py:446
  8.9 7.7 %collective-permute-start.5 = (f32[32,8,128]{2,1,0:T(8,128)S(1)}, f32[32,8,128]{2,1,0:T(8,128)S(1)}, u32[]{:S(2)}, u32[]{:S(2)}) collective-permute-start(f32[32,8,128]{2,1,0:T(8,128)S(1)} %get-tuple-element.151), channel_id=1, source_target_pairs={{0,1},{1,0},{2,3},{3,2},{4,5},{5,4},{6,7},{7,6},{8,9},{9,8},{10,11... | collective-permute-start | bytes 393224 | tf_op jit(solution)/shard_map/cond/branch_1_fun/ppermute | solution.py:446
  10.2 8.1 %collective-permute-start.8 = (f32[12,8,128]{2,1,0:T(8,128)S(1)}, f32[12,8,128]{2,1,0:T(8,128)S(1)}, u32[]{:S(2)}, u32[]{:S(2)}) collective-permute-start(f32[12,8,128]{2,1,0:T(8,128)S(1)} %get-tuple-element.164), channel_id=1, source_target_pairs={{2,1},{3,0},{4,3},{5,2},{6,5},{7,4},{8,7},{9,6},{10,9},{11,8},{12,... | collective-permute-start | bytes 147464 | tf_op jit(solution)/shard_map/cond/branch_1_fun/ppermute | solution.py:446
  12.1 6.2 %collective-permute-start.9 = (f32[6,8,128]{2,1,0:T(8,128)S(1)}, f32[6,8,128]{2,1,0:T(8,128)S(1)}, u32[]{:S(2)}, u32[]{:S(2)}) collective-permute-start(f32[6,8,128]{2,1,0:T(8,128)S(1)} %get-tuple-element.165), channel_id=1, source_target_pairs={{0,3},{1,2},{2,5},{3,4},{4,7},{5,6},{6,9},{7,8},{8,11},{9,10},{10,... | collective-permute-start | bytes 73736 | tf_op jit(solution)/shard_map/cond/branch_1_fun/ppermute | solution.py:446

commit v5 on v4

v5 whole, which is shorter than its diff:
```python
import functools

import jax
import jax.numpy as jnp
from jax import lax
from jax.experimental import pallas as pl
from jax.experimental.pallas import tpu as pltpu
from jax.sharding import PartitionSpec as P

STEPS = 3
TILE = 8
HALF = 4
GROUP = 4
TIME_STEP = 0.5
CURRENT_SCALE = 0.1
VMEM = pl.BlockSpec(memory_space=pltpu.VMEM)
SMEM = pl.BlockSpec(memory_space=pltpu.SMEM)
ANY = pl.BlockSpec(memory_space=pl.ANY)
EX, EY, ES, BX, BY, BS, CODES, BUNCH = range(8)
CASES = ((1, 1), (1, 0), (2, 1), (2, 0))


def down_counts(case):
    moves, now = case
    later = moves - now
    return (moves + 1,) * 6 + (later + 1, later + 1)


def up_counts(case):
    moves, now = case
    below = 3 - moves
    later = moves - now
    return (below - 1, below - 1, below, below, below, below - 1, 2 - later, 2 - later)


def offsets(counts):
    starts = [0]
    for count in counts:
        starts.append(starts[-1] + count)
    return starts


def tile_planes(count, width):
    return -(-count // (width // TILE))


def tile_of(ref, start, n, width):
    per_plane = width // TILE
    return start + n // per_plane, pl.ds(n % per_plane * TILE, TILE)


def column_scales(place, total):
    place = place.astype(jnp.float32)
    whole = 1.0 + (place - total / 2) / (2 * total)
    half = 1.0 + (place + 0.5 - total / 2) / (2 * total)
    return whole, half


def turned(tiles):
    return pltpu.roll(tiles, HALF, tiles.ndim - 2)


def next_y(v):
    depth = v.shape[-1]
    lane = lax.broadcasted_iota(jnp.int32, v.shape[-2:], 1)
    return jnp.where(lane < depth - 1, pltpu.roll(v, depth - 1, v.ndim - 1), 0.0)


def last_y(v):
    lane = lax.broadcasted_iota(jnp.int32, v.shape[-2:], 1)
    return jnp.where(lane > 0, pltpu.roll(v, 1, v.ndim - 1), 0.0)


def next_x(v):
    return pltpu.roll(v, v.shape[-2] - 1, v.ndim - 2)


def last_x(v):
    return pltpu.roll(v, 1, v.ndim - 2)


def low_half(depth):
    return lax.broadcasted_iota(jnp.int32, (TILE, depth), 0) < HALF


def pack_kernel(*refs):
    sources, moved = refs[:8], refs[8]
    which, moved_here = refs[9:11]
    sent = refs[11 : 11 + len(CASES)]
    near, near_int, sems, moved_sem = refs[11 + len(CASES) :]
    _, count, width, depth = near.shape
    gx = lax.axis_index("gx")
    total = width * lax.axis_size("gx")

    get_moved = pltpu.make_async_copy(moved, moved_here, moved_sem)
    get_moved.start()
    copies = []
    for a in range(8):
        goal = near.at[a] if a < 6 else near_int.at[a - 6]
        copies.append(pltpu.make_async_copy(sources[a].at[pl.ds(0, count)], goal, sems.at[a]))
        copies[-1].start()
    get_moved.wait()
    now = moved_here[0]
    later = moved_here[1] + moved_here[2]
    case_index = jnp.where(now + later == 1, 1 - now, 3 - now)
    which[0] = case_index

    row = lax.broadcasted_iota(jnp.int32, (width, depth), 0)
    whole, half = column_scales(gx * width + row, total)
    one_whole, one_half = 1.0 / whole, 1.0 / half
    step_whole, step_half = TIME_STEP * one_whole, TIME_STEP * one_half
    low = low_half(depth)
    for item in copies:
        item.wait()

    for c, case in enumerate(CASES):
        down = sent[c]
        downs = down_counts(case)
        at = offsets(downs[:6])
        moves = case[0]
        far = moves + 1
        cell = 1 + moves - case[1]

        @pl.when(case_index == c)
        def _():
            field = lambda a, plane: near[a, plane]
            for a in range(6):
                down[pl.ds(at[a], far)] = near[a, :far]
            folded = {}
            for plane in (far - 1, far):
                folded[BX, plane] = field(BX, plane) + step_whole * field(EY, plane + 1)
                folded[BY, plane] = field(BY, plane) - step_half * field(EX, plane + 1)
            down[at[BX] + far - 1] = folded[BX, far - 1]
            down[at[BY] + far - 1] = folded[BY, far - 1]

            def magnetic(plane):
                ex, ey, es = field(EX, plane), field(EY, plane), field(ES, plane)
                weighted = whole * es
                bx = folded[BX, plane] - TIME_STEP * (next_y(es) - es) - step_whole * ey
                by = folded[BY, plane] + step_half * (ex + next_x(weighted) - weighted)
                return bx, by

            bx_below, by_below = magnetic(far - 1)
            bx, by = magnetic(far)
            ex, ey = field(EX, far), field(EY, far)
            bs = field(BS, far) - TIME_STEP * ((next_x(ey) - ey) - (next_y(ex) - ex))
            code = near_int[0, cell]
            kept, gained = coefficients(code)
            weighted = half * bs
            place = at[-1]
            down[place] = kept * ex + gained * ((bs - last_y(bs)) - one_half * (by - by_below))
            down[place + 1] = kept * ey + gained * (
                one_whole * ((bx - bx_below) - (weighted - last_x(weighted)))
            )
            place += 2
            for n, a in enumerate((CODES, BUNCH)):
                down[pl.ds(place, cell)] = near_int[n, :cell].astype(jnp.float32)
                place += cell
            edges = [ex, ey, field(ES, far), folded[BX, far], folded[BY, far], field(BS, far)]
            edges.append(code.astype(jnp.float32))
            for n, v in enumerate(edges):
                tile = jnp.where(low, turned(v[width - TILE :]), turned(v[:TILE]))
                plane, rows = tile_of(down, place, n, width)
                down[plane, rows] = tile


def pack(arrays, moved):
    planes, width, depth = arrays[0].shape
    near = max(case[0] for case in CASES) + 3
    shapes = [pltpu.SMEM((1,), jnp.int32), pltpu.SMEM((STEPS,), jnp.int32)]
    for case in CASES:
        count = sum(down_counts(case)) + 2 + tile_planes(7, width)
        shapes.append(pltpu.VMEM((count, width, depth), jnp.float32))
    found = pl.pallas_call(
        pack_kernel,
        out_shape=shapes,
        in_specs=[ANY] * 9,
        out_specs=[SMEM] * 2 + [VMEM] * len(CASES),
        scratch_shapes=[
            pltpu.VMEM((6, near, width, depth), jnp.float32),
            pltpu.VMEM((2, near, width, depth), jnp.int32),
            pltpu.SemaphoreType.DMA((8,)),
            pltpu.SemaphoreType.DMA,
        ],
        compiler_params=pltpu.CompilerParams(vmem_limit_bytes=32 * 2**20),
        name="pack",
    )(*(pltpu.with_memory_space_constraint(a, pltpu.HBM) for a in (*arrays, moved)))
    return found[0], found[1], found[2:]


def edges_kernel(sides, *refs):
    own, across = refs[:8], refs[8:]
    planes, width, depth = own[0].shape
    gx = lax.axis_index("gx")
    low = low_half(depth)
    for n, side in enumerate(sides):
        if side == "swap":
            at, high = pl.multiple_of(jnp.where(gx == 0, width - TILE, 0), TILE), gx == 0
        else:
            at, high = (width - TILE, True) if side == "right" else (0, False)
        for a in range(4):
            first = own[a][:, pl.ds(at, TILE)]
            second = own[a + 4][:, pl.ds(at, TILE)].astype(jnp.float32)
            if side == "swap":
                first = jnp.where(high, turned(first), first)
                second = jnp.where(high, second, turned(second))
            elif high:
                first = turned(first)
            else:
                second = turned(second)
            across[n][pl.ds(a * planes, planes)] = jnp.where(low, first, second)


def edges(sides, own):
    planes, width, depth = own[0].shape
    return pl.pallas_call(
        functools.partial(edges_kernel, sides),
        out_shape=[pltpu.VMEM((4 * planes, TILE, depth), jnp.float32)] * len(sides),
        in_specs=[VMEM] * 8,
        out_specs=[VMEM] * len(sides),
        compiler_params=pltpu.CompilerParams(vmem_limit_bytes=32 * 2**20),
        name="edges",
    )(*own)


def relay_kernel(case, n_sides, *refs):
    own, beside = refs[:8], refs[8 : 8 + n_sides]
    up, corners = refs[8 + n_sides :]
    planes, width, depth = own[0].shape
    moves = case[0]
    gx = lax.axis_index("gx")
    start = gx * width
    total = width * lax.axis_size("gx")
    low = low_half(depth)
    row = lax.broadcasted_iota(jnp.int32, (TILE, depth), 0)
    ups = up_counts(case)
    up_at = offsets(ups)

    column = lax.broadcasted_iota(jnp.int32, (width, depth), 0)
    whole, half = column_scales(start + column, total)
    bottom = planes - (3 - moves)
    for a in range(8):
        if ups[a]:
            up[pl.ds(up_at[a], ups[a])] = own[a][planes - ups[a] :].astype(jnp.float32)
    up[up_at[BX]] = own[BX][bottom] - (TIME_STEP / whole) * own[EY][bottom]
    up[up_at[BY]] = own[BY][bottom] + (TIME_STEP / half) * own[EX][bottom]

    for n in range(n_sides):
        if n_sides == 1:
            left_column = jnp.where(gx == 0, start + width, start - HALF)
        else:
            left_column = start - HALF if n == 0 else start + width
        whole, half = column_scales(left_column + jnp.where(row < HALF, row, row - HALF), total)
        step_whole, step_half = TIME_STEP / whole, TIME_STEP / half
        tile = lambda a, plane: beside[n][a * planes + plane]

        def folded(a, plane, source, sign):
            if a == BX:
                return tile(a, plane) + jnp.where(low, sign * step_whole * tile(EY, source), 0.0)
            if a == BY - 4:
                return tile(a, plane) - jnp.where(low, 0.0, turned(sign * step_half * tile(EX, source)))
            return tile(a, plane)

        count = moves + 2
        for a in range(4):
            to = (n * 4 + a) * count
            corners[pl.ds(to, count)] = beside[n][pl.ds(a * planes, count)]
            if a in (BX, BY - 4):
                for plane in (moves, moves + 1):
                    corners[to + plane] = folded(a, plane, plane + 1, 1.0)
            for i in range(3 - moves):
                plane, rows = tile_of(up, up_at[-1], (n * 4 + a) * (3 - moves) + i, width)
                value = folded(a, bottom, bottom, -1.0) if i == 0 else tile(a, bottom + i)
                up[plane, rows] = value


def relay(case, own, beside):
    planes, width, depth = own[0].shape
    moves = case[0]
    tiles = len(beside) * 4
    n_up = sum(up_counts(case)) + tile_planes(tiles * (3 - moves), width)
    return pl.pallas_call(
        functools.partial(relay_kernel, case, len(beside)),
        out_shape=[
            pltpu.VMEM((n_up, width, depth), jnp.float32),
            pltpu.VMEM((tiles * (moves + 2), TILE, depth), jnp.float32),
        ],
        in_specs=[VMEM] * (8 + len(beside)),
        out_specs=[VMEM] * 2,
        compiler_params=pltpu.CompilerParams(vmem_limit_bytes=32 * 2**20),
        name="relay",
    )(*own, *beside)


def coefficients(code):
    kind = code.dtype.type
    five, six, seven = code == kind(5), code == kind(6), code == kind(7)
    keep = jnp.where(five, 0.0, jnp.where(six, 0.8 / 1.2, jnp.where(seven, 0.4 / 1.6, 1.0)))
    gain = jnp.where(
        five,
        0.0,
        jnp.where(six, TIME_STEP / 1.2, jnp.where(seven, TIME_STEP / 1.6, TIME_STEP)),
    )
    return keep, gain


def ghost_inside(width, depth):
    gx = lax.axis_index("gx")
    row = lax.broadcasted_iota(jnp.int32, (1, TILE, depth), 1)
    right = gx < lax.axis_size("gx") - 1
    return jnp.where(row < HALF, right.astype(jnp.int32), (gx > 0).astype(jnp.int32)) == 1


def spread_tiles(beside, upper):
    gx = lax.axis_index("gx")
    if len(beside) == 1:
        same = (gx > 0) if upper else (gx == 0)
        return jnp.where(same, beside[0], turned(beside[0]))
    from_left, from_right = beside
    if upper:
        from_right = turned(from_right)
    else:
        from_left = turned(from_left)
    return jnp.where(low_half(from_left.shape[-1]), from_right, from_left)


class Cells:
    def __init__(self, refs, width):
        self.ext, (self.keep, self.gain, self.current, self.rows) = refs[:6], refs[6:]
        self.width = width
        self.tall, self.depth = self.keep.shape[1:]
        self.ghost_in = ghost_inside(width, self.depth)

    def put(self, a, at, count, value, ghost):
        here = pl.ds(at, count)
        where = pl.ds(self.width, TILE) if ghost else pl.ds(0, self.width)
        mask = (lambda v: jnp.where(self.ghost_in, v, 0.0)) if ghost else (lambda v: v)
        if a < 6:
            self.ext[a][here, where] = mask(value)
        elif a == CODES:
            kept, gained = coefficients(value)
            self.keep[here, where], self.gain[here, where] = mask(kept), mask(gained)
        else:
            self.current[here, where] = CURRENT_SCALE * mask(value.astype(jnp.float32))

    def magnetic(self, e, count):
        ext, rows = self.ext, self.rows
        here, above = pl.ds(e, count), pl.ds(e + 1, count)
        ex, ey, es = ext[EX][here], ext[EY][here], ext[ES][here]
        bx = ext[BX][here] - (rows[4] * (next_y(es) - es) - rows[5] * (ext[EY][above] - ey))
        by = ext[BY][here] - rows[6] * ((ext[EX][above] - ex) - (next_x(rows[0] * es) - rows[0] * es))
        bs = ext[BS][here] - rows[4] * ((next_x(ey) - ey) - (next_y(ex) - ex))
        ext[BX][here], ext[BY][here], ext[BS][here] = bx, by, bs

    def electric(self, e, count, moved_now):
        ext, rows = self.ext, self.rows
        here, below, cells = pl.ds(e, count), pl.ds(e - 1, count), pl.ds(e - moved_now, count)
        bx, by, bs = ext[BX][here], ext[BY][here], ext[BS][here]
        kept, gained = self.keep[cells], self.gain[cells]
        ex = kept * ext[EX][here] + gained * ((bs - last_y(bs)) - rows[3] * (by - ext[BY][below]))
        ey = kept * ext[EY][here] + gained * (
            rows[2] * ((bx - ext[BX][below]) - (rows[1] * bs - last_x(rows[1] * bs)))
        )
        es = kept * ext[ES][here] + gained * (
            (by - last_x(by)) - (bx - last_y(bx)) - self.current[cells]
        )
        ext[EX][here], ext[EY][here], ext[ES][here] = ex, ey, es

    def leave(self, plane):
        for a in (BX, BY):
            self.ext[a][plane] = jnp.zeros((self.tall, self.depth), jnp.float32)


def in_groups(start, count, body):
    whole = max(count, 0) // GROUP
    if whole:

        @pl.loop(0, whole)
        def _(i):
            body(start + i * GROUP, GROUP)

    if count > 0 and count % GROUP:
        body(start + whole * GROUP, count % GROUP)


def prepare_kernel(moves, n_sides, moved, *refs):
    own, beside = refs[:8], refs[8 : 8 + n_sides]
    planes, width, depth = own[0].shape
    cells = Cells(refs[8 + n_sides :], width)
    tall, rows = cells.tall, cells.rows
    base = 3 - moves
    top = base + planes - 1
    total = width * lax.axis_size("gx")

    row = lax.broadcasted_iota(jnp.int32, (tall, depth), 0)
    place = lax.axis_index("gx") * width + jnp.where(row < width + HALF, row, row - tall)
    inside = (place >= 0) & (place < total)
    whole, half = column_scales(place, total)
    step = jnp.where(inside, TIME_STEP, 0.0)
    for n, value in enumerate((whole, half, 1.0 / whole, 1.0 / half, step, step / whole, step / half)):
        rows[n] = value
    for a in range(8):
        cells.put(a, base, planes, own[a][...], False)
        tiles = [side[pl.ds(a % 4 * planes, planes)] for side in beside]
        cells.put(a, base, planes, spread_tiles(tiles, a >= 4), True)
    for a in (EX, EY):
        cells.ext[a][0] = jnp.zeros((tall, depth), jnp.float32)
        cells.ext[a][planes + 4] = jnp.zeros((tall, depth), jnp.float32)

    moved_now = 0
    for t in range(STEPS):
        moved_now = moved_now + moved[t]
        in_groups(base + t, planes - 1 - 2 * t, cells.magnetic)

        @pl.when((lax.axis_index("gz") == 0) & (moved_now == t + 1))
        def _():
            cells.leave(base + t)

        in_groups(base + t + 1, planes - 2 - 2 * t, lambda e, n: cells.electric(e, n, moved_now))


def prepare(moves, moved, own, beside):
    planes, width, depth = own[0].shape
    tall = width + TILE
    vmem = lambda *shape: pltpu.VMEM(shape, jnp.float32)
    shapes = [vmem(planes + 5, tall, depth)] * 9
    shapes += [vmem(7, tall, depth)]
    return pl.pallas_call(
        functools.partial(prepare_kernel, moves, len(beside)),
        out_shape=shapes,
        in_specs=[SMEM] + [VMEM] * (8 + len(beside)),
        out_specs=[VMEM] * len(shapes),
        compiler_params=pltpu.CompilerParams(vmem_limit_bytes=32 * 2**20),
        cost_estimate=pl.CostEstimate(flops=10**7, bytes_accessed=10**7, transcendentals=0),
        name="prepare",
    )(moved, *own, *beside)


def steps_kernel(case, n_sides, planes, width, moved, *refs):
    rows, down, up, corners = refs[9:13]
    outs = refs[13:19]
    cells = Cells((*refs[19:28], rows), width)
    sems = refs[28]
    ext = cells.ext
    moves = case[0]
    base = 3 - moves
    top = base + planes - 1
    far = planes + 4
    first = lax.axis_index("gz") == 0
    last = lax.axis_index("gz") == lax.axis_size("gz") - 1
    downs, ups = down_counts(case), up_counts(case)
    at, up_at = offsets(downs[:6]), offsets(ups)
    far_at = at[-1]
    at = at[:6] + [far_at + 2, far_at + 2 + downs[CODES]]
    tiles_at = at[BUNCH] + downs[BUNCH]
    copies = []

    def send(a, start, end):
        if end > start:
            item = pltpu.make_async_copy(
                ext[a].at[pl.ds(start, end - start), pl.ds(0, width)],
                outs[a].at[pl.ds(start - 3, end - start)],
                sems.at[len(copies)],
            )
            item.start()
            copies.append(item)

    for a in range(6):
        send(a, base + (2 if a >= BX else 3), top - 2)

    def corner(a, plane, count):
        first_tile = [(n * 4 + a % 4) * (moves + 2) + plane for n in range(n_sides)]
        return spread_tiles([corners[pl.ds(t, count)] for t in first_tile], a >= 4)

    for a in range(8):
        cells.put(a, top + 1, downs[a], down[pl.ds(at[a], downs[a])], False)
        cells.put(a, top + 1, downs[a], corner(a, 0, downs[a]), True)
        if ups[a]:
            cells.put(a, base - ups[a], ups[a], up[pl.ds(up_at[a], ups[a])], False)
            for i in range(base - ups[a], base):
                tiles = []
                for n in range(n_sides):
                    plane, here = tile_of(up, up_at[-1], (n * 4 + a % 4) * base + i, width)
                    tiles.append(up[plane, here])
                cells.put(a, i, 1, spread_tiles(tiles, a >= 4)[None], True)

    low = low_half(cells.depth)
    left, right, ghost = pl.ds(0, TILE), pl.ds(width - TILE, TILE), pl.ds(width, TILE)

    def blocks(right_tile, ghost_tile, left_tile):
        return jnp.where(low, right_tile, ghost_tile), jnp.where(low, ghost_tile, left_tile)

    def far_plane():
        def kept_blocks(ref, *plane):
            return blocks(*(turned(ref[(*plane, where)]) for where in (right, ghost, left)))

        def sent_blocks(a, ghost_tile):
            plane, here = tile_of(down, tiles_at, min(a, 6), width)
            tile = down[plane, here]
            return tile, jnp.where(cells.ghost_in[0], ghost_tile, 0.0)

        raw = []
        for a in range(6):
            tile, beyond = sent_blocks(a, corner(a, moves + 1, 1)[0])
            raw.append(blocks(tile, turned(beyond), tile))
        tile, beyond = sent_blocks(CODES, corner(CODES, downs[CODES], 1)[0])
        factors = [
            blocks(mine, turned(jnp.where(cells.ghost_in[0], theirs, 0.0)), mine)
            for mine, theirs in zip(coefficients(tile), coefficients(beyond))
        ]
        const = [kept_blocks(rows, n) for n in range(7)]
        below = [kept_blocks(ext[a], far - 1) for a in (BX, BY)]
        found = []
        for b in range(2):
            ex, ey, es, bx, by, bs = (v[b] for v in raw)
            kept, gained = (v[b] for v in factors)
            row = [v[b] for v in const]
            weighted = row[0] * es
            bx = bx - row[4] * (next_y(es) - es) - row[5] * ey
            by = by + row[6] * (ex + next_x(weighted) - weighted)
            bs = bs - row[4] * ((next_x(ey) - ey) - (next_y(ex) - ex))
            weighted = row[1] * bs
            ex = kept * ex + gained * ((bs - last_y(bs)) - row[3] * (by - below[1][b]))
            ey = kept * ey + gained * (
                row[2] * ((bx - below[0][b]) - (weighted - last_x(weighted)))
            )
            found.append((ex, ey))
        n_row = lax.broadcasted_iota(jnp.int32, (TILE, cells.depth), 0)
        for a in (EX, EY):
            right_block, left_block = found[0][a], found[1][a]
            ext[a][far, pl.ds(0, width)] = down[far_at + a]
            ext[a][far, right] = jnp.where(
                n_row == TILE - 1, turned(right_block), down[far_at + a, right]
            )
            ext[a][far, left] = jnp.where(n_row == 0, turned(left_block), down[far_at + a, left])
            ext[a][far, ghost] = turned(jnp.where(low, left_block, right_block))

    moved_now = 0
    for t in range(STEPS):
        moved_now = moved_now + moved[t]
        above = moves + (2 if t == 0 else 3)
        cells.magnetic(t, base)
        cells.magnetic(top - t, above)

        @pl.when(first)
        def _():
            cells.leave(base + moved_now - 1)

        if t == STEPS - 1:
            for a in (BX, BY, BS):
                send(a, 3, base + 2)
                send(a, top - 2, planes + 3)
        cells.electric(t + 1, base, moved_now)
        if t == STEPS - 1:
            for a in (EX, EY, ES):
                send(a, 3, base + 3)
        cells.electric(top - t, above, moved_now)
        if t == 0:
            far_plane()
        if t == STEPS - 1:
            for a in (EX, EY, ES):
                send(a, top - 2, planes + 3)
        else:

            @pl.when(last)
            def _():
                for a in (EX, EY, ES):
                    ext[a][top + 1 + moved_now] = jnp.zeros((cells.tall, cells.depth), jnp.float32)

    for item in copies:
        item.wait()


def advance(case, n_sides, moved, shape, ready, ghosts):
    planes, width, depth = shape
    block = jax.ShapeDtypeStruct(shape, jnp.float32)
    n_in = 11 + len(ghosts)
    found = pl.pallas_call(
        functools.partial(steps_kernel, case, n_sides, planes, width),
        out_shape=[block] * 6 + [pltpu.VMEM(x.shape, x.dtype) for x in ready[:9]],
        in_specs=[SMEM] + [VMEM] * (n_in - 1),
        out_specs=[ANY] * 6 + [VMEM] * 9,
        input_output_aliases={1 + n: 6 + n for n in range(9)},
        scratch_shapes=[pltpu.SemaphoreType.DMA((18,))],
        compiler_params=pltpu.CompilerParams(vmem_limit_bytes=32 * 2**20),
        name="steps",
    )(moved, *ready, *ghosts)
    return tuple(found[:6])


def passed(block, dz, side):
    size_z, size_x = lax.axis_size("gz"), lax.axis_size("gx")
    steps_x = {"swap": (1, -1), "right": (1,), "left": (-1,), None: (0,)}[side]
    route = [
        (z * size_x + x, (z + dz) * size_x + x + dx)
        for z in range(size_z)
        for x in range(size_x)
        for dx in steps_x
        if 0 <= z + dz < size_z and 0 <= x + dx < size_x
    ]
    return lax.ppermute(block, ("gz", "gx"), route)


def on_device(*args):
    arrays, moved = args[:8], args[8]
    arrays = arrays[:6] + (arrays[7], arrays[6])
    sides = ("swap",) if lax.axis_size("gx") == 2 else ("right", "left")
    which, moved, sent = pack(arrays, moved)

    def run(c, own, sent, moved):
        case = CASES[c]
        down = passed(sent[c], -1, None)
        across = edges(sides, own)
        beside = [passed(block, 0, side) for block, side in zip(across, sides)]
        up, corners = relay(case, own, beside)
        up, corners = passed(up, 1, None), passed(corners, -1, None)
        ready = prepare(case[0], moved, own, beside)
        return advance(case, len(sides), moved, own[0].shape, ready, [down, up, corners])

    return lax.switch(
        which[0],
        [functools.partial(run, c) for c in range(len(CASES))],
        arrays,
        sent,
        moved,
    )


def solution(mesh):
    block = P("gz", "gx", None)
    return jax.shard_map(
        on_device,
        mesh=mesh,
        in_specs=(block,) * 8 + (P(),),
        out_specs=(block,) * 6,
        check_vma=False,
    )
```

time: 24.4 us -> 24.2 us (level)
  starting transfers between devices: 14.2 us -> 11 us
  waiting for transfers between devices: 2.83 us -> 5.39 us
    ppermute x5 -> x4, starting transfers between devices: 14.2 us -> 11 us  [passed(): return lax.ppermute(block, ('gz', 'gx'), route)]
    ppermute x5 -> x4, waiting for transfers between devices: 2.83 us -> 5.39 us  [passed(): return lax.ppermute(block, ('gz', 'gx'), route)]
    pallas_call x2 -> x4, Pallas kernels: 4.42 us -> 4.44 us  [the longest x1 2.6 us: advance(): pl.pallas_call(functools.partial(steps_kernel, case, n_sides, planes, wid...]
  transfers between devices with their start and end apart: 5 -> 4, of which waited for: 1 -> 2; matrix products, arithmetic and copies ran while one was open for 0% -> 0% of each run, Pallas kernels for 7% -> 7%
where the time goes in v5:
time: 24.2 us; the launch traced here: 23.8 us
  starting transfers between devices  11 us (45%)
  Pallas kernels  6.03 us (25%)
  waiting for transfers between devices  5.39 us (22%)
  between operations  0.94 us (4%)
  loops' own time  0.28 us (1%)
    ppermute x4, starting transfers between devices, passed(): return lax.ppermute(block, ('gz', 'gx'), route)  11 us
    ppermute x4, waiting for transfers between devices, passed(): return lax.ppermute(block, ('gz', 'gx'), route)  5.39 us
    pallas_call x1, Pallas kernels, advance(): pl.pallas_call(functools.partial(steps_kernel, case, n_sides, planes, wid...  2.6 us
    pallas_call x1, Pallas kernels, pack(): pl.pallas_call(pack_kernel, out_shape=shapes, in_specs=[ANY] * 9, out_spe...  1.75 us
    pallas_call x1, Pallas kernels, prepare(): pl.pallas_call(functools.partial(prepare_kernel, moves, len(beside)), out...  1.59 us
  transfers between devices with their start and end apart: 4, of which 2 were waited for; matrix products, arithmetic and copies ran while one was open for 0% of the time, Pallas kernels for 7%

profile of v5, /device:TPU:1, one launch (start us, length us, event | category | flops | bytes accessed | tf_op | source)
XLA Modules:
  0.0 23.8 jit_solution(1847084125327414504)
XLA Ops:
  0.6 0.0 copy-start.6
  0.6 0.0 copy-start.7
  0.7 0.0 copy-start.5
  0.7 0.0 copy-start.4
  0.7 0.0 copy-start.3
  0.7 0.0 copy-start.2
  0.7 0.0 copy-start.1
  0.7 0.0 copy-start
  0.7 1.7 %pack.1 = (s32[1]{0:T(128)S(4)}, s32[3]{0:T(128)S(4)}, f32[17,64,128]{2,1,0:T(8,128)S(1)}, f32[19,64,128]{2,1,0:T(8,128)S(1)}, f32[25,64,128]{2,1,0:T(8,128)S(1)}, /*index=5*/f32[27,64,128]{2,1,0:T(8,128)S(1)}) custom-call(f32[8,64,128]{2,1,0:T(8,128)} %refs_0_.1, f32[8,64,128]{2,1,0:T(8,128)} %refs_1_.1, f32[8,64,128]{2,1,0:T(8,128)} %refs_2_.1, ...), custom_call_target="tpu_custom_call" | custom-call | tf_op jit(solution)/shard_map/pack/pallas_call | solution.py:174
  2.5 0.0 copy-done.6
  2.5 0.0 copy-done.7
  2.5 0.0 copy-done.1
  2.6 0.1 copy-done
  2.7 21.0 %conditional.1 = (f32[8,64,128]{2,1,0:T(8,128)}, f32[8,64,128]{2,1,0:T(8,128)}, f32[8,64,128]{2,1,0:T(8,128)}, f32[8,64,128]{2,1,0:T(8,128)}, f32[8,64,128]{2,1,0:T(8,128)}, /*index=5*/f32[8,64,128]{2,1,0:T(8,128)}) conditional(s32[]{:T(128)} %bitcast, (f32[8,64,128]{2,1,0:T(8,128)S(1)}, f32[8,64,128]{2,1,0:T(8,128)S(1)}, ...), branch_computations={%region_0.0_spmd, %region_1.0_spmd, %region_2.0_spmd, %region_3.0_... | conditional | flops 10000000 | bytes 14849872 | solution.py:620
  2.7 2.0 %collective-permute-start.9 = (f32[25,64,128]{2,1,0:T(8,128)S(1)}, f32[25,64,128]{2,1,0:T(8,128)S(1)}, u32[]{:S(2)}, u32[]{:S(2)}) collective-permute-start(f32[25,64,128]{2,1,0:T(8,128)S(1)} %get-tuple-element.155), channel_id=1, source_target_pairs={{2,0},{3,1},{4,2},{5,3},{6,4},{7,5},{8,6},{9,7},{10,8},{11,9},{12,... | collective-permute-start | bytes 2457608 | tf_op jit(solution)/shard_map/cond/branch_2_fun/ppermute | solution.py:601
  4.7 2.7 %collective-permute-start.8 = (f32[32,8,128]{2,1,0:T(8,128)S(1)}, f32[32,8,128]{2,1,0:T(8,128)S(1)}, u32[]{:S(2)}, u32[]{:S(2)}) collective-permute-start(f32[32,8,128]{2,1,0:T(8,128)S(1)} %edges.6), channel_id=1, source_target_pairs={{0,1},{1,0},{2,3},{3,2},{4,5},{5,4},{6,7},{7,6},{8,9},{9,8},{10,11... | collective-permute-start | bytes 393224 | tf_op jit(solution)/shard_map/cond/branch_2_fun/ppermute | solution.py:601
  7.4 3.3 %collective-permute-done.8.refs_8_ = f32[32,8,128]{2,1,0:T(8,128)S(1)} collective-permute-done((f32[32,8,128]{2,1,0:T(8,128)S(1)}, f32[32,8,128]{2,1,0:T(8,128)S(1)}, u32[]{:S(2)}, u32[]{:S(2)}) %collective-permute-start.8) | collective-permute-done | bytes 131104 | tf_op jit(solution)/shard_map/cond/branch_2_fun/ppermute | solution.py:601
  10.8 4.4 %collective-permute-start.10 = (f32[6,64,128]{2,1,0:T(8,128)S(1)}, f32[6,64,128]{2,1,0:T(8,128)S(1)}, u32[]{:S(2)}, u32[]{:S(2)}) collective-permute-start(f32[6,64,128]{2,1,0:T(8,128)S(1)} %get-tuple-element.156), channel_id=1, source_target_pairs={{0,2},{1,3},{2,4},{3,5},{4,6},{5,7},{6,8},{7,9},{8,10},{9,11},{10,... | collective-permute-start | bytes 589832 | tf_op jit(solution)/shard_map/cond/branch_2_fun/ppermute | solution.py:601
  15.2 1.9 %collective-permute-start.11 = (f32[16,8,128]{2,1,0:T(8,128)S(1)}, f32[16,8,128]{2,1,0:T(8,128)S(1)}, u32[]{:S(2)}, u32[]{:S(2)}) collective-permute-start(f32[16,8,128]{2,1,0:T(8,128)S(1)} %get-tuple-element.157), channel_id=1, source_target_pairs={{2,0},{3,1},{4,2},{5,3},{6,4},{7,5},{8,6},{9,7},{10,8},{11,9},{12,... | collective-permute-start | bytes 196616 | tf_op jit(solution)/shard_map/cond/branch_2_fun/ppermute | solution.py:601
  17.1 1.6 %prepare.6 = (f32[13,72,128]{2,1,0:T(8,128)S(1)}, f32[13,72,128]{2,1,0:T(8,128)S(1)}, f32[13,72,128]{2,1,0:T(8,128)S(1)}, f32[13,72,128]{2,1,0:T(8,128)S(1)}, f3...) custom-call(s32[3]{0:T(128)S(4)} %get-tuple-element.136.moved, ...), custom_call_target="tpu_custom_call" | custom-call | flops 10000000 | bytes 10000000 | tf_op jit(solution)/shard_map/cond/branch_2_fun/prepare/pallas_call | solution.py:428
  18.7 2.1 %collective-permute-done.11.refs_12_ = f32[16,8,128]{2,1,0:T(8,128)S(1)} collective-permute-done((f32[16,8,128]{2,1,0:T(8,128)S(1)}, f32[16,8,128]{2,1,0:T(8,128)S(1)}, u32[]{:S(2)}, u32[]{:S(2)}) %collective-permute-start.11) | collective-permute-done | bytes 65568 | tf_op jit(solution)/shard_map/cond/branch_2_fun/ppermute | solution.py:601
  20.8 0.0 collective-permute-done.10.refs_11_
  20.8 0.0 collective-permute-done.9.refs_10_
  20.8 2.6 %steps.6 = (f32[8,64,128]{2,1,0:T(8,128)}, f32[8,64,128]{2,1,0:T(8,128)}, f32[8,64,128]{2,1,0:T(8,128)}, f32[8,64,128]{2,1,0:T(8,128)}, f32[8,64,128]{2,1,0:T(8,...) custom-call(s32[3]{0:T(128)S(4)} %get-tuple-element.136.moved, ...), custom_call_target="tpu_custom_call", output_to_operand_aliasing={{6}: (1, {}), {7}: (2, {}), {8}: (3, {}), {9}: (4, {}), {10... | custom-call | tf_op jit(solution)/shard_map/cond/branch_2_fun/steps/pallas_call | solution.py:578
  (6 shorter events, 0.1 us)
Async XLA Ops:
  0.6 1.8 %copy-start.6 = (s32[8,64,128]{2,1,0:T(8,128)S(1)}, s32[8,64,128]{2,1,0:T(8,128)}, u32[]{:S(2)}) copy-start(s32[8,64,128]{2,1,0:T(8,128)} %refs_6_.1) | copy-start | bytes 786436
  0.6 1.8 %copy-start.7 = (s32[8,64,128]{2,1,0:T(8,128)S(1)}, s32[8,64,128]{2,1,0:T(8,128)}, u32[]{:S(2)}) copy-start(s32[8,64,128]{2,1,0:T(8,128)} %refs_7_.1) | copy-start | bytes 786436
  0.7 1.8 %copy-start.5 = (f32[8,64,128]{2,1,0:T(8,128)S(1)}, f32[8,64,128]{2,1,0:T(8,128)}, u32[]{:S(2)}) copy-start(f32[8,64,128]{2,1,0:T(8,128)} %refs_5_.1) | copy-start | bytes 786436
  0.7 1.8 %copy-start.4 = (f32[8,64,128]{2,1,0:T(8,128)S(1)}, f32[8,64,128]{2,1,0:T(8,128)}, u32[]{:S(2)}) copy-start(f32[8,64,128]{2,1,0:T(8,128)} %refs_4_.1) | copy-start | bytes 786436
  0.7 1.8 %copy-start.3 = (f32[8,64,128]{2,1,0:T(8,128)S(1)}, f32[8,64,128]{2,1,0:T(8,128)}, u32[]{:S(2)}) copy-start(f32[8,64,128]{2,1,0:T(8,128)} %refs_3_.1) | copy-start | bytes 786436
  0.7 1.8 %copy-start.2 = (f32[8,64,128]{2,1,0:T(8,128)S(1)}, f32[8,64,128]{2,1,0:T(8,128)}, u32[]{:S(2)}) copy-start(f32[8,64,128]{2,1,0:T(8,128)} %refs_2_.1) | copy-start | bytes 786436
  0.7 1.9 %copy-start.1 = (f32[8,64,128]{2,1,0:T(8,128)S(1)}, f32[8,64,128]{2,1,0:T(8,128)}, u32[]{:S(2)}) copy-start(f32[8,64,128]{2,1,0:T(8,128)} %refs_1_.1) | copy-start | bytes 786436
  0.7 2.0 %copy-start = (f32[8,64,128]{2,1,0:T(8,128)S(1)}, f32[8,64,128]{2,1,0:T(8,128)}, u32[]{:S(2)}) copy-start(f32[8,64,128]{2,1,0:T(8,128)} %refs_0_.1) | copy-start | bytes 786436
  2.7 18.1 %collective-permute-start.9 = (f32[25,64,128]{2,1,0:T(8,128)S(1)}, f32[25,64,128]{2,1,0:T(8,128)S(1)}, u32[]{:S(2)}, u32[]{:S(2)}) collective-permute-start(f32[25,64,128]{2,1,0:T(8,128)S(1)} %get-tuple-element.155), channel_id=1, source_target_pairs={{2,0},{3,1},{4,2},{5,3},{6,4},{7,5},{8,6},{9,7},{10,8},{11,9},{12,... | collective-permute-start | bytes 2457608 | tf_op jit(solution)/shard_map/cond/branch_2_fun/ppermute | solution.py:601
  4.7 6.0 %collective-permute-start.8 = (f32[32,8,128]{2,1,0:T(8,128)S(1)}, f32[32,8,128]{2,1,0:T(8,128)S(1)}, u32[]{:S(2)}, u32[]{:S(2)}) collective-permute-start(f32[32,8,128]{2,1,0:T(8,128)S(1)} %edges.6), channel_id=1, source_target_pairs={{0,1},{1,0},{2,3},{3,2},{4,5},{5,4},{6,7},{7,6},{8,9},{9,8},{10,11... | collective-permute-start | bytes 393224 | tf_op jit(solution)/shard_map/cond/branch_2_fun/ppermute | solution.py:601
  10.8 10.0 %collective-permute-start.10 = (f32[6,64,128]{2,1,0:T(8,128)S(1)}, f32[6,64,128]{2,1,0:T(8,128)S(1)}, u32[]{:S(2)}, u32[]{:S(2)}) collective-permute-start(f32[6,64,128]{2,1,0:T(8,128)S(1)} %get-tuple-element.156), channel_id=1, source_target_pairs={{0,2},{1,3},{2,4},{3,5},{4,6},{5,7},{6,8},{7,9},{8,10},{9,11},{10,... | collective-permute-start | bytes 589832 | tf_op jit(solution)/shard_map/cond/branch_2_fun/ppermute | solution.py:601
  15.2 5.6 %collective-permute-start.11 = (f32[16,8,128]{2,1,0:T(8,128)S(1)}, f32[16,8,128]{2,1,0:T(8,128)S(1)}, u32[]{:S(2)}, u32[]{:S(2)}) collective-permute-start(f32[16,8,128]{2,1,0:T(8,128)S(1)} %get-tuple-element.157), channel_id=1, source_target_pairs={{2,0},{3,1},{4,2},{5,3},{6,4},{7,5},{8,6},{9,7},{10,8},{11,9},{12,... | collective-permute-start | bytes 196616 | tf_op jit(solution)/shard_map/cond/branch_2_fun/ppermute | solution.py:601

commit v6 on v5

--- a/solution.py
+++ b/solution.py
@@ -223,73 +223,95 @@
     )(*own)
 
 
-def relay_kernel(case, n_sides, *refs):
-    own, beside = refs[:8], refs[8 : 8 + n_sides]
-    up, corners = refs[8 + n_sides :]
+def lift_kernel(case, *refs):
+    own, up = refs[:8], refs[-1]
     planes, width, depth = own[0].shape
-    moves = case[0]
-    gx = lax.axis_index("gx")
-    start = gx * width
-    total = width * lax.axis_size("gx")
-    low = low_half(depth)
-    row = lax.broadcasted_iota(jnp.int32, (TILE, depth), 0)
     ups = up_counts(case)
     up_at = offsets(ups)
-
     column = lax.broadcasted_iota(jnp.int32, (width, depth), 0)
-    whole, half = column_scales(start + column, total)
-    bottom = planes - (3 - moves)
+    whole, half = column_scales(lax.axis_index("gx") * width + column, width * lax.axis_size("gx"))
+    bottom = planes - (3 - case[0])
     for a in range(8):
         if ups[a]:
             up[pl.ds(up_at[a], ups[a])] = own[a][planes - ups[a] :].astype(jnp.float32)
     up[up_at[BX]] = own[BX][bottom] - (TIME_STEP / whole) * own[EY][bottom]
     up[up_at[BY]] = own[BY][bottom] + (TIME_STEP / half) * own[EX][bottom]
 
-    for n in range(n_sides):
-        if n_sides == 1:
-            left_column = jnp.where(gx == 0, start + width, start - HALF)
-        else:
-            left_column = start - HALF if n == 0 else start + width
-        whole, half = column_scales(left_column + jnp.where(row < HALF, row, row - HALF), total)
-        step_whole, step_half = TIME_STEP / whole, TIME_STEP / half
-        tile = lambda a, plane: beside[n][a * planes + plane]
-
-        def folded(a, plane, source, sign):
-            if a == BX:
-                return tile(a, plane) + jnp.where(low, sign * step_whole * tile(EY, source), 0.0)
-            if a == BY - 4:
-                return tile(a, plane) - jnp.where(low, 0.0, turned(sign * step_half * tile(EX, source)))
-            return tile(a, plane)
-
-        count = moves + 2
-        for a in range(4):
-            to = (n * 4 + a) * count
-            corners[pl.ds(to, count)] = beside[n][pl.ds(a * planes, count)]
-            if a in (BX, BY - 4):
-                for plane in (moves, moves + 1):
-                    corners[to + plane] = folded(a, plane, plane + 1, 1.0)
-            for i in range(3 - moves):
-                plane, rows = tile_of(up, up_at[-1], (n * 4 + a) * (3 - moves) + i, width)
-                value = folded(a, bottom, bottom, -1.0) if i == 0 else tile(a, bottom + i)
-                up[plane, rows] = value
-
-
-def relay(case, own, beside):
+
+def lift(case, own, after):
     planes, width, depth = own[0].shape
+    return pl.pallas_call(
+        functools.partial(lift_kernel, case),
+        out_shape=pltpu.VMEM((sum(up_counts(case)), width, depth), jnp.float32),
+        in_specs=[VMEM] * 8 + [ANY] * len(after),
+        out_specs=VMEM,
+        compiler_params=pltpu.CompilerParams(vmem_limit_bytes=32 * 2**20),
+        cost_estimate=pl.CostEstimate(flops=10**7, bytes_accessed=10**7, transcendentals=0),
+        name="lift",
+    )(*own, *after)
+
+
+def relay_kernel(case, planes, width, n_sides, *refs):
+    beside, (on, off) = refs[:n_sides], refs[n_sides:]
+    depth = on.shape[-1]
     moves = case[0]
-    tiles = len(beside) * 4
-    n_up = sum(up_counts(case)) + tile_planes(tiles * (3 - moves), width)
+    gx = lax.axis_index("gx")
+    even = lax.axis_index("gz") % 2 == 0
+    start = gx * width
+    total = width * lax.axis_size("gx")
+    low = low_half(depth)
+    row = lax.broadcasted_iota(jnp.int32, (TILE, depth), 0)
+    bottom = planes - (3 - moves)
+
+    def fill(to_before, to_after):
+        for n in range(n_sides):
+            if n_sides == 1:
+                left_column = jnp.where(gx == 0, start + width, start - HALF)
+            else:
+                left_column = start - HALF if n == 0 else start + width
+            whole, half = column_scales(left_column + jnp.where(row < HALF, row, row - HALF), total)
+            step_whole, step_half = TIME_STEP / whole, TIME_STEP / half
+            tile = lambda a, plane: beside[n][a * planes + plane]
+
+            def folded(a, plane, source, sign):
+                if a == BX:
+                    return tile(a, plane) + jnp.where(low, sign * step_whole * tile(EY, source), 0.0)
+                return tile(a, plane) - jnp.where(
+                    low, 0.0, turned(sign * step_half * tile(EX, source))
+                )
+
+            for a in range(4):
+                for ref, first, count, folds in (
+                    (to_before, 0, moves + 2, ((moves, 1), (moves + 1, 1))),
+                    (to_after, bottom, 3 - moves, ((0, 0),)),
+                ):
+                    to = (n * 4 + a) * count
+                    ref[pl.ds(to, count)] = beside[n][pl.ds(a * planes + first, count)]
+                    if a in (BX, BY - 4):
+                        for plane, above in folds:
+                            at = first + plane
+                            ref[to + plane] = folded(a, at, at + above, 1.0 if above else -1.0)
+
+    @pl.when(even)
+    def _():
+        fill(off, on)
+
+    @pl.when(jnp.logical_not(even))
+    def _():
+        fill(on, off)
+
+
+def relay(case, shape, beside):
+    planes, width, depth = shape
+    tiles = pltpu.VMEM((len(beside) * 4 * (case[0] + 2), TILE, depth), jnp.float32)
     return pl.pallas_call(
-        functools.partial(relay_kernel, case, len(beside)),
-        out_shape=[
-            pltpu.VMEM((n_up, width, depth), jnp.float32),
-            pltpu.VMEM((tiles * (moves + 2), TILE, depth), jnp.float32),
-        ],
-        in_specs=[VMEM] * (8 + len(beside)),
+        functools.partial(relay_kernel, case, planes, width, len(beside)),
+        out_shape=[tiles] * 2,
+        in_specs=[VMEM] * len(beside),
         out_specs=[VMEM] * 2,
         compiler_params=pltpu.CompilerParams(vmem_limit_bytes=32 * 2**20),
         name="relay",
-    )(*own, *beside)
+    )(*beside)
 
 
 def coefficients(code):
@@ -437,10 +459,10 @@
 
 
 def steps_kernel(case, n_sides, planes, width, moved, *refs):
-    rows, down, up, corners = refs[9:13]
-    outs = refs[13:19]
-    cells = Cells((*refs[19:28], rows), width)
-    sems = refs[28]
+    rows, down, up, on, off = refs[9:14]
+    outs = refs[14:20]
+    cells = Cells((*refs[20:29], rows), width)
+    sems = refs[29]
     ext = cells.ext
     moves = case[0]
     base = 3 - moves
@@ -448,6 +470,7 @@
     far = planes + 4
     first = lax.axis_index("gz") == 0
     last = lax.axis_index("gz") == lax.axis_size("gz") - 1
+    even = lax.axis_index("gz") % 2 == 0
     downs, ups = down_counts(case), up_counts(case)
     at, up_at = offsets(downs[:6]), offsets(ups)
     far_at = at[-1]
@@ -468,21 +491,20 @@
     for a in range(6):
         send(a, base + (2 if a >= BX else 3), top - 2)
 
-    def corner(a, plane, count):
-        first_tile = [(n * 4 + a % 4) * (moves + 2) + plane for n in range(n_sides)]
-        return spread_tiles([corners[pl.ds(t, count)] for t in first_tile], a >= 4)
-
+    def corner(a, plane, count, stack, above):
+        tiles = []
+        for n in range(n_sides):
+            span = pl.ds((n * 4 + a % 4) * stack + plane, count)
+            tiles.append(jnp.where(even, on[span], off[span]) if above else jnp.where(even, off[span], on[span]))
+        return spread_tiles(tiles, a >= 4)
+
+    from_above = lambda a, plane, count: corner(a, plane, count, moves + 2, True)
     for a in range(8):
         cells.put(a, top + 1, downs[a], down[pl.ds(at[a], downs[a])], False)
-        cells.put(a, top + 1, downs[a], corner(a, 0, downs[a]), True)
+        cells.put(a, top + 1, downs[a], from_above(a, 0, downs[a]), True)
         if ups[a]:
             cells.put(a, base - ups[a], ups[a], up[pl.ds(up_at[a], ups[a])], False)
-            for i in range(base - ups[a], base):
-                tiles = []
-                for n in range(n_sides):
-                    plane, here = tile_of(up, up_at[-1], (n * 4 + a % 4) * base + i, width)
-                    tiles.append(up[plane, here])
-                cells.put(a, i, 1, spread_tiles(tiles, a >= 4)[None], True)
+            cells.put(a, base - ups[a], ups[a], corner(a, base - ups[a], ups[a], base, False), True)
 
     low = low_half(cells.depth)
     left, right, ghost = pl.ds(0, TILE), pl.ds(width - TILE, TILE), pl.ds(width, TILE)
@@ -501,9 +523,9 @@
 
         raw = []
         for a in range(6):
-            tile, beyond = sent_blocks(a, corner(a, moves + 1, 1)[0])
+            tile, beyond = sent_blocks(a, from_above(a, moves + 1, 1)[0])
             raw.append(blocks(tile, turned(beyond), tile))
-        tile, beyond = sent_blocks(CODES, corner(CODES, downs[CODES], 1)[0])
+        tile, beyond = sent_blocks(CODES, from_above(CODES, downs[CODES], 1)[0])
         factors = [
             blocks(mine, turned(jnp.where(cells.ghost_in[0], theirs, 0.0)), mine)
             for mine, theirs in zip(coefficients(tile), coefficients(beyond))
@@ -588,15 +610,14 @@
     return tuple(found[:6])
 
 
-def passed(block, dz, side):
+def passed(block, to, sides=(0,)):
     size_z, size_x = lax.axis_size("gz"), lax.axis_size("gx")
-    steps_x = {"swap": (1, -1), "right": (1,), "left": (-1,), None: (0,)}[side]
     route = [
-        (z * size_x + x, (z + dz) * size_x + x + dx)
+        (z * size_x + x, to(z) * size_x + x + dx)
         for z in range(size_z)
         for x in range(size_x)
-        for dx in steps_x
-        if 0 <= z + dz < size_z and 0 <= x + dx < size_x
+        for dx in sides
+        if 0 <= to(z) < size_z and 0 <= x + dx < size_x
     ]
     return lax.ppermute(block, ("gz", "gx"), route)
 
@@ -609,13 +630,15 @@
 
     def run(c, own, sent, moved):
         case = CASES[c]
-        down = passed(sent[c], -1, None)
+        down = passed(sent[c], lambda z: z - 1)
         across = edges(sides, own)
-        beside = [passed(block, 0, side) for block, side in zip(across, sides)]
-        up, corners = relay(case, own, beside)
-        up, corners = passed(up, 1, None), passed(corners, -1, None)
+        ways = {"swap": (1, -1), "right": (1,), "left": (-1,)}
+        beside = [passed(block, lambda z: z, ways[side]) for block, side in zip(across, sides)]
+        up = passed(lift(case, own, across), lambda z: z + 1)
+        on, off = relay(case, own[0].shape, beside)
+        on, off = passed(on, lambda z: z ^ 1), passed(off, lambda z: z + 1 if z % 2 else z - 1)
         ready = prepare(case[0], moved, own, beside)
-        return advance(case, len(sides), moved, own[0].shape, ready, [down, up, corners])
+        return advance(case, len(sides), moved, own[0].shape, ready, [down, up, on, off])
 
     return lax.switch(
         which[0],

time: 24.2 us -> 23.6 us (0.975); the launches traced: 23.8 us -> 23.5 us
  waiting for transfers between devices: 5.39 us -> 3.5 us
  starting transfers between devices: 11 us -> 12.6 us
    ppermute x4 -> x5, waiting for transfers between devices: 5.39 us -> 3.5 us  [passed(): return lax.ppermute(block, ('gz', 'gx'), route)]
    ppermute x4 -> x5, starting transfers between devices: 11 us -> 12.6 us  [passed(): return lax.ppermute(block, ('gz', 'gx'), route)]
  transfers between devices with their start and end apart: 4 -> 5, of which waited for: 2 -> 2; matrix products, arithmetic and copies ran while one was open for 0% -> 0% of each run, Pallas kernels for 7% -> 7%
where the time goes in v6:
time: 23.6 us; the launch traced here: 23.5 us
  starting transfers between devices  12.6 us (53%)
  Pallas kernels  6.06 us (26%)
  waiting for transfers between devices  3.5 us (15%)
  between operations  0.94 us (4%)
  loops' own time  0.28 us (1%)
    ppermute x5, starting transfers between devices, passed(): return lax.ppermute(block, ('gz', 'gx'), route)  12.6 us
    ppermute x5, waiting for transfers between devices, passed(): return lax.ppermute(block, ('gz', 'gx'), route)  3.5 us
    pallas_call x1, Pallas kernels, advance(): pl.pallas_call(functools.partial(steps_kernel, case, n_sides, planes, wid...  2.61 us
    pallas_call x1, Pallas kernels, pack(): pl.pallas_call(pack_kernel, out_shape=shapes, in_specs=[ANY] * 9, out_spe...  1.75 us
    pallas_call x1, Pallas kernels, prepare(): pl.pallas_call(functools.partial(prepare_kernel, moves, len(beside)), out...  1.59 us
  transfers between devices with their start and end apart: 5, of which 2 were waited for; matrix products, arithmetic and copies ran while one was open for 0% of the time, Pallas kernels for 7%

profile of v6, /device:TPU:1, one launch (start us, length us, event | category | flops | bytes accessed | tf_op | source)
XLA Modules:
  0.0 23.5 jit_solution(8898253849255833699)
XLA Ops:
  0.6 0.0 copy-start.6
  0.6 0.0 copy-start.7
  0.7 0.0 copy-start.5
  0.7 0.0 copy-start.4
  0.7 0.0 copy-start.3
  0.7 0.0 copy-start.2
  0.7 0.0 copy-start.1
  0.7 0.0 copy-start
  0.7 1.7 %pack.1 = (s32[1]{0:T(128)S(4)}, s32[3]{0:T(128)S(4)}, f32[17,64,128]{2,1,0:T(8,128)S(1)}, f32[19,64,128]{2,1,0:T(8,128)S(1)}, f32[25,64,128]{2,1,0:T(8,128)S(1)}, /*index=5*/f32[27,64,128]{2,1,0:T(8,128)S(1)}) custom-call(f32[8,64,128]{2,1,0:T(8,128)} %refs_0_.1, f32[8,64,128]{2,1,0:T(8,128)} %refs_1_.1, f32[8,64,128]{2,1,0:T(8,128)} %refs_2_.1, ...), custom_call_target="tpu_custom_call" | custom-call | tf_op jit(solution)/shard_map/pack/pallas_call | solution.py:174
  2.5 0.0 copy-done.1
  2.6 0.1 copy-done
  2.7 20.7 %conditional.1 = (f32[8,64,128]{2,1,0:T(8,128)}, f32[8,64,128]{2,1,0:T(8,128)}, f32[8,64,128]{2,1,0:T(8,128)}, f32[8,64,128]{2,1,0:T(8,128)}, f32[8,64,128]{2,1,0:T(8,128)}, /*index=5*/f32[8,64,128]{2,1,0:T(8,128)}) conditional(s32[]{:T(128)} %bitcast, (f32[8,64,128]{2,1,0:T(8,128)S(1)}, f32[8,64,128]{2,1,0:T(8,128)S(1)}, ...), branch_computations={%region_0.0_spmd, %region_1.0_spmd, %region_2.0_spmd, %region_3.0_... | conditional | flops 20000000 | bytes 24980984 | solution.py:643
  2.7 2.1 %collective-permute-start.16 = (f32[27,64,128]{2,1,0:T(8,128)S(1)}, f32[27,64,128]{2,1,0:T(8,128)S(1)}, u32[]{:S(2)}, u32[]{:S(2)}) collective-permute-start(f32[27,64,128]{2,1,0:T(8,128)S(1)} %get-tuple-element.183), channel_id=1, source_target_pairs={{2,0},{3,1},{4,2},{5,3},{6,4},{7,5},{8,6},{9,7},{10,8},{11,9},{12,... | collective-permute-start | bytes 2654216 | tf_op jit(solution)/shard_map/cond/branch_3_fun/ppermute | solution.py:622
  4.9 2.7 %collective-permute-start.15 = (f32[32,8,128]{2,1,0:T(8,128)S(1)}, f32[32,8,128]{2,1,0:T(8,128)S(1)}, u32[]{:S(2)}, u32[]{:S(2)}) collective-permute-start(f32[32,8,128]{2,1,0:T(8,128)S(1)} %edges.7.refs_8_), channel_id=1, source_target_pairs={{0,1},{1,0},{2,3},{3,2},{4,5},{5,4},{6,7},{7,6},{8,9},{9,8},{10,11... | collective-permute-start | bytes 393224 | tf_op jit(solution)/shard_map/cond/branch_3_fun/ppermute | solution.py:622
  7.6 3.3 %collective-permute-start.17 = (f32[3,64,128]{2,1,0:T(8,128)S(1)}, f32[3,64,128]{2,1,0:T(8,128)S(1)}, u32[]{:S(2)}, u32[]{:S(2)}) collective-permute-start(f32[3,64,128]{2,1,0:T(8,128)S(1)} %lift.7), channel_id=1, source_target_pairs={{0,2},{1,3},{2,4},{3,5},{4,6},{5,7},{6,8},{7,9},{8,10},{9,11},{10,... | collective-permute-start | bytes 294920 | tf_op jit(solution)/shard_map/cond/branch_3_fun/ppermute | solution.py:622
  10.9 0.0 collective-permute-done.15.refs_8_.refs_0_
  11.0 0.3 %collective-permute-start.18 = (f32[16,8,128]{2,1,0:T(8,128)S(1)}, f32[16,8,128]{2,1,0:T(8,128)S(1)}, u32[]{:S(2)}, u32[]{:S(2)}) collective-permute-start(f32[16,8,128]{2,1,0:T(8,128)S(1)} %get-tuple-element.184), channel_id=1, source_target_pairs={{0,2},{1,3},{2,0},{3,1},{4,6},{5,7},{6,4},{7,5},{8,10},{9,11},{10,... | collective-permute-start | bytes 196616 | tf_op jit(solution)/shard_map/cond/branch_3_fun/ppermute | solution.py:622
  11.3 4.1 %collective-permute-start.19 = (f32[16,8,128]{2,1,0:T(8,128)S(1)}, f32[16,8,128]{2,1,0:T(8,128)S(1)}, u32[]{:S(2)}, u32[]{:S(2)}) collective-permute-start(f32[16,8,128]{2,1,0:T(8,128)S(1)} %get-tuple-element.185), channel_id=1, source_target_pairs={{2,4},{3,5},{4,2},{5,3},{6,8},{7,9},{8,6},{9,7},{10,12},{11,13},{1... | collective-permute-start | bytes 196616 | tf_op jit(solution)/shard_map/cond/branch_3_fun/ppermute | solution.py:622
  15.4 1.6 %prepare.7 = (f32[13,72,128]{2,1,0:T(8,128)S(1)}, f32[13,72,128]{2,1,0:T(8,128)S(1)}, f32[13,72,128]{2,1,0:T(8,128)S(1)}, f32[13,72,128]{2,1,0:T(8,128)S(1)}, f3...) custom-call(s32[3]{0:T(128)S(4)} %get-tuple-element.164.moved, ...), custom_call_target="tpu_custom_call" | custom-call | flops 10000000 | bytes 10000000 | tf_op jit(solution)/shard_map/cond/branch_3_fun/prepare/pallas_call | solution.py:450
  17.0 2.8 %collective-permute-done.17.refs_11_ = f32[3,64,128]{2,1,0:T(8,128)S(1)} collective-permute-done((f32[3,64,128]{2,1,0:T(8,128)S(1)}, f32[3,64,128]{2,1,0:T(8,128)S(1)}, u32[]{:S(2)}, u32[]{:S(2)}) %collective-permute-start.17) | collective-permute-done | bytes 98336 | tf_op jit(solution)/shard_map/cond/branch_3_fun/ppermute | solution.py:622
  19.8 0.0 collective-permute-done.18.refs_12_
  19.8 0.7 %collective-permute-done.19.refs_13_ = f32[16,8,128]{2,1,0:T(8,128)S(1)} collective-permute-done((f32[16,8,128]{2,1,0:T(8,128)S(1)}, f32[16,8,128]{2,1,0:T(8,128)S(1)}, u32[]{:S(2)}, u32[]{:S(2)}) %collective-permute-start.19) | collective-permute-done | bytes 65568 | tf_op jit(solution)/shard_map/cond/branch_3_fun/ppermute | solution.py:622
  20.5 0.0 collective-permute-done.16.refs_10_
  20.5 2.6 %steps.7 = (f32[8,64,128]{2,1,0:T(8,128)}, f32[8,64,128]{2,1,0:T(8,128)}, f32[8,64,128]{2,1,0:T(8,128)}, f32[8,64,128]{2,1,0:T(8,128)}, f32[8,64,128]{2,1,0:T(8,...) custom-call(s32[3]{0:T(128)S(4)} %get-tuple-element.164.moved, ...), custom_call_target="tpu_custom_call", output_to_operand_aliasing={{6}: (1, {}), {7}: (2, {}), {8}: (3, {}), {9}: (4, {}), {10... | custom-call | tf_op jit(solution)/shard_map/cond/branch_3_fun/steps/pallas_call | solution.py:600
  (9 shorter events, 0.1 us)
Async XLA Ops:
  0.6 1.8 %copy-start.6 = (s32[8,64,128]{2,1,0:T(8,128)S(1)}, s32[8,64,128]{2,1,0:T(8,128)}, u32[]{:S(2)}) copy-start(s32[8,64,128]{2,1,0:T(8,128)} %refs_6_.1) | copy-start | bytes 786436
  0.6 1.8 %copy-start.7 = (s32[8,64,128]{2,1,0:T(8,128)S(1)}, s32[8,64,128]{2,1,0:T(8,128)}, u32[]{:S(2)}) copy-start(s32[8,64,128]{2,1,0:T(8,128)} %refs_7_.1) | copy-start | bytes 786436
  0.7 1.8 %copy-start.5 = (f32[8,64,128]{2,1,0:T(8,128)S(1)}, f32[8,64,128]{2,1,0:T(8,128)}, u32[]{:S(2)}) copy-start(f32[8,64,128]{2,1,0:T(8,128)} %refs_5_.1) | copy-start | bytes 786436
  0.7 1.8 %copy-start.4 = (f32[8,64,128]{2,1,0:T(8,128)S(1)}, f32[8,64,128]{2,1,0:T(8,128)}, u32[]{:S(2)}) copy-start(f32[8,64,128]{2,1,0:T(8,128)} %refs_4_.1) | copy-start | bytes 786436
  0.7 1.8 %copy-start.3 = (f32[8,64,128]{2,1,0:T(8,128)S(1)}, f32[8,64,128]{2,1,0:T(8,128)}, u32[]{:S(2)}) copy-start(f32[8,64,128]{2,1,0:T(8,128)} %refs_3_.1) | copy-start | bytes 786436
  0.7 1.8 %copy-start.2 = (f32[8,64,128]{2,1,0:T(8,128)S(1)}, f32[8,64,128]{2,1,0:T(8,128)}, u32[]{:S(2)}) copy-start(f32[8,64,128]{2,1,0:T(8,128)} %refs_2_.1) | copy-start | bytes 786436
  0.7 1.9 %copy-start.1 = (f32[8,64,128]{2,1,0:T(8,128)S(1)}, f32[8,64,128]{2,1,0:T(8,128)}, u32[]{:S(2)}) copy-start(f32[8,64,128]{2,1,0:T(8,128)} %refs_1_.1) | copy-start | bytes 786436
  0.7 2.0 %copy-start = (f32[8,64,128]{2,1,0:T(8,128)S(1)}, f32[8,64,128]{2,1,0:T(8,128)}, u32[]{:S(2)}) copy-start(f32[8,64,128]{2,1,0:T(8,128)} %refs_0_.1) | copy-start | bytes 786436
  2.7 17.9 %collective-permute-start.16 = (f32[27,64,128]{2,1,0:T(8,128)S(1)}, f32[27,64,128]{2,1,0:T(8,128)S(1)}, u32[]{:S(2)}, u32[]{:S(2)}) collective-permute-start(f32[27,64,128]{2,1,0:T(8,128)S(1)} %get-tuple-element.183), channel_id=1, source_target_pairs={{2,0},{3,1},{4,2},{5,3},{6,4},{7,5},{8,6},{9,7},{10,8},{11,9},{12,... | collective-permute-start | bytes 2654216 | tf_op jit(solution)/shard_map/cond/branch_3_fun/ppermute | solution.py:622
  4.9 6.1 %collective-permute-start.15 = (f32[32,8,128]{2,1,0:T(8,128)S(1)}, f32[32,8,128]{2,1,0:T(8,128)S(1)}, u32[]{:S(2)}, u32[]{:S(2)}) collective-permute-start(f32[32,8,128]{2,1,0:T(8,128)S(1)} %edges.7.refs_8_), channel_id=1, source_target_pairs={{0,1},{1,0},{2,3},{3,2},{4,5},{5,4},{6,7},{7,6},{8,9},{9,8},{10,11... | collective-permute-start | bytes 393224 | tf_op jit(solution)/shard_map/cond/branch_3_fun/ppermute | solution.py:622
  7.6 12.2 %collective-permute-start.17 = (f32[3,64,128]{2,1,0:T(8,128)S(1)}, f32[3,64,128]{2,1,0:T(8,128)S(1)}, u32[]{:S(2)}, u32[]{:S(2)}) collective-permute-start(f32[3,64,128]{2,1,0:T(8,128)S(1)} %lift.7), channel_id=1, source_target_pairs={{0,2},{1,3},{2,4},{3,5},{4,6},{5,7},{6,8},{7,9},{8,10},{9,11},{10,... | collective-permute-start | bytes 294920 | tf_op jit(solution)/shard_map/cond/branch_3_fun/ppermute | solution.py:622
  11.0 8.8 %collective-permute-start.18 = (f32[16,8,128]{2,1,0:T(8,128)S(1)}, f32[16,8,128]{2,1,0:T(8,128)S(1)}, u32[]{:S(2)}, u32[]{:S(2)}) collective-permute-start(f32[16,8,128]{2,1,0:T(8,128)S(1)} %get-tuple-element.184), channel_id=1, source_target_pairs={{0,2},{1,3},{2,0},{3,1},{4,6},{5,7},{6,4},{7,5},{8,10},{9,11},{10,... | collective-permute-start | bytes 196616 | tf_op jit(solution)/shard_map/cond/branch_3_fun/ppermute | solution.py:622
  11.3 9.2 %collective-permute-start.19 = (f32[16,8,128]{2,1,0:T(8,128)S(1)}, f32[16,8,128]{2,1,0:T(8,128)S(1)}, u32[]{:S(2)}, u32[]{:S(2)}) collective-permute-start(f32[16,8,128]{2,1,0:T(8,128)S(1)} %get-tuple-element.185), channel_id=1, source_target_pairs={{2,4},{3,5},{4,2},{5,3},{6,8},{7,9},{8,6},{9,7},{10,12},{11,13},{1... | collective-permute-start | bytes 196616 | tf_op jit(solution)/shard_map/cond/branch_3_fun/ppermute | solution.py:622

commit v7 on v6

--- a/solution.py
+++ b/solution.py
@@ -23,7 +23,7 @@
 def down_counts(case):
     moves, now = case
     later = moves - now
-    return (moves + 1,) * 6 + (later + 1, later + 1)
+    return (moves,) * 6 + (later + 1, later)
 
 
 def up_counts(case):
@@ -117,48 +117,82 @@
         down = sent[c]
         downs = down_counts(case)
         at = offsets(downs[:6])
-        moves = case[0]
-        far = moves + 1
-        cell = 1 + moves - case[1]
+        far, first_move = case
 
         @pl.when(case_index == c)
         def _():
             field = lambda a, plane: near[a, plane]
             for a in range(6):
                 down[pl.ds(at[a], far)] = near[a, :far]
+
             folded = {}
-            for plane in (far - 1, far):
+            for plane in range(far - 1, far + 2):
                 folded[BX, plane] = field(BX, plane) + step_whole * field(EY, plane + 1)
                 folded[BY, plane] = field(BY, plane) - step_half * field(EX, plane + 1)
             down[at[BX] + far - 1] = folded[BX, far - 1]
             down[at[BY] + far - 1] = folded[BY, far - 1]
 
-            def magnetic(plane):
-                ex, ey, es = field(EX, plane), field(EY, plane), field(ES, plane)
+            def radial_vertical(bx, by, ex, ey, es):
                 weighted = whole * es
-                bx = folded[BX, plane] - TIME_STEP * (next_y(es) - es) - step_whole * ey
-                by = folded[BY, plane] + step_half * (ex + next_x(weighted) - weighted)
+                bx = bx - TIME_STEP * (next_y(es) - es) - step_whole * ey
+                by = by + step_half * (ex + next_x(weighted) - weighted)
                 return bx, by
 
-            bx_below, by_below = magnetic(far - 1)
-            bx, by = magnetic(far)
-            ex, ey = field(EX, far), field(EY, far)
-            bs = field(BS, far) - TIME_STEP * ((next_x(ey) - ey) - (next_y(ex) - ex))
-            code = near_int[0, cell]
-            kept, gained = coefficients(code)
-            weighted = half * bs
+            def longitudinal(bs, ex, ey):
+                return bs - TIME_STEP * ((next_x(ey) - ey) - (next_y(ex) - ex))
+
+            def electric(ex, ey, bs, over_x, over_y, factors):
+                kept, gained = factors
+                weighted = half * bs
+                ex = kept * ex + gained * ((bs - last_y(bs)) - one_half * over_y)
+                ey = kept * ey + gained * (one_whole * (over_x - (weighted - last_x(weighted))))
+                return ex, ey
+
+            now_b = {}
+            for plane in range(far - 1, far + 2):
+                now_b[plane] = radial_vertical(
+                    folded[BX, plane],
+                    folded[BY, plane],
+                    field(EX, plane),
+                    field(EY, plane),
+                    field(ES, plane),
+                )
+            now_e, now_s = {}, {}
+            for plane in (far, far + 1):
+                ex, ey = field(EX, plane), field(EY, plane)
+                now_s[plane] = longitudinal(field(BS, plane), ex, ey)
+                factors = coefficients(near_int[0, plane - first_move])
+                over = [up - under for up, under in zip(now_b[plane], now_b[plane - 1])]
+                now_e[plane] = electric(ex, ey, now_s[plane], *over, factors)
+                if plane == far:
+                    bx, by = now_b[far]
+                    current = CURRENT_SCALE * near_int[1, far - first_move].astype(jnp.float32)
+                    es = factors[0] * field(ES, far) + factors[1] * (
+                        (by - last_x(by)) - (bx - last_y(bx)) - current
+                    )
             place = at[-1]
-            down[place] = kept * ex + gained * ((bs - last_y(bs)) - one_half * (by - by_below))
-            down[place + 1] = kept * ey + gained * (
-                one_whole * ((bx - bx_below) - (weighted - last_x(weighted)))
+            down[place], down[place + 1] = now_e[far]
+
+            ex, ey = now_e[far]
+            bx, by = now_b[far]
+            bx, by = radial_vertical(
+                bx + step_whole * now_e[far + 1][1], by - step_half * now_e[far + 1][0], ex, ey, es
             )
-            place += 2
+            bs = longitudinal(now_s[far], ex, ey)
+            factors = coefficients(near_int[0, far - (first_move + moved_here[1])])
+            down[place + 2], down[place + 3] = electric(ex, ey, bs, bx, by, factors)
+
+            place += 4
             for n, a in enumerate((CODES, BUNCH)):
-                down[pl.ds(place, cell)] = near_int[n, :cell].astype(jnp.float32)
-                place += cell
-            edges = [ex, ey, field(ES, far), folded[BX, far], folded[BY, far], field(BS, far)]
-            edges.append(code.astype(jnp.float32))
-            for n, v in enumerate(edges):
+                if downs[a]:
+                    down[pl.ds(place, downs[a])] = near_int[n, : downs[a]].astype(jnp.float32)
+                place += downs[a]
+            tiles = [field(a, far) for a in range(6)]
+            tiles.append(near_int[1, far - first_move].astype(jnp.float32))
+            tiles += [field(EX, far + 1), field(EY, far + 1), field(ES, far + 1)]
+            tiles += [folded[BX, far + 1], folded[BY, far + 1], field(BS, far + 1)]
+            tiles.append(near_int[0, far + 1 - first_move].astype(jnp.float32))
+            for n, v in enumerate(tiles):
                 tile = jnp.where(low, turned(v[width - TILE :]), turned(v[:TILE]))
                 plane, rows = tile_of(down, place, n, width)
                 down[plane, rows] = tile
@@ -169,7 +203,8 @@
     near = max(case[0] for case in CASES) + 3
     shapes = [pltpu.SMEM((1,), jnp.int32), pltpu.SMEM((STEPS,), jnp.int32)]
     for case in CASES:
-        count = sum(down_counts(case)) + 2 + tile_planes(7, width)
+        count = sum(down_counts(case)) + 4 + tile_planes(14, width)
+        count += case == (1, 1)
         shapes.append(pltpu.VMEM((count, width, depth), jnp.float32))
     found = pl.pallas_call(
         pack_kernel,
@@ -282,7 +317,7 @@
 
             for a in range(4):
                 for ref, first, count, folds in (
-                    (to_before, 0, moves + 2, ((moves, 1), (moves + 1, 1))),
+                    (to_before, 0, moves + 2, ((moves - 1, 1), (moves + 1, 1))),
                     (to_after, bottom, 3 - moves, ((0, 0),)),
                 ):
                     to = (n * 4 + a) * count
@@ -427,7 +462,7 @@
         cells.put(a, base, planes, spread_tiles(tiles, a >= 4), True)
     for a in (EX, EY):
         cells.ext[a][0] = jnp.zeros((tall, depth), jnp.float32)
-        cells.ext[a][planes + 4] = jnp.zeros((tall, depth), jnp.float32)
+        cells.ext[a][planes + 3] = jnp.zeros((tall, depth), jnp.float32)
 
     moved_now = 0
     for t in range(STEPS):
@@ -445,7 +480,7 @@
     planes, width, depth = own[0].shape
     tall = width + TILE
     vmem = lambda *shape: pltpu.VMEM(shape, jnp.float32)
-    shapes = [vmem(planes + 5, tall, depth)] * 9
+    shapes = [vmem(planes + 4, tall, depth)] * 9
     shapes += [vmem(7, tall, depth)]
     return pl.pallas_call(
         functools.partial(prepare_kernel, moves, len(beside)),
@@ -453,7 +488,7 @@
         in_specs=[SMEM] + [VMEM] * (8 + len(beside)),
         out_specs=[VMEM] * len(shapes),
         compiler_params=pltpu.CompilerParams(vmem_limit_bytes=32 * 2**20),
-        cost_estimate=pl.CostEstimate(flops=10**7, bytes_accessed=10**7, transcendentals=0),
+        cost_estimate=pl.CostEstimate(flops=32 * 10**8, bytes_accessed=10**7, transcendentals=0),
         name="prepare",
     )(moved, *own, *beside)
 
@@ -467,14 +502,14 @@
     moves = case[0]
     base = 3 - moves
     top = base + planes - 1
-    far = planes + 4
+    far = planes + 3
     first = lax.axis_index("gz") == 0
     last = lax.axis_index("gz") == lax.axis_size("gz") - 1
     even = lax.axis_index("gz") % 2 == 0
     downs, ups = down_counts(case), up_counts(case)
     at, up_at = offsets(downs[:6]), offsets(ups)
     far_at = at[-1]
-    at = at[:6] + [far_at + 2, far_at + 2 + downs[CODES]]
+    at = at[:6] + [far_at + 4, far_at + 4 + downs[CODES]]
     tiles_at = at[BUNCH] + downs[BUNCH]
     copies = []
 
@@ -500,8 +535,9 @@
 
     from_above = lambda a, plane, count: corner(a, plane, count, moves + 2, True)
     for a in range(8):
-        cells.put(a, top + 1, downs[a], down[pl.ds(at[a], downs[a])], False)
-        cells.put(a, top + 1, downs[a], from_above(a, 0, downs[a]), True)
+        if downs[a]:
+            cells.put(a, top + 1, downs[a], down[pl.ds(at[a], downs[a])], False)
+            cells.put(a, top + 1, downs[a], from_above(a, 0, downs[a]), True)
         if ups[a]:
             cells.put(a, base - ups[a], ups[a], up[pl.ds(up_at[a], ups[a])], False)
             cells.put(a, base - ups[a], ups[a], corner(a, base - ups[a], ups[a], base, False), True)
@@ -512,55 +548,92 @@
     def blocks(right_tile, ghost_tile, left_tile):
         return jnp.where(low, right_tile, ghost_tile), jnp.where(low, ghost_tile, left_tile)
 
-    def far_plane():
-        def kept_blocks(ref, *plane):
-            return blocks(*(turned(ref[(*plane, where)]) for where in (right, ghost, left)))
-
-        def sent_blocks(a, ghost_tile):
-            plane, here = tile_of(down, tiles_at, min(a, 6), width)
-            tile = down[plane, here]
-            return tile, jnp.where(cells.ghost_in[0], ghost_tile, 0.0)
-
-        raw = []
-        for a in range(6):
-            tile, beyond = sent_blocks(a, from_above(a, moves + 1, 1)[0])
-            raw.append(blocks(tile, turned(beyond), tile))
-        tile, beyond = sent_blocks(CODES, from_above(CODES, downs[CODES], 1)[0])
-        factors = [
-            blocks(mine, turned(jnp.where(cells.ghost_in[0], theirs, 0.0)), mine)
-            for mine, theirs in zip(coefficients(tile), coefficients(beyond))
-        ]
-        const = [kept_blocks(rows, n) for n in range(7)]
+    def kept_blocks(ref, *plane):
+        return blocks(*(turned(ref[(*plane, where)]) for where in (right, ghost, left)))
+
+    def sent_blocks(a, n, plane):
+        where, here = tile_of(down, tiles_at, n, width)
+        tile = down[where, here]
+        beyond = jnp.where(cells.ghost_in[0], from_above(a, plane, 1)[0], 0.0)
+        return tile, beyond
+
+    def both(tiles):
+        return blocks(tiles[0], turned(tiles[1]), tiles[0])
+
+    const = [kept_blocks(rows, n) for n in range(7)]
+
+    def block_magnetic(fields, next_e, b):
+        ex, ey, es, bx, by, bs = fields
+        row = [v[b] for v in const]
+        weighted = row[0] * es
+        above_x, above_y = next_e if next_e else (0.0, 0.0)
+        bx = bx - row[4] * (next_y(es) - es) + row[5] * (above_y - ey)
+        by = by - row[6] * ((above_x - ex) - (next_x(weighted) - weighted))
+        bs = bs - row[4] * ((next_x(ey) - ey) - (next_y(ex) - ex))
+        return ex, ey, es, bx, by, bs
+
+    def block_electric(fields, below, factors, b):
+        ex, ey, _, bx, by, bs = fields
+        row = [v[b] for v in const]
+        kept, gained = factors
+        weighted = row[1] * bs
+        ex = kept * ex + gained * ((bs - last_y(bs)) - row[3] * (by - below[1]))
+        ey = kept * ey + gained * (row[2] * ((bx - below[0]) - (weighted - last_x(weighted))))
+        return ex, ey
+
+    tile_row = lax.broadcasted_iota(jnp.int32, (TILE, cells.depth), 0)
+
+    def set_far(values, found, edge):
+        for a in (EX, EY):
+            right_block, left_block = found[0][a], found[1][a]
+            ext[a][far, pl.ds(0, width)] = jnp.where(last, 0.0, values[a])
+            at_right = jnp.where(tile_row >= TILE - edge, turned(right_block), values[a][width - TILE :])
+            at_left = jnp.where(tile_row < edge, turned(left_block), values[a][:TILE])
+            ext[a][far, right] = jnp.where(last, 0.0, at_right)
+            ext[a][far, left] = jnp.where(last, 0.0, at_left)
+            beyond = turned(jnp.where(low, left_block, right_block))
+            ext[a][far, ghost] = jnp.where(last, 0.0, beyond)
+
+    def far_first(moved_now):
+        planes_raw = [[both(sent_blocks(a, n * 7 + a, moves + n)) for a in range(6)] for n in range(2)]
+        bunch = both(sent_blocks(BUNCH, 6, moves - case[1]))
+        tile, beyond = sent_blocks(CODES, 13, moves + 1 - case[1])
+        over = [both(pair) for pair in zip(coefficients(tile), coefficients(beyond))]
+        own = [kept_blocks(ref, far - moved_now) for ref in (cells.keep, cells.gain)]
+        below = [kept_blocks(ext[a], far - 1) for a in (BX, BY)]
+        state = []
+        for b in range(2):
+            raw, raw_over = ([v[b] for v in plane] for plane in planes_raw)
+            mine = block_magnetic(raw, raw_over[:2], b)
+            theirs = block_magnetic(raw_over, None, b)
+            factors = [v[b] for v in own]
+            ex, ey = block_electric(mine, [v[b] for v in below], factors, b)
+            ex_over, ey_over = block_electric(theirs, mine[3:5], [v[b] for v in over], b)
+            bx, by = mine[3:5]
+            es = factors[0] * mine[2] + factors[1] * (
+                (by - last_x(by)) - (bx - last_y(bx)) - CURRENT_SCALE * bunch[b]
+            )
+            state.append(((ex, ey, es, *mine[3:]), (ex_over, ey_over)))
+        set_far([down[far_at], down[far_at + 1]], [fields[:2] for fields, _ in state], 1)
+        return state
+
+    def far_second(state, moved_now):
+        own = [kept_blocks(ref, far - moved_now) for ref in (cells.keep, cells.gain)]
         below = [kept_blocks(ext[a], far - 1) for a in (BX, BY)]
         found = []
         for b in range(2):
-            ex, ey, es, bx, by, bs = (v[b] for v in raw)
-            kept, gained = (v[b] for v in factors)
-            row = [v[b] for v in const]
-            weighted = row[0] * es
-            bx = bx - row[4] * (next_y(es) - es) - row[5] * ey
-            by = by + row[6] * (ex + next_x(weighted) - weighted)
-            bs = bs - row[4] * ((next_x(ey) - ey) - (next_y(ex) - ex))
-            weighted = row[1] * bs
-            ex = kept * ex + gained * ((bs - last_y(bs)) - row[3] * (by - below[1][b]))
-            ey = kept * ey + gained * (
-                row[2] * ((bx - below[0][b]) - (weighted - last_x(weighted)))
-            )
-            found.append((ex, ey))
-        n_row = lax.broadcasted_iota(jnp.int32, (TILE, cells.depth), 0)
-        for a in (EX, EY):
-            right_block, left_block = found[0][a], found[1][a]
-            ext[a][far, pl.ds(0, width)] = down[far_at + a]
-            ext[a][far, right] = jnp.where(
-                n_row == TILE - 1, turned(right_block), down[far_at + a, right]
-            )
-            ext[a][far, left] = jnp.where(n_row == 0, turned(left_block), down[far_at + a, left])
-            ext[a][far, ghost] = turned(jnp.where(low, left_block, right_block))
-
+            fields = block_magnetic(*state[b], b)
+            found.append(block_electric(fields, [v[b] for v in below], [v[b] for v in own], b))
+        gained = cells.gain[far - moved_now, mine]
+        ex = down[far_at + 2] + gained * (rows[3, mine] * ext[BY][far - 1, mine])
+        ey = down[far_at + 3] - gained * (rows[2, mine] * ext[BX][far - 1, mine])
+        set_far([ex, ey], found, 2)
+
+    mine = pl.ds(0, width)
     moved_now = 0
     for t in range(STEPS):
         moved_now = moved_now + moved[t]
-        above = moves + (2 if t == 0 else 3)
+        above = moves + 1 + t
         cells.magnetic(t, base)
         cells.magnetic(top - t, above)
 
@@ -578,7 +651,9 @@
                 send(a, 3, base + 3)
         cells.electric(top - t, above, moved_now)
         if t == 0:
-            far_plane()
+            edge_state = far_first(moved_now)
+        elif t == 1:
+            far_second(edge_state, moved_now)
         if t == STEPS - 1:
             for a in (EX, EY, ES):
                 send(a, top - 2, planes + 3)

time: 23.6 us -> 22.1 us (0.936)
  waiting for transfers between devices: 3.5 us -> 2.15 us
    ppermute x5, waiting for transfers between devices: 3.5 us -> 2.15 us  [passed(): return lax.ppermute(block, ('gz', 'gx'), route)]
where the time goes in v7:
time: 22.1 us
  starting transfers between devices  12.6 us (57%)
  Pallas kernels  5.98 us (27%)
  waiting for transfers between devices  2.15 us (10%)
  between operations  0.96 us (4%)
  loops' own time  0.31 us (1%)
    ppermute x5, starting transfers between devices, passed(): return lax.ppermute(block, ('gz', 'gx'), route)  12.6 us
    pallas_call x1, Pallas kernels, advance(): pl.pallas_call(functools.partial(steps_kernel, case, n_sides, planes, wid...  2.4 us
    ppermute x5, waiting for transfers between devices, passed(): return lax.ppermute(block, ('gz', 'gx'), route)  2.15 us
    pallas_call x1, Pallas kernels, pack(): pl.pallas_call(pack_kernel, out_shape=shapes, in_specs=[ANY] * 9, out_spe...  1.93 us
    pallas_call x1, Pallas kernels, prepare(): pl.pallas_call(functools.partial(prepare_kernel, moves, len(beside)), out...  1.53 us
  transfers between devices with their start and end apart: 5, of which 2 were waited for; matrix products, arithmetic and copies ran while one was open for 0% of the time, Pallas kernels for 7%

profile of v7, /device:TPU:1, one launch (start us, length us, event | category | flops | bytes accessed | tf_op | source)
XLA Modules:
  0.0 22.1 jit_solution(5353570888706962903)
XLA Ops:
  0.6 0.0 copy-start.6
  0.6 0.0 copy-start.7
  0.7 0.0 copy-start.5
  0.7 0.0 copy-start.4
  0.7 0.0 copy-start.3
  0.7 0.0 copy-start.2
  0.7 0.0 copy-start.1
  0.7 0.0 copy-start
  0.7 1.9 %pack.1 = (s32[1]{0:T(128)S(4)}, s32[3]{0:T(128)S(4)}, f32[14,64,128]{2,1,0:T(8,128)S(1)}, f32[15,64,128]{2,1,0:T(8,128)S(1)}, f32[21,64,128]{2,1,0:T(8,128)S(1)}, /*index=5*/f32[23,64,128]{2,1,0:T(8,128)S(1)}) custom-call(f32[8,64,128]{2,1,0:T(8,128)} %refs_0_.1, f32[8,64,128]{2,1,0:T(8,128)} %refs_1_.1, f32[8,64,128]{2,1,0:T(8,128)} %refs_2_.1, ...), custom_call_target="tpu_custom_call" | custom-call | tf_op jit(solution)/shard_map/pack/pallas_call | solution.py:209
  2.7 0.0 copy-done.6
  2.7 0.0 copy-done.7
  2.7 19.1 %conditional.1 = (f32[8,64,128]{2,1,0:T(8,128)}, f32[8,64,128]{2,1,0:T(8,128)}, f32[8,64,128]{2,1,0:T(8,128)}, f32[8,64,128]{2,1,0:T(8,128)}, f32[8,64,128]{2,1,0:T(8,128)}, /*index=5*/f32[8,64,128]{2,1,0:T(8,128)}) conditional(s32[]{:T(128)} %bitcast, (f32[8,64,128]{2,1,0:T(8,128)S(1)}, f32[8,64,128]{2,1,0:T(8,128)S(1)}, ...), branch_computations={%region_0.0_spmd, %region_1.0_spmd, %region_2.0_spmd, %region_3.0_... | conditional | flops 3209999872 | bytes 24456696 | solution.py:718
  2.8 2.1 %collective-permute-start.16 = (f32[23,64,128]{2,1,0:T(8,128)S(1)}, f32[23,64,128]{2,1,0:T(8,128)S(1)}, u32[]{:S(2)}, u32[]{:S(2)}) collective-permute-start(f32[23,64,128]{2,1,0:T(8,128)S(1)} %get-tuple-element.183), channel_id=1, source_target_pairs={{2,0},{3,1},{4,2},{5,3},{6,4},{7,5},{8,6},{9,7},{10,8},{11,9},{12,... | collective-permute-start | bytes 2261000 | tf_op jit(solution)/shard_map/cond/branch_3_fun/ppermute | solution.py:697
  5.0 2.7 %collective-permute-start.15 = (f32[32,8,128]{2,1,0:T(8,128)S(1)}, f32[32,8,128]{2,1,0:T(8,128)S(1)}, u32[]{:S(2)}, u32[]{:S(2)}) collective-permute-start(f32[32,8,128]{2,1,0:T(8,128)S(1)} %edges.7.refs_8_), channel_id=1, source_target_pairs={{0,1},{1,0},{2,3},{3,2},{4,5},{5,4},{6,7},{7,6},{8,9},{9,8},{10,11... | collective-permute-start | bytes 393224 | tf_op jit(solution)/shard_map/cond/branch_3_fun/ppermute | solution.py:697
  7.7 3.3 %collective-permute-start.17 = (f32[3,64,128]{2,1,0:T(8,128)S(1)}, f32[3,64,128]{2,1,0:T(8,128)S(1)}, u32[]{:S(2)}, u32[]{:S(2)}) collective-permute-start(f32[3,64,128]{2,1,0:T(8,128)S(1)} %lift.7), channel_id=1, source_target_pairs={{0,2},{1,3},{2,4},{3,5},{4,6},{5,7},{6,8},{7,9},{8,10},{9,11},{10,... | collective-permute-start | bytes 294920 | tf_op jit(solution)/shard_map/cond/branch_3_fun/ppermute | solution.py:697
  11.1 0.0 collective-permute-done.15.refs_8_.refs_0_
  11.1 0.3 %collective-permute-start.18 = (f32[16,8,128]{2,1,0:T(8,128)S(1)}, f32[16,8,128]{2,1,0:T(8,128)S(1)}, u32[]{:S(2)}, u32[]{:S(2)}) collective-permute-start(f32[16,8,128]{2,1,0:T(8,128)S(1)} %get-tuple-element.184), channel_id=1, source_target_pairs={{0,2},{1,3},{2,0},{3,1},{4,6},{5,7},{6,4},{7,5},{8,10},{9,11},{10,... | collective-permute-start | bytes 196616 | tf_op jit(solution)/shard_map/cond/branch_3_fun/ppermute | solution.py:697
  11.5 4.1 %collective-permute-start.19 = (f32[16,8,128]{2,1,0:T(8,128)S(1)}, f32[16,8,128]{2,1,0:T(8,128)S(1)}, u32[]{:S(2)}, u32[]{:S(2)}) collective-permute-start(f32[16,8,128]{2,1,0:T(8,128)S(1)} %get-tuple-element.185), channel_id=1, source_target_pairs={{2,4},{3,5},{4,2},{5,3},{6,8},{7,9},{8,6},{9,7},{10,12},{11,13},{1... | collective-permute-start | bytes 196616 | tf_op jit(solution)/shard_map/cond/branch_3_fun/ppermute | solution.py:697
  15.6 1.5 %prepare.7 = (f32[12,72,128]{2,1,0:T(8,128)S(1)}, f32[12,72,128]{2,1,0:T(8,128)S(1)}, f32[12,72,128]{2,1,0:T(8,128)S(1)}, f32[12,72,128]{2,1,0:T(8,128)S(1)}, f3...) custom-call(s32[3]{0:T(128)S(4)} %get-tuple-element.164.moved, ...), custom_call_target="tpu_custom_call" | custom-call | flops 3200000000 | bytes 10000000 | tf_op jit(solution)/shard_map/cond/branch_3_fun/prepare/pallas_call | solution.py:485
  17.1 0.8 %collective-permute-done.17.refs_11_ = f32[3,64,128]{2,1,0:T(8,128)S(1)} collective-permute-done((f32[3,64,128]{2,1,0:T(8,128)S(1)}, f32[3,64,128]{2,1,0:T(8,128)S(1)}, u32[]{:S(2)}, u32[]{:S(2)}) %collective-permute-start.17) | collective-permute-done | bytes 98336 | tf_op jit(solution)/shard_map/cond/branch_3_fun/ppermute | solution.py:697
  17.9 0.0 collective-permute-done.18.refs_12_
  17.9 1.4 %collective-permute-done.19.refs_13_ = f32[16,8,128]{2,1,0:T(8,128)S(1)} collective-permute-done((f32[16,8,128]{2,1,0:T(8,128)S(1)}, f32[16,8,128]{2,1,0:T(8,128)S(1)}, u32[]{:S(2)}, u32[]{:S(2)}) %collective-permute-start.19) | collective-permute-done | bytes 65568 | tf_op jit(solution)/shard_map/cond/branch_3_fun/ppermute | solution.py:697
  19.2 0.0 collective-permute-done.16.refs_10_
  19.3 2.4 %steps.7 = (f32[8,64,128]{2,1,0:T(8,128)}, f32[8,64,128]{2,1,0:T(8,128)}, f32[8,64,128]{2,1,0:T(8,128)}, f32[8,64,128]{2,1,0:T(8,128)}, f32[8,64,128]{2,1,0:T(8,...) custom-call(s32[3]{0:T(128)S(4)} %get-tuple-element.164.moved, ...), custom_call_target="tpu_custom_call", output_to_operand_aliasing={{6}: (1, {}), {7}: (2, {}), {8}: (3, {}), {9}: (4, {}), {10... | custom-call | tf_op jit(solution)/shard_map/cond/branch_3_fun/steps/pallas_call | solution.py:675
  (9 shorter events, 0.1 us)
Async XLA Ops:
  0.6 2.0 %copy-start.6 = (s32[8,64,128]{2,1,0:T(8,128)S(1)}, s32[8,64,128]{2,1,0:T(8,128)}, u32[]{:S(2)}) copy-start(s32[8,64,128]{2,1,0:T(8,128)} %refs_6_.1) | copy-start | bytes 786436
  0.6 2.0 %copy-start.7 = (s32[8,64,128]{2,1,0:T(8,128)S(1)}, s32[8,64,128]{2,1,0:T(8,128)}, u32[]{:S(2)}) copy-start(s32[8,64,128]{2,1,0:T(8,128)} %refs_7_.1) | copy-start | bytes 786436
  0.7 2.0 %copy-start.5 = (f32[8,64,128]{2,1,0:T(8,128)S(1)}, f32[8,64,128]{2,1,0:T(8,128)}, u32[]{:S(2)}) copy-start(f32[8,64,128]{2,1,0:T(8,128)} %refs_5_.1) | copy-start | bytes 786436
  0.7 2.0 %copy-start.4 = (f32[8,64,128]{2,1,0:T(8,128)S(1)}, f32[8,64,128]{2,1,0:T(8,128)}, u32[]{:S(2)}) copy-start(f32[8,64,128]{2,1,0:T(8,128)} %refs_4_.1) | copy-start | bytes 786436
  0.7 2.0 %copy-start.3 = (f32[8,64,128]{2,1,0:T(8,128)S(1)}, f32[8,64,128]{2,1,0:T(8,128)}, u32[]{:S(2)}) copy-start(f32[8,64,128]{2,1,0:T(8,128)} %refs_3_.1) | copy-start | bytes 786436
  0.7 2.0 %copy-start.2 = (f32[8,64,128]{2,1,0:T(8,128)S(1)}, f32[8,64,128]{2,1,0:T(8,128)}, u32[]{:S(2)}) copy-start(f32[8,64,128]{2,1,0:T(8,128)} %refs_2_.1) | copy-start | bytes 786436
  0.7 2.0 %copy-start.1 = (f32[8,64,128]{2,1,0:T(8,128)S(1)}, f32[8,64,128]{2,1,0:T(8,128)}, u32[]{:S(2)}) copy-start(f32[8,64,128]{2,1,0:T(8,128)} %refs_1_.1) | copy-start | bytes 786436
  0.7 2.0 %copy-start = (f32[8,64,128]{2,1,0:T(8,128)S(1)}, f32[8,64,128]{2,1,0:T(8,128)}, u32[]{:S(2)}) copy-start(f32[8,64,128]{2,1,0:T(8,128)} %refs_0_.1) | copy-start | bytes 786436
  2.8 16.5 %collective-permute-start.16 = (f32[23,64,128]{2,1,0:T(8,128)S(1)}, f32[23,64,128]{2,1,0:T(8,128)S(1)}, u32[]{:S(2)}, u32[]{:S(2)}) collective-permute-start(f32[23,64,128]{2,1,0:T(8,128)S(1)} %get-tuple-element.183), channel_id=1, source_target_pairs={{2,0},{3,1},{4,2},{5,3},{6,4},{7,5},{8,6},{9,7},{10,8},{11,9},{12,... | collective-permute-start | bytes 2261000 | tf_op jit(solution)/shard_map/cond/branch_3_fun/ppermute | solution.py:697
  5.0 6.1 %collective-permute-start.15 = (f32[32,8,128]{2,1,0:T(8,128)S(1)}, f32[32,8,128]{2,1,0:T(8,128)S(1)}, u32[]{:S(2)}, u32[]{:S(2)}) collective-permute-start(f32[32,8,128]{2,1,0:T(8,128)S(1)} %edges.7.refs_8_), channel_id=1, source_target_pairs={{0,1},{1,0},{2,3},{3,2},{4,5},{5,4},{6,7},{7,6},{8,9},{9,8},{10,11... | collective-permute-start | bytes 393224 | tf_op jit(solution)/shard_map/cond/branch_3_fun/ppermute | solution.py:697
  7.7 10.1 %collective-permute-start.17 = (f32[3,64,128]{2,1,0:T(8,128)S(1)}, f32[3,64,128]{2,1,0:T(8,128)S(1)}, u32[]{:S(2)}, u32[]{:S(2)}) collective-permute-start(f32[3,64,128]{2,1,0:T(8,128)S(1)} %lift.7), channel_id=1, source_target_pairs={{0,2},{1,3},{2,4},{3,5},{4,6},{5,7},{6,8},{7,9},{8,10},{9,11},{10,... | collective-permute-start | bytes 294920 | tf_op jit(solution)/shard_map/cond/branch_3_fun/ppermute | solution.py:697
  11.1 6.7 %collective-permute-start.18 = (f32[16,8,128]{2,1,0:T(8,128)S(1)}, f32[16,8,128]{2,1,0:T(8,128)S(1)}, u32[]{:S(2)}, u32[]{:S(2)}) collective-permute-start(f32[16,8,128]{2,1,0:T(8,128)S(1)} %get-tuple-element.184), channel_id=1, source_target_pairs={{0,2},{1,3},{2,0},{3,1},{4,6},{5,7},{6,4},{7,5},{8,10},{9,11},{10,... | collective-permute-start | bytes 196616 | tf_op jit(solution)/shard_map/cond/branch_3_fun/ppermute | solution.py:697
  11.5 7.8 %collective-permute-start.19 = (f32[16,8,128]{2,1,0:T(8,128)S(1)}, f32[16,8,128]{2,1,0:T(8,128)S(1)}, u32[]{:S(2)}, u32[]{:S(2)}) collective-permute-start(f32[16,8,128]{2,1,0:T(8,128)S(1)} %get-tuple-element.185), channel_id=1, source_target_pairs={{2,4},{3,5},{4,2},{5,3},{6,8},{7,9},{8,6},{9,7},{10,12},{11,13},{1... | collective-permute-start | bytes 196616 | tf_op jit(solution)/shard_map/cond/branch_3_fun/ppermute | solution.py:697

commit v8 on v7

--- a/solution.py
+++ b/solution.py
@@ -28,9 +28,14 @@
 
 def up_counts(case):
     moves, now = case
-    below = 3 - moves
     later = moves - now
-    return (below - 1, below - 1, below, below, below, below - 1, 2 - later, 2 - later)
+    if moves == 1:
+        return (0,) * 6 + (2 - later, 1)
+    return (0, 0, 1, 1, 1, 0, 2 - later, 2 - later)
+
+
+def up_traces(case):
+    return (4, 10) if case[0] == 1 else (0, 0)
 
 
 def offsets(counts):
@@ -83,12 +88,49 @@
     return lax.broadcasted_iota(jnp.int32, (TILE, depth), 0) < HALF
 
 
+def tile_of_edges(v):
+    return jnp.where(low_half(v.shape[-1]), turned(v[-TILE:]), turned(v[:TILE]))
+
+
+class Plane:
+    def __init__(self, start, width, depth, total):
+        row = lax.broadcasted_iota(jnp.int32, (width, depth), 0)
+        self.whole, self.half = column_scales(start + row, total)
+        self.one_whole, self.one_half = 1.0 / self.whole, 1.0 / self.half
+        self.step_whole, self.step_half = TIME_STEP * self.one_whole, TIME_STEP * self.one_half
+
+    def add_above(self, bx, by, ex, ey):
+        return bx + self.step_whole * ey, by - self.step_half * ex
+
+    def radial_vertical(self, bx, by, ex, ey, es):
+        weighted = self.whole * es
+        bx = bx - TIME_STEP * (next_y(es) - es) - self.step_whole * ey
+        by = by + self.step_half * (ex + next_x(weighted) - weighted)
+        return bx, by
+
+    def longitudinal(self, bs, ex, ey):
+        return bs - TIME_STEP * ((next_x(ey) - ey) - (next_y(ex) - ex))
+
+    def electric(self, ex, ey, bs, over_x, over_y, factors):
+        kept, gained = factors
+        weighted = self.half * bs
+        ex = kept * ex + gained * ((bs - last_y(bs)) - self.one_half * over_y)
+        ey = kept * ey + gained * (self.one_whole * (over_x - (weighted - last_x(weighted))))
+        return ex, ey
+
+    def electric_s(self, es, bx, by, bunch, factors):
+        current = CURRENT_SCALE * bunch.astype(jnp.float32)
+        return factors[0] * es + factors[1] * ((by - last_x(by)) - (bx - last_y(bx)) - current)
+
+
 def pack_kernel(*refs):
     sources, moved = refs[:8], refs[8]
     which, moved_here = refs[9:11]
     sent = refs[11 : 11 + len(CASES)]
     near, near_int, sems, moved_sem = refs[11 + len(CASES) :]
-    _, count, width, depth = near.shape
+    _, _, width, depth = near.shape
+    most = max(case[0] for case in CASES)
+    fetched = (most + 3,) * 2 + (most + 2,) * 5 + (most + 1,)
     gx = lax.axis_index("gx")
     total = width * lax.axis_size("gx")
 
@@ -96,8 +138,9 @@
     get_moved.start()
     copies = []
     for a in range(8):
-        goal = near.at[a] if a < 6 else near_int.at[a - 6]
-        copies.append(pltpu.make_async_copy(sources[a].at[pl.ds(0, count)], goal, sems.at[a]))
+        span = pl.ds(0, fetched[a])
+        goal = near.at[a, span] if a < 6 else near_int.at[a - 6, span]
+        copies.append(pltpu.make_async_copy(sources[a].at[span], goal, sems.at[a]))
         copies[-1].start()
     get_moved.wait()
     now = moved_here[0]
@@ -105,12 +148,8 @@
     case_index = jnp.where(now + later == 1, 1 - now, 3 - now)
     which[0] = case_index
 
-    row = lax.broadcasted_iota(jnp.int32, (width, depth), 0)
-    whole, half = column_scales(gx * width + row, total)
-    one_whole, one_half = 1.0 / whole, 1.0 / half
-    step_whole, step_half = TIME_STEP * one_whole, TIME_STEP * one_half
-    low = low_half(depth)
-    for item in copies:
+    flat = Plane(gx * width, width, depth, total)
+    for item in copies[:6]:
         item.wait()
 
     for c, case in enumerate(CASES):
@@ -125,62 +164,33 @@
             for a in range(6):
                 down[pl.ds(at[a], far)] = near[a, :far]
 
-            folded = {}
+            folded, now_b = {}, {}
             for plane in range(far - 1, far + 2):
-                folded[BX, plane] = field(BX, plane) + step_whole * field(EY, plane + 1)
-                folded[BY, plane] = field(BY, plane) - step_half * field(EX, plane + 1)
-            down[at[BX] + far - 1] = folded[BX, far - 1]
-            down[at[BY] + far - 1] = folded[BY, far - 1]
-
-            def radial_vertical(bx, by, ex, ey, es):
-                weighted = whole * es
-                bx = bx - TIME_STEP * (next_y(es) - es) - step_whole * ey
-                by = by + step_half * (ex + next_x(weighted) - weighted)
-                return bx, by
-
-            def longitudinal(bs, ex, ey):
-                return bs - TIME_STEP * ((next_x(ey) - ey) - (next_y(ex) - ex))
-
-            def electric(ex, ey, bs, over_x, over_y, factors):
-                kept, gained = factors
-                weighted = half * bs
-                ex = kept * ex + gained * ((bs - last_y(bs)) - one_half * over_y)
-                ey = kept * ey + gained * (one_whole * (over_x - (weighted - last_x(weighted))))
-                return ex, ey
-
-            now_b = {}
-            for plane in range(far - 1, far + 2):
-                now_b[plane] = radial_vertical(
-                    folded[BX, plane],
-                    folded[BY, plane],
-                    field(EX, plane),
-                    field(EY, plane),
-                    field(ES, plane),
-                )
+                above = field(EX, plane + 1), field(EY, plane + 1)
+                folded[plane] = flat.add_above(field(BX, plane), field(BY, plane), *above)
+                fields = field(EX, plane), field(EY, plane), field(ES, plane)
+                now_b[plane] = flat.radial_vertical(*folded[plane], *fields)
+            down[at[BX] + far - 1], down[at[BY] + far - 1] = folded[far - 1]
+            for item in copies[6:]:
+                item.wait()
             now_e, now_s = {}, {}
             for plane in (far, far + 1):
                 ex, ey = field(EX, plane), field(EY, plane)
-                now_s[plane] = longitudinal(field(BS, plane), ex, ey)
+                now_s[plane] = flat.longitudinal(field(BS, plane), ex, ey)
                 factors = coefficients(near_int[0, plane - first_move])
                 over = [up - under for up, under in zip(now_b[plane], now_b[plane - 1])]
-                now_e[plane] = electric(ex, ey, now_s[plane], *over, factors)
+                now_e[plane] = flat.electric(ex, ey, now_s[plane], *over, factors)
                 if plane == far:
-                    bx, by = now_b[far]
-                    current = CURRENT_SCALE * near_int[1, far - first_move].astype(jnp.float32)
-                    es = factors[0] * field(ES, far) + factors[1] * (
-                        (by - last_x(by)) - (bx - last_y(bx)) - current
-                    )
+                    bunch = near_int[1, far - first_move]
+                    es = flat.electric_s(field(ES, far), *now_b[far], bunch, factors)
             place = at[-1]
             down[place], down[place + 1] = now_e[far]
 
-            ex, ey = now_e[far]
-            bx, by = now_b[far]
-            bx, by = radial_vertical(
-                bx + step_whole * now_e[far + 1][1], by - step_half * now_e[far + 1][0], ex, ey, es
-            )
-            bs = longitudinal(now_s[far], ex, ey)
+            bx, by = flat.add_above(*now_b[far], *now_e[far + 1])
+            bx, by = flat.radial_vertical(bx, by, *now_e[far], es)
+            bs = flat.longitudinal(now_s[far], *now_e[far])
             factors = coefficients(near_int[0, far - (first_move + moved_here[1])])
-            down[place + 2], down[place + 3] = electric(ex, ey, bs, bx, by, factors)
+            down[place + 2], down[place + 3] = flat.electric(*now_e[far], bs, bx, by, factors)
 
             place += 4
             for n, a in enumerate((CODES, BUNCH)):
@@ -190,12 +200,11 @@
             tiles = [field(a, far) for a in range(6)]
             tiles.append(near_int[1, far - first_move].astype(jnp.float32))
             tiles += [field(EX, far + 1), field(EY, far + 1), field(ES, far + 1)]
-            tiles += [folded[BX, far + 1], folded[BY, far + 1], field(BS, far + 1)]
+            tiles += [*folded[far + 1], field(BS, far + 1)]
             tiles.append(near_int[0, far + 1 - first_move].astype(jnp.float32))
             for n, v in enumerate(tiles):
-                tile = jnp.where(low, turned(v[width - TILE :]), turned(v[:TILE]))
                 plane, rows = tile_of(down, place, n, width)
-                down[plane, rows] = tile
+                down[plane, rows] = tile_of_edges(v)
 
 
 def pack(arrays, moved):
@@ -204,7 +213,6 @@
     shapes = [pltpu.SMEM((1,), jnp.int32), pltpu.SMEM((STEPS,), jnp.int32)]
     for case in CASES:
         count = sum(down_counts(case)) + 4 + tile_planes(14, width)
-        count += case == (1, 1)
         shapes.append(pltpu.VMEM((count, width, depth), jnp.float32))
     found = pl.pallas_call(
         pack_kernel,
@@ -262,22 +270,44 @@
     own, up = refs[:8], refs[-1]
     planes, width, depth = own[0].shape
     ups = up_counts(case)
-    up_at = offsets(ups)
-    column = lax.broadcasted_iota(jnp.int32, (width, depth), 0)
-    whole, half = column_scales(lax.axis_index("gx") * width + column, width * lax.axis_size("gx"))
-    bottom = planes - (3 - case[0])
+    traces, n_tiles = up_traces(case)
+    at = [traces + n for n in offsets(ups)]
+    flat = Plane(lax.axis_index("gx") * width, width, depth, width * lax.axis_size("gx"))
     for a in range(8):
         if ups[a]:
-            up[pl.ds(up_at[a], ups[a])] = own[a][planes - ups[a] :].astype(jnp.float32)
-    up[up_at[BX]] = own[BX][bottom] - (TIME_STEP / whole) * own[EY][bottom]
-    up[up_at[BY]] = own[BY][bottom] + (TIME_STEP / half) * own[EX][bottom]
+            up[pl.ds(at[a], ups[a])] = own[a][planes - ups[a] :].astype(jnp.float32)
+    bottom = planes - (3 - case[0])
+    ex, ey, es, bx, by, bs = (own[a][bottom] for a in range(6))
+    under = flat.add_above(bx, by, -ex, -ey)
+    if not traces:
+        up[at[BX]], up[at[BY]] = under
+        return
+    edge = [es, *under]
+    fields = [own[a][bottom + 1] for a in range(6)]
+    edge += fields
+    below_x, below_y = flat.radial_vertical(*flat.add_above(bx, by, *fields[:2]), ex, ey, es)
+    ex, ey, es, bx, by, bs = fields
+    bx, by = flat.radial_vertical(bx, by, ex, ey, es)
+    bs = flat.longitudinal(bs, ex, ey)
+    up[0], up[1] = bx, by
+    factors = coefficients(own[CODES][planes - 1 - case[1]])
+    bunch = own[BUNCH][planes - 1 - case[1]]
+    ex, ey = flat.electric(ex, ey, bs, bx - below_x, by - below_y, factors)
+    es = flat.electric_s(es, bx, by, bunch, factors)
+    up[2], up[3] = flat.radial_vertical(bx, by, ex, ey, es)
+    edge.append(bunch.astype(jnp.float32))
+    for n, v in enumerate(edge):
+        plane, rows = tile_of(up, at[-1], n, width)
+        up[plane, rows] = tile_of_edges(v)
 
 
 def lift(case, own, after):
     planes, width, depth = own[0].shape
+    traces, n_tiles = up_traces(case)
+    count = sum(up_counts(case)) + traces + tile_planes(n_tiles, width)
     return pl.pallas_call(
         functools.partial(lift_kernel, case),
-        out_shape=pltpu.VMEM((sum(up_counts(case)), width, depth), jnp.float32),
+        out_shape=pltpu.VMEM((count, width, depth), jnp.float32),
         in_specs=[VMEM] * 8 + [ANY] * len(after),
         out_specs=VMEM,
         compiler_params=pltpu.CompilerParams(vmem_limit_bytes=32 * 2**20),
@@ -488,7 +518,7 @@
         in_specs=[SMEM] + [VMEM] * (8 + len(beside)),
         out_specs=[VMEM] * len(shapes),
         compiler_params=pltpu.CompilerParams(vmem_limit_bytes=32 * 2**20),
-        cost_estimate=pl.CostEstimate(flops=32 * 10**8, bytes_accessed=10**7, transcendentals=0),
+        cost_estimate=pl.CostEstimate(flops=27 * 10**8, bytes_accessed=10**7, transcendentals=0),
         name="prepare",
     )(moved, *own, *beside)
 
@@ -507,7 +537,8 @@
     last = lax.axis_index("gz") == lax.axis_size("gz") - 1
     even = lax.axis_index("gz") % 2 == 0
     downs, ups = down_counts(case), up_counts(case)
-    at, up_at = offsets(downs[:6]), offsets(ups)
+    traces, _ = up_traces(case)
+    at, up_at = offsets(downs[:6]), [traces + n for n in offsets(ups)]
     far_at = at[-1]
     at = at[:6] + [far_at + 4, far_at + 4 + downs[CODES]]
     tiles_at = at[BUNCH] + downs[BUNCH]
@@ -551,11 +582,11 @@
     def kept_blocks(ref, *plane):
         return blocks(*(turned(ref[(*plane, where)]) for where in (right, ghost, left)))
 
-    def sent_blocks(a, n, plane):
-        where, here = tile_of(down, tiles_at, n, width)
-        tile = down[where, here]
-        beyond = jnp.where(cells.ghost_in[0], from_above(a, plane, 1)[0], 0.0)
-        return tile, beyond
+    def sent_blocks(a, n, plane, above=True):
+        message, start = (down, tiles_at) if above else (up, up_at[-1])
+        where, here = tile_of(message, start, n, width)
+        ghosts = corner(a, plane, 1, moves + 2 if above else base, above)[0]
+        return message[where, here], jnp.where(cells.ghost_in[0], ghosts, 0.0)
 
     def both(tiles):
         return blocks(tiles[0], turned(tiles[1]), tiles[0])
@@ -581,18 +612,59 @@
         ey = kept * ey + gained * (row[2] * ((bx - below[0]) - (weighted - last_x(weighted))))
         return ex, ey
 
+    def block_electric_s(fields, bunch, factors):
+        bx, by = fields[3:5]
+        return factors[0] * fields[2] + factors[1] * (
+            (by - last_x(by)) - (bx - last_y(bx)) - CURRENT_SCALE * bunch
+        )
+
     tile_row = lax.broadcasted_iota(jnp.int32, (TILE, cells.depth), 0)
 
-    def set_far(values, found, edge):
+    def with_edges(value, right_block, left_block):
+        at_right = jnp.where(tile_row >= TILE - 2, turned(right_block), value[width - TILE :])
+        at_left = jnp.where(tile_row < 2, turned(left_block), value[:TILE])
+        beyond = turned(jnp.where(low, left_block, right_block))
+        return jnp.concatenate([at_left, value[TILE : width - TILE], at_right, beyond], 0)
+
+    def set_far(values, found):
         for a in (EX, EY):
-            right_block, left_block = found[0][a], found[1][a]
-            ext[a][far, pl.ds(0, width)] = jnp.where(last, 0.0, values[a])
-            at_right = jnp.where(tile_row >= TILE - edge, turned(right_block), values[a][width - TILE :])
-            at_left = jnp.where(tile_row < edge, turned(left_block), values[a][:TILE])
-            ext[a][far, right] = jnp.where(last, 0.0, at_right)
-            ext[a][far, left] = jnp.where(last, 0.0, at_left)
-            beyond = turned(jnp.where(low, left_block, right_block))
-            ext[a][far, ghost] = jnp.where(last, 0.0, beyond)
+            value = with_edges(values[a], found[0][a], found[1][a])
+            ext[a][far] = jnp.where(last, 0.0, value)
+
+    def below_first(moved_now):
+        es_under, bx_under, by_under = (
+            both(sent_blocks(a, n, 0, False)) for n, a in enumerate((ES, BX, BY))
+        )
+        raw = [both(sent_blocks(a, 3 + a, 1, False)) for a in range(6)]
+        bunch = both(sent_blocks(BUNCH, 9, 1 - case[1], False))
+        own = [kept_blocks(ref, 1 - moved_now) for ref in (cells.keep, cells.gain)]
+        found = []
+        for b in range(2):
+            fields, factors = [v[b] for v in raw], [v[b] for v in own]
+            zero = jnp.zeros_like(fields[0])
+            under = (zero, zero, es_under[b], bx_under[b], by_under[b], zero)
+            under = block_magnetic(under, fields[:2], b)[3:5]
+            fields = block_magnetic(fields, None, b)
+            first_b = fields[3:5]
+            es = block_electric_s(fields, bunch[b], factors)
+            ex, ey = block_electric(fields, under, factors, b)
+            found.append((first_b, block_magnetic((ex, ey, es, *fields[3:]), None, b)[3:5]))
+        once = [with_edges(up[n], found[0][0][n], found[1][0][n]) for n in range(2)]
+        twice = [with_edges(up[2 + n], found[0][1][n], found[1][1][n]) for n in range(2)]
+
+        bx, by = rows[5] * ext[EY][base], -rows[6] * ext[EX][base]
+        gained = cells.gain[1 - moved_now]
+        ex, ey = -gained * (rows[3] * by), gained * (rows[2] * bx)
+        es = gained * ((by - last_x(by)) - (bx - last_y(bx)))
+        weighted = rows[0] * es
+        ext[BX][1], ext[BY][1] = once[0] + bx, once[1] + by
+        bx = bx - rows[4] * (next_y(es) - es) - rows[5] * ey
+        by = by + rows[6] * (ex + next_x(weighted) - weighted)
+        return twice[0] + bx, twice[1] + by
+
+    def below_second(state):
+        ext[BX][1] = state[0] + rows[5] * ext[EY][base]
+        ext[BY][1] = state[1] - rows[6] * ext[EX][base]
 
     def far_first(moved_now):
         planes_raw = [[both(sent_blocks(a, n * 7 + a, moves + n)) for a in range(6)] for n in range(2)]
@@ -609,12 +681,9 @@
             factors = [v[b] for v in own]
             ex, ey = block_electric(mine, [v[b] for v in below], factors, b)
             ex_over, ey_over = block_electric(theirs, mine[3:5], [v[b] for v in over], b)
-            bx, by = mine[3:5]
-            es = factors[0] * mine[2] + factors[1] * (
-                (by - last_x(by)) - (bx - last_y(bx)) - CURRENT_SCALE * bunch[b]
-            )
+            es = block_electric_s(mine, bunch[b], factors)
             state.append(((ex, ey, es, *mine[3:]), (ex_over, ey_over)))
-        set_far([down[far_at], down[far_at + 1]], [fields[:2] for fields, _ in state], 1)
+        set_far([down[far_at], down[far_at + 1]], [fields[:2] for fields, _ in state])
         return state
 
     def far_second(state, moved_now):
@@ -627,15 +696,25 @@
         gained = cells.gain[far - moved_now, mine]
         ex = down[far_at + 2] + gained * (rows[3, mine] * ext[BY][far - 1, mine])
         ey = down[far_at + 3] - gained * (rows[2, mine] * ext[BX][far - 1, mine])
-        set_far([ex, ey], found, 2)
+        set_far([ex, ey], found)
 
     mine = pl.ds(0, width)
     moved_now = 0
     for t in range(STEPS):
         moved_now = moved_now + moved[t]
         above = moves + 1 + t
-        cells.magnetic(t, base)
+        if moves == 1:
+            count, lowest = min(t, 2), 2
+            count_e, lowest_e = min(t + 1, 2), max(t + 1, 2)
+        else:
+            count, lowest, count_e, lowest_e = base, t, base, t + 1
+        if moves == 1 and t == 0:
+            below_state = below_first(moved_now)
+        if count:
+            cells.magnetic(lowest, count)
         cells.magnetic(top - t, above)
+        if moves == 1 and t == 1:
+            below_second(below_state)
 
         @pl.when(first)
         def _():
@@ -645,19 +724,22 @@
             for a in (BX, BY, BS):
                 send(a, 3, base + 2)
                 send(a, top - 2, planes + 3)
-        cells.electric(t + 1, base, moved_now)
-        if t == STEPS - 1:
+        cells.electric(lowest_e, count_e, moved_now)
+        if t < STEPS - 1:
+            cells.electric(top - t, above, moved_now)
+        else:
             for a in (EX, EY, ES):
                 send(a, 3, base + 3)
-        cells.electric(top - t, above, moved_now)
+            cut = above // 2
+            for start, end in ((top - 2, top - 2 + cut), (top - 2 + cut, planes + 3)):
+                cells.electric(start, end - start, moved_now)
+                for a in (EX, EY, ES):
+                    send(a, start, end)
         if t == 0:
             edge_state = far_first(moved_now)
         elif t == 1:
             far_second(edge_state, moved_now)
-        if t == STEPS - 1:
-            for a in (EX, EY, ES):
-                send(a, top - 2, planes + 3)
-        else:
+        if t < STEPS - 1:
 
             @pl.when(last)
             def _():
@@ -678,7 +760,7 @@
         in_specs=[SMEM] + [VMEM] * (n_in - 1),
         out_specs=[ANY] * 6 + [VMEM] * 9,
         input_output_aliases={1 + n: 6 + n for n in range(9)},
-        scratch_shapes=[pltpu.SemaphoreType.DMA((18,))],
+        scratch_shapes=[pltpu.SemaphoreType.DMA((21,))],
         compiler_params=pltpu.CompilerParams(vmem_limit_bytes=32 * 2**20),
         name="steps",
     )(moved, *ready, *ghosts)

time: 22.1 us -> 20.7 us (0.937)
  the two profiles are of different devices: /device:TPU:1 before, /device:TPU:5 now
where the time goes in v8:
time: 20.7 us; the launch traced here: 20.5 us
  starting transfers between devices  11.4 us (55%)
  Pallas kernels  6.14 us (30%)
  waiting for transfers between devices  1.66 us (8%)
  between operations  0.96 us (5%)
  loops' own time  0.32 us (2%)
    ppermute x5, starting transfers between devices, passed(): return lax.ppermute(block, ('gz', 'gx'), route)  11.4 us
    pallas_call x1, Pallas kernels, advance(): pl.pallas_call(functools.partial(steps_kernel, case, n_sides, planes, wid...  2.38 us
    pallas_call x1, Pallas kernels, pack(): pl.pallas_call(pack_kernel, out_shape=shapes, in_specs=[ANY] * 9, out_spe...  1.86 us
    ppermute x5, waiting for transfers between devices, passed(): return lax.ppermute(block, ('gz', 'gx'), route)  1.66 us
    pallas_call x1, Pallas kernels, prepare(): pl.pallas_call(functools.partial(prepare_kernel, moves, len(beside)), out...  1.57 us
  transfers between devices with their start and end apart: 5, of which 1 were waited for; matrix products, arithmetic and copies ran while one was open for 0% of the time, Pallas kernels for 9%

profile of v8, /device:TPU:5, one launch (start us, length us, event | category | flops | bytes accessed | tf_op | source)
XLA Modules:
  0.0 20.5 jit_solution(12240286471163083947)
XLA Ops:
  0.6 0.0 copy-start.6
  0.7 1.9 %pack.1 = (s32[1]{0:T(128)S(4)}, s32[3]{0:T(128)S(4)}, f32[13,64,128]{2,1,0:T(8,128)S(1)}, f32[15,64,128]{2,1,0:T(8,128)S(1)}, f32[21,64,128]{2,1,0:T(8,128)S(1)}, /*index=5*/f32[23,64,128]{2,1,0:T(8,128)S(1)}) custom-call(f32[8,64,128]{2,1,0:T(8,128)} %refs_0_.1, f32[8,64,128]{2,1,0:T(8,128)} %refs_1_.1, f32[8,64,128]{2,1,0:T(8,128)} %refs_2_.1, ...), custom_call_target="tpu_custom_call" | custom-call | tf_op jit(solution)/shard_map/pack/pallas_call | solution.py:217
  2.6 0.0 copy-done.6
  2.6 0.0 copy-done.7
  2.6 0.0 copy-done.5
  2.6 0.0 copy-done.4
  2.6 0.0 copy-done.3
  2.6 0.0 copy-done.2
  2.6 0.0 copy-done.1
  2.7 0.0 copy-done
  2.7 17.7 %conditional.1 = (f32[8,64,128]{2,1,0:T(8,128)}, f32[8,64,128]{2,1,0:T(8,128)}, f32[8,64,128]{2,1,0:T(8,128)}, f32[8,64,128]{2,1,0:T(8,128)}, f32[8,64,128]{2,1,0:T(8,128)}, /*index=5*/f32[8,64,128]{2,1,0:T(8,128)}) conditional(s32[]{:T(128)} %bitcast, (f32[8,64,128]{2,1,0:T(8,128)S(1)}, f32[8,64,128]{2,1,0:T(8,128)S(1)}, ...), branch_computations={%region_0.0_spmd, %region_1.0_spmd, %region_2.0_spmd, %region_3.0_... | conditional | flops 2710000128 | bytes 24456696 | solution.py:800
  2.7 2.6 %collective-permute-start.6 = (f32[15,64,128]{2,1,0:T(8,128)S(1)}, f32[15,64,128]{2,1,0:T(8,128)S(1)}, u32[]{:S(2)}, u32[]{:S(2)}) collective-permute-start(f32[15,64,128]{2,1,0:T(8,128)S(1)} %get-tuple-element.127), channel_id=1, source_target_pairs={{2,0},{3,1},{4,2},{5,3},{6,4},{7,5},{8,6},{9,7},{10,8},{11,9},{12,... | collective-permute-start | bytes 1474568 | tf_op jit(solution)/shard_map/cond/branch_1_fun/ppermute | solution.py:779
  5.3 1.3 %collective-permute-start.5 = (f32[32,8,128]{2,1,0:T(8,128)S(1)}, f32[32,8,128]{2,1,0:T(8,128)S(1)}, u32[]{:S(2)}, u32[]{:S(2)}) collective-permute-start(f32[32,8,128]{2,1,0:T(8,128)S(1)} %edges.5.refs_8_), channel_id=1, source_target_pairs={{0,1},{1,0},{2,3},{3,2},{4,5},{5,4},{6,7},{7,6},{8,9},{9,8},{10,11... | collective-permute-start | bytes 393224 | tf_op jit(solution)/shard_map/cond/branch_1_fun/ppermute | solution.py:779
  6.6 0.2 %lift.5 = f32[8,64,128]{2,1,0:T(8,128)S(1)} custom-call(f32[8,64,128]{2,1,0:T(8,128)S(1)} %get-tuple-element.109.refs_0_, f32[8,64,128]{2,1,0:T(8,128)S(1)} %get-tuple-element.110.refs_1_, f32[8,64,128]{2,1,0:T(8,128)S(1)} %get-tuple-element.111.refs_2_, f32[8,64,128]{2,1,0:T(8,128)S(1)} %get-tuple-element.112.refs_3_, ...), custom_call_target="tpu_custom_call" | custom-call | flops 10000000 | bytes 10000000 | tf_op jit(solution)/shard_map/cond/branch_1_fun/lift/pallas_call | solution.py:308
  6.8 4.2 %collective-permute-start.7 = (f32[8,64,128]{2,1,0:T(8,128)S(1)}, f32[8,64,128]{2,1,0:T(8,128)S(1)}, u32[]{:S(2)}, u32[]{:S(2)}) collective-permute-start(f32[8,64,128]{2,1,0:T(8,128)S(1)} %lift.5), channel_id=1, source_target_pairs={{0,2},{1,3},{2,4},{3,5},{4,6},{5,7},{6,8},{7,9},{8,10},{9,11},{10,... | collective-permute-start | bytes 786440 | tf_op jit(solution)/shard_map/cond/branch_1_fun/ppermute | solution.py:779
  11.0 0.0 collective-permute-done.5.refs_8_.refs_0_
  11.1 0.3 %collective-permute-start.8 = (f32[12,8,128]{2,1,0:T(8,128)S(1)}, f32[12,8,128]{2,1,0:T(8,128)S(1)}, u32[]{:S(2)}, u32[]{:S(2)}) collective-permute-start(f32[12,8,128]{2,1,0:T(8,128)S(1)} %get-tuple-element.128), channel_id=1, source_target_pairs={{0,2},{1,3},{2,0},{3,1},{4,6},{5,7},{6,4},{7,5},{8,10},{9,11},{10,... | collective-permute-start | bytes 147464 | tf_op jit(solution)/shard_map/cond/branch_1_fun/ppermute | solution.py:779
  11.4 3.0 %collective-permute-start.9 = (f32[12,8,128]{2,1,0:T(8,128)S(1)}, f32[12,8,128]{2,1,0:T(8,128)S(1)}, u32[]{:S(2)}, u32[]{:S(2)}) collective-permute-start(f32[12,8,128]{2,1,0:T(8,128)S(1)} %get-tuple-element.129), channel_id=1, source_target_pairs={{2,4},{3,5},{4,2},{5,3},{6,8},{7,9},{8,6},{9,7},{10,12},{11,13},{1... | collective-permute-start | bytes 147464 | tf_op jit(solution)/shard_map/cond/branch_1_fun/ppermute | solution.py:779
  14.5 1.6 %prepare.5 = (f32[12,72,128]{2,1,0:T(8,128)S(1)}, f32[12,72,128]{2,1,0:T(8,128)S(1)}, f32[12,72,128]{2,1,0:T(8,128)S(1)}, f32[12,72,128]{2,1,0:T(8,128)S(1)}, f3...) custom-call(s32[3]{0:T(128)S(4)} %get-tuple-element.108.moved, ...), custom_call_target="tpu_custom_call" | custom-call | flops 2700000000 | bytes 10000000 | tf_op jit(solution)/shard_map/cond/branch_1_fun/prepare/pallas_call | solution.py:515
  16.0 0.0 collective-permute-done.8.refs_12_
  16.1 1.6 %collective-permute-done.9.refs_13_ = f32[12,8,128]{2,1,0:T(8,128)S(1)} collective-permute-done((f32[12,8,128]{2,1,0:T(8,128)S(1)}, f32[12,8,128]{2,1,0:T(8,128)S(1)}, u32[]{:S(2)}, u32[]{:S(2)}) %collective-permute-start.9) | collective-permute-done | bytes 49184 | tf_op jit(solution)/shard_map/cond/branch_1_fun/ppermute | solution.py:779
  17.7 0.0 collective-permute-done.7.refs_11_
  17.7 0.0 collective-permute-done.6.refs_10_
  17.7 2.4 %steps.5 = (f32[8,64,128]{2,1,0:T(8,128)}, f32[8,64,128]{2,1,0:T(8,128)}, f32[8,64,128]{2,1,0:T(8,128)}, f32[8,64,128]{2,1,0:T(8,128)}, f32[8,64,128]{2,1,0:T(8,...) custom-call(s32[3]{0:T(128)S(4)} %get-tuple-element.108.moved, ...), custom_call_target="tpu_custom_call", output_to_operand_aliasing={{6}: (1, {}), {7}: (2, {}), {8}: (3, {}), {9}: (4, {}), {10... | custom-call | tf_op jit(solution)/shard_map/cond/branch_1_fun/steps/pallas_call | solution.py:757
  (9 shorter events, 0.1 us)
Async XLA Ops:
  0.6 2.0 %copy-start.6 = (s32[8,64,128]{2,1,0:T(8,128)S(1)}, s32[8,64,128]{2,1,0:T(8,128)}, u32[]{:S(2)}) copy-start(s32[8,64,128]{2,1,0:T(8,128)} %refs_6_.1) | copy-start | bytes 786436
  0.6 2.0 %copy-start.7 = (s32[8,64,128]{2,1,0:T(8,128)S(1)}, s32[8,64,128]{2,1,0:T(8,128)}, u32[]{:S(2)}) copy-start(s32[8,64,128]{2,1,0:T(8,128)} %refs_7_.1) | copy-start | bytes 786436
  0.7 2.0 %copy-start.5 = (f32[8,64,128]{2,1,0:T(8,128)S(1)}, f32[8,64,128]{2,1,0:T(8,128)}, u32[]{:S(2)}) copy-start(f32[8,64,128]{2,1,0:T(8,128)} %refs_5_.1) | copy-start | bytes 786436
  0.7 2.0 %copy-start.4 = (f32[8,64,128]{2,1,0:T(8,128)S(1)}, f32[8,64,128]{2,1,0:T(8,128)}, u32[]{:S(2)}) copy-start(f32[8,64,128]{2,1,0:T(8,128)} %refs_4_.1) | copy-start | bytes 786436
  0.7 2.0 %copy-start.3 = (f32[8,64,128]{2,1,0:T(8,128)S(1)}, f32[8,64,128]{2,1,0:T(8,128)}, u32[]{:S(2)}) copy-start(f32[8,64,128]{2,1,0:T(8,128)} %refs_3_.1) | copy-start | bytes 786436
  0.7 2.0 %copy-start.2 = (f32[8,64,128]{2,1,0:T(8,128)S(1)}, f32[8,64,128]{2,1,0:T(8,128)}, u32[]{:S(2)}) copy-start(f32[8,64,128]{2,1,0:T(8,128)} %refs_2_.1) | copy-start | bytes 786436
  0.7 2.0 %copy-start.1 = (f32[8,64,128]{2,1,0:T(8,128)S(1)}, f32[8,64,128]{2,1,0:T(8,128)}, u32[]{:S(2)}) copy-start(f32[8,64,128]{2,1,0:T(8,128)} %refs_1_.1) | copy-start | bytes 786436
  0.7 2.0 %copy-start = (f32[8,64,128]{2,1,0:T(8,128)S(1)}, f32[8,64,128]{2,1,0:T(8,128)}, u32[]{:S(2)}) copy-start(f32[8,64,128]{2,1,0:T(8,128)} %refs_0_.1) | copy-start | bytes 786436
  2.7 15.0 %collective-permute-start.6 = (f32[15,64,128]{2,1,0:T(8,128)S(1)}, f32[15,64,128]{2,1,0:T(8,128)S(1)}, u32[]{:S(2)}, u32[]{:S(2)}) collective-permute-start(f32[15,64,128]{2,1,0:T(8,128)S(1)} %get-tuple-element.127), channel_id=1, source_target_pairs={{2,0},{3,1},{4,2},{5,3},{6,4},{7,5},{8,6},{9,7},{10,8},{11,9},{12,... | collective-permute-start | bytes 1474568 | tf_op jit(solution)/shard_map/cond/branch_1_fun/ppermute | solution.py:779
  5.3 5.7 %collective-permute-start.5 = (f32[32,8,128]{2,1,0:T(8,128)S(1)}, f32[32,8,128]{2,1,0:T(8,128)S(1)}, u32[]{:S(2)}, u32[]{:S(2)}) collective-permute-start(f32[32,8,128]{2,1,0:T(8,128)S(1)} %edges.5.refs_8_), channel_id=1, source_target_pairs={{0,1},{1,0},{2,3},{3,2},{4,5},{5,4},{6,7},{7,6},{8,9},{9,8},{10,11... | collective-permute-start | bytes 393224 | tf_op jit(solution)/shard_map/cond/branch_1_fun/ppermute | solution.py:779
  6.8 10.9 %collective-permute-start.7 = (f32[8,64,128]{2,1,0:T(8,128)S(1)}, f32[8,64,128]{2,1,0:T(8,128)S(1)}, u32[]{:S(2)}, u32[]{:S(2)}) collective-permute-start(f32[8,64,128]{2,1,0:T(8,128)S(1)} %lift.5), channel_id=1, source_target_pairs={{0,2},{1,3},{2,4},{3,5},{4,6},{5,7},{6,8},{7,9},{8,10},{9,11},{10,... | collective-permute-start | bytes 786440 | tf_op jit(solution)/shard_map/cond/branch_1_fun/ppermute | solution.py:779
  11.1 5.0 %collective-permute-start.8 = (f32[12,8,128]{2,1,0:T(8,128)S(1)}, f32[12,8,128]{2,1,0:T(8,128)S(1)}, u32[]{:S(2)}, u32[]{:S(2)}) collective-permute-start(f32[12,8,128]{2,1,0:T(8,128)S(1)} %get-tuple-element.128), channel_id=1, source_target_pairs={{0,2},{1,3},{2,0},{3,1},{4,6},{5,7},{6,4},{7,5},{8,10},{9,11},{10,... | collective-permute-start | bytes 147464 | tf_op jit(solution)/shard_map/cond/branch_1_fun/ppermute | solution.py:779
  11.4 6.3 %collective-permute-start.9 = (f32[12,8,128]{2,1,0:T(8,128)S(1)}, f32[12,8,128]{2,1,0:T(8,128)S(1)}, u32[]{:S(2)}, u32[]{:S(2)}) collective-permute-start(f32[12,8,128]{2,1,0:T(8,128)S(1)} %get-tuple-element.129), channel_id=1, source_target_pairs={{2,4},{3,5},{4,2},{5,3},{6,8},{7,9},{8,6},{9,7},{10,12},{11,13},{1... | collective-permute-start | bytes 147464 | tf_op jit(solution)/shard_map/cond/branch_1_fun/ppermute | solution.py:779

commit v9 on v8

v9 whole, which is shorter than its diff:
```python
import functools

import jax
import jax.numpy as jnp
from jax import lax
from jax.experimental import pallas as pl
from jax.experimental.pallas import tpu as pltpu
from jax.sharding import PartitionSpec as P

STEPS = 3
TILE = 8
HALF = 4
GROUP = 4
TIME_STEP = 0.5
CURRENT_SCALE = 0.1
VMEM = pl.BlockSpec(memory_space=pltpu.VMEM)
SMEM = pl.BlockSpec(memory_space=pltpu.SMEM)
ANY = pl.BlockSpec(memory_space=pl.ANY)
EX, EY, ES, BX, BY, BS, CODES, BUNCH = range(8)
CASES = ((1, 1), (1, 0), (2, 1), (2, 0))


def down_counts(case):
    moves, now = case
    later = moves - now
    return (moves,) * 6 + (later + 1, later)


def up_counts(case):
    moves, now = case
    later = moves - now
    return (0,) * 6 + (2 - later, 1 if moves == 1 else 2 - later)


def up_traces(case):
    return 4 if case[0] == 1 else 2


def offsets(counts):
    starts = [0]
    for count in counts:
        starts.append(starts[-1] + count)
    return starts


def column_scales(place, total):
    place = place.astype(jnp.float32)
    whole = 1.0 + (place - total / 2) / (2 * total)
    half = 1.0 + (place + 0.5 - total / 2) / (2 * total)
    return whole, half


def turned(tiles):
    return pltpu.roll(tiles, HALF, tiles.ndim - 2)


def next_y(v):
    depth = v.shape[-1]
    lane = lax.broadcasted_iota(jnp.int32, v.shape[-2:], 1)
    return jnp.where(lane < depth - 1, pltpu.roll(v, depth - 1, v.ndim - 1), 0.0)


def last_y(v):
    lane = lax.broadcasted_iota(jnp.int32, v.shape[-2:], 1)
    return jnp.where(lane > 0, pltpu.roll(v, 1, v.ndim - 1), 0.0)


def next_x(v):
    return pltpu.roll(v, v.shape[-2] - 1, v.ndim - 2)


def last_x(v):
    return pltpu.roll(v, 1, v.ndim - 2)


def low_half(depth):
    return lax.broadcasted_iota(jnp.int32, (TILE, depth), 0) < HALF


class Plane:
    def __init__(self, start, width, depth, total, masked=False):
        column = start + lax.broadcasted_iota(jnp.int32, (width, depth), 0)
        self.inside = (column >= 0) & (column < total) if masked else None
        self.whole, self.half = column_scales(column, total)
        self.one_whole, self.one_half = 1.0 / self.whole, 1.0 / self.half
        self.step_whole, self.step_half = TIME_STEP * self.one_whole, TIME_STEP * self.one_half

    def kept(self, *values):
        if self.inside is None:
            return values
        return tuple(jnp.where(self.inside, v, 0.0) for v in values)

    def add_above(self, bx, by, ex, ey):
        return bx + self.step_whole * ey, by - self.step_half * ex

    def radial_vertical(self, bx, by, ex, ey, es):
        weighted = self.whole * es
        bx = bx - TIME_STEP * (next_y(es) - es) - self.step_whole * ey
        by = by + self.step_half * (ex + next_x(weighted) - weighted)
        return self.kept(bx, by)

    def longitudinal(self, bs, ex, ey):
        return self.kept(bs - TIME_STEP * ((next_x(ey) - ey) - (next_y(ex) - ex)))[0]

    def electric(self, ex, ey, bs, over_x, over_y, factors):
        kept, gained = factors
        weighted = self.half * bs
        ex = kept * ex + gained * ((bs - last_y(bs)) - self.one_half * over_y)
        ey = kept * ey + gained * (self.one_whole * (over_x - (weighted - last_x(weighted))))
        return self.kept(ex, ey)

    def electric_s(self, es, bx, by, bunch, factors):
        current = CURRENT_SCALE * bunch.astype(jnp.float32)
        es = factors[0] * es + factors[1] * ((by - last_x(by)) - (bx - last_y(bx)) - current)
        return self.kept(es)[0]


def far_traces(flat, case, second_move, field, code, bunch, codes_ready=lambda: None):
    far, first_move = case
    folded, now_b = {}, {}
    for plane in range(far - 1, far + 2):
        above = field(EX, plane + 1), field(EY, plane + 1)
        folded[plane] = flat.add_above(field(BX, plane), field(BY, plane), *above)
        fields = field(EX, plane), field(EY, plane), field(ES, plane)
        now_b[plane] = flat.radial_vertical(*folded[plane], *fields)
    codes_ready()
    now_e, now_s = {}, {}
    for plane in (far, far + 1):
        ex, ey = field(EX, plane), field(EY, plane)
        now_s[plane] = flat.longitudinal(field(BS, plane), ex, ey)
        factors = coefficients(code(plane - first_move))
        over = [up - under for up, under in zip(now_b[plane], now_b[plane - 1])]
        now_e[plane] = flat.electric(ex, ey, now_s[plane], *over, factors)
        if plane == far:
            es = flat.electric_s(field(ES, far), *now_b[far], bunch(far - first_move), factors)
    bx, by = flat.add_above(*now_b[far], *now_e[far + 1])
    bx, by = flat.radial_vertical(bx, by, *now_e[far], es)
    bs = flat.longitudinal(now_s[far], *now_e[far])
    factors = coefficients(code(far - first_move - second_move))
    return folded[far - 1], (*now_e[far], *flat.electric(*now_e[far], bs, bx, by, factors))


def near_traces(flat, case, planes, field, code, bunch):
    top = planes - 1
    ex, ey, es, bx, by, bs = (field(a, top) for a in range(6))
    first = flat.radial_vertical(bx, by, ex, ey, es)
    if case[0] == 2:
        return first
    under = flat.add_above(field(BX, top - 1), field(BY, top - 1), ex, ey)
    under = flat.radial_vertical(*under, *(field(a, top - 1) for a in (EX, EY, ES)))
    bs = flat.longitudinal(bs, ex, ey)
    factors = coefficients(code(top - case[1]))
    ex, ey = flat.electric(ex, ey, bs, first[0] - under[0], first[1] - under[1], factors)
    es = flat.electric_s(es, *first, bunch(top - case[1]), factors)
    return (*first, *flat.radial_vertical(*first, ex, ey, es))


def pack_kernel(*refs):
    sources, moved = refs[:8], refs[8]
    which, moved_here = refs[9:11]
    sent = refs[11 : 11 + len(CASES)]
    near, near_int, sems, moved_sem = refs[11 + len(CASES) :]
    _, _, width, depth = near.shape
    most = max(case[0] for case in CASES)
    fetched = (most + 3,) * 2 + (most + 2,) * 5 + (most + 1,)
    gx = lax.axis_index("gx")
    total = width * lax.axis_size("gx")

    get_moved = pltpu.make_async_copy(moved, moved_here, moved_sem)
    get_moved.start()
    copies = []
    for a in range(8):
        span = pl.ds(0, fetched[a])
        goal = near.at[a, span] if a < 6 else near_int.at[a - 6, span]
        copies.append(pltpu.make_async_copy(sources[a].at[span], goal, sems.at[a]))
        copies[-1].start()
    get_moved.wait()
    now = moved_here[0]
    later = moved_here[1] + moved_here[2]
    case_index = jnp.where(now + later == 1, 1 - now, 3 - now)
    which[0] = case_index

    flat = Plane(gx * width, width, depth, total)
    for item in copies[:6]:
        item.wait()

    for c, case in enumerate(CASES):
        down = sent[c]
        downs = down_counts(case)
        at = offsets(downs[:6])
        far = case[0]

        @pl.when(case_index == c)
        def _():
            field = lambda a, plane: near[a, plane]
            for a in range(6):
                down[pl.ds(at[a], far)] = near[a, :far]

            folded, traces = far_traces(
                flat,
                case,
                moved_here[1],
                field,
                lambda plane: near_int[0, plane],
                lambda plane: near_int[1, plane],
                lambda: [item.wait() for item in copies[6:]],
            )
            down[at[BX] + far - 1], down[at[BY] + far - 1] = folded
            place = at[-1]
            for v in traces:
                down[place] = v
                place += 1
            for n, a in enumerate((CODES, BUNCH)):
                if downs[a]:
                    down[pl.ds(place, downs[a])] = near_int[n, : downs[a]].astype(jnp.float32)
                place += downs[a]


def pack(arrays, moved):
    planes, width, depth = arrays[0].shape
    near = max(case[0] for case in CASES) + 3
    shapes = [pltpu.SMEM((1,), jnp.int32), pltpu.SMEM((STEPS,), jnp.int32)]
    for case in CASES:
        count = sum(down_counts(case)) + 4
        shapes.append(pltpu.VMEM((count, width, depth), jnp.float32))
    found = pl.pallas_call(
        pack_kernel,
        out_shape=shapes,
        in_specs=[ANY] * 9,
        out_specs=[SMEM] * 2 + [VMEM] * len(CASES),
        scratch_shapes=[
            pltpu.VMEM((6, near, width, depth), jnp.float32),
            pltpu.VMEM((2, near, width, depth), jnp.int32),
            pltpu.SemaphoreType.DMA((8,)),
            pltpu.SemaphoreType.DMA,
        ],
        compiler_params=pltpu.CompilerParams(vmem_limit_bytes=32 * 2**20),
        name="pack",
    )(*(pltpu.with_memory_space_constraint(a, pltpu.HBM) for a in (*arrays, moved)))
    return found[0], found[1], found[2:]


def edges_kernel(sides, *refs):
    own, across = refs[:8], refs[8:]
    planes, width, depth = own[0].shape
    gx = lax.axis_index("gx")
    low = low_half(depth)
    for n, side in enumerate(sides):
        if side == "swap":
            at, high = pl.multiple_of(jnp.where(gx == 0, width - TILE, 0), TILE), gx == 0
        else:
            at, high = (width - TILE, True) if side == "right" else (0, False)
        for a in range(4):
            first = own[a][:, pl.ds(at, TILE)]
            second = own[a + 4][:, pl.ds(at, TILE)].astype(jnp.float32)
            if side == "swap":
                first = jnp.where(high, turned(first), first)
                second = jnp.where(high, second, turned(second))
            elif high:
                first = turned(first)
            else:
                second = turned(second)
            across[n][pl.ds(a * planes, planes)] = jnp.where(low, first, second)


def edges(sides, own):
    planes, width, depth = own[0].shape
    return pl.pallas_call(
        functools.partial(edges_kernel, sides),
        out_shape=[pltpu.VMEM((4 * planes, TILE, depth), jnp.float32)] * len(sides),
        in_specs=[VMEM] * 8,
        out_specs=[VMEM] * len(sides),
        compiler_params=pltpu.CompilerParams(vmem_limit_bytes=32 * 2**20),
        name="edges",
    )(*own)


def lift_kernel(case, *refs):
    own, up = refs[:8], refs[-1]
    planes, width, depth = own[0].shape
    ups = up_counts(case)
    at = [up_traces(case) + n for n in offsets(ups)]
    flat = Plane(lax.axis_index("gx") * width, width, depth, width * lax.axis_size("gx"))
    for a in (CODES, BUNCH):
        if ups[a]:
            up[pl.ds(at[a], ups[a])] = own[a][planes - ups[a] :].astype(jnp.float32)
    values = near_traces(
        flat,
        case,
        planes,
        lambda a, plane: own[a][plane],
        lambda plane: own[CODES][plane],
        lambda plane: own[BUNCH][plane],
    )
    for n, v in enumerate(values):
        up[n] = v


def lift(case, own, after):
    planes, width, depth = own[0].shape
    count = sum(up_counts(case)) + up_traces(case)
    return pl.pallas_call(
        functools.partial(lift_kernel, case),
        out_shape=pltpu.VMEM((count, width, depth), jnp.float32),
        in_specs=[VMEM] * 8 + [ANY] * len(after),
        out_specs=VMEM,
        compiler_params=pltpu.CompilerParams(vmem_limit_bytes=32 * 2**20),
        cost_estimate=pl.CostEstimate(flops=10**7, bytes_accessed=10**7, transcendentals=0),
        name="lift",
    )(*own, *after)


def edge_blocks(right_tile, ghost_tile, left_tile):
    right_tile, ghost_tile, left_tile = turned(right_tile), turned(ghost_tile), turned(left_tile)
    low = low_half(right_tile.shape[-1])
    return jnp.where(low, right_tile, ghost_tile), jnp.where(low, ghost_tile, left_tile)


def corner_starts(case):
    moves = case[0]
    return offsets((moves, moves, moves + 1, moves))


def relay_kernel(case, n_sides, moved, *refs):
    own, beside, (on, off) = refs[:8], refs[8 : 8 + n_sides], refs[8 + n_sides :]
    planes, width, depth = own[0].shape
    moves = case[0]
    gx = lax.axis_index("gx")
    even = lax.axis_index("gz") % 2 == 0
    start = gx * width
    total = width * lax.axis_size("gx")
    low = low_half(depth)
    row = lax.broadcasted_iota(jnp.int32, (TILE, depth), 0)
    ghost_in = ghost_inside(width, depth)[0]

    def block_traces(b):
        flat = Plane(start - HALF if b else start + width - HALF, TILE, depth, total, True)

        def value(a, plane):
            ghost_tile = spread_tiles([side[a % 4 * planes + plane] for side in beside], a >= 4)
            ghost_tile = jnp.where(ghost_in, ghost_tile, 0.0)
            first = own[a][plane, pl.ds(0, TILE)].astype(jnp.float32)
            last = own[a][plane, pl.ds(width - TILE, TILE)].astype(jnp.float32)
            return edge_blocks(last, ghost_tile, first)[b]

        code, bunch = functools.partial(value, CODES), functools.partial(value, BUNCH)
        above = far_traces(flat, case, moved[1], value, code, bunch)[1]
        return above, near_traces(flat, case, planes, value, code, bunch)

    blocks = [block_traces(b) for b in range(2)]
    before = [v for pair in zip(blocks[0][0], blocks[1][0]) for v in pair]
    after = [v for pair in zip(blocks[0][1], blocks[1][1]) for v in pair]

    def fill(to_before, to_after):
        for n, v in enumerate(before):
            to_before[n] = v
        for n, v in enumerate(after):
            to_after[n] = v
        starts = corner_starts(case)
        for n in range(n_sides):
            if n_sides == 1:
                left_column = jnp.where(gx == 0, start + width, start - HALF)
            else:
                left_column = start - HALF if n == 0 else start + width
            whole, half = column_scales(left_column + jnp.where(row < HALF, row, row - HALF), total)
            at = len(before) + n * starts[-1]
            for a in range(4):
                count = starts[a + 1] - starts[a]
                to_before[pl.ds(at + starts[a], count)] = beside[n][pl.ds(a * planes, count)]
            plane = moves - 1
            tile = lambda a, plane: beside[n][a * planes + plane]
            to_before[at + starts[BX] + plane] = tile(BX, plane) + jnp.where(
                low, (TIME_STEP / whole) * tile(EY, moves), 0.0
            )
            to_before[at + plane] = tile(BY - 4, plane) - jnp.where(
                low, 0.0, turned((TIME_STEP / half) * tile(EX, moves))
            )
            base = 3 - moves
            for a in (2, 3):
                to = len(after) + (2 * n + a - 2) * base
                to_after[pl.ds(to, base)] = beside[n][pl.ds((a + 1) * planes - base, base)]

    @pl.when(even)
    def _():
        fill(off, on)

    @pl.when(jnp.logical_not(even))
    def _():
        fill(on, off)


def relay(case, moved, own, beside):
    planes, width, depth = own[0].shape
    count = 8 + len(beside) * corner_starts(case)[-1]
    return pl.pallas_call(
        functools.partial(relay_kernel, case, len(beside)),
        out_shape=[pltpu.VMEM((n, TILE, depth), jnp.float32) for n in (count + 1, count)],
        in_specs=[SMEM] + [VMEM] * (8 + len(beside)),
        out_specs=[VMEM] * 2,
        compiler_params=pltpu.CompilerParams(vmem_limit_bytes=32 * 2**20),
        name="relay",
    )(moved, *own, *beside)


def coefficients(code):
    kind = code.dtype.type
    five, six, seven = code == kind(5), code == kind(6), code == kind(7)
    keep = jnp.where(five, 0.0, jnp.where(six, 0.8 / 1.2, jnp.where(seven, 0.4 / 1.6, 1.0)))
    gain = jnp.where(
        five,
        0.0,
        jnp.where(six, TIME_STEP / 1.2, jnp.where(seven, TIME_STEP / 1.6, TIME_STEP)),
    )
    return keep, gain


def ghost_inside(width, depth):
    gx = lax.axis_index("gx")
    row = lax.broadcasted_iota(jnp.int32, (1, TILE, depth), 1)
    right = gx < lax.axis_size("gx") - 1
    return jnp.where(row < HALF, right.astype(jnp.int32), (gx > 0).astype(jnp.int32)) == 1


def spread_tiles(beside, upper):
    gx = lax.axis_index("gx")
    if len(beside) == 1:
        same = (gx > 0) if upper else (gx == 0)
        return jnp.where(same, beside[0], turned(beside[0]))
    from_left, from_right = beside
    if upper:
        from_right = turned(from_right)
    else:
        from_left = turned(from_left)
    return jnp.where(low_half(from_left.shape[-1]), from_right, from_left)


class Cells:
    def __init__(self, refs, width):
        self.ext, (self.keep, self.gain, self.current, self.rows) = refs[:6], refs[6:]
        self.width = width
        self.tall, self.depth = self.keep.shape[1:]
        self.ghost_in = ghost_inside(width, self.depth)

    def put(self, a, at, count, value, ghost):
        here = pl.ds(at, count)
        where = pl.ds(self.width, TILE) if ghost else pl.ds(0, self.width)
        mask = (lambda v: jnp.where(self.ghost_in, v, 0.0)) if ghost else (lambda v: v)
        if a < 6:
            self.ext[a][here, where] = mask(value)
        elif a == CODES:
            kept, gained = coefficients(value)
            self.keep[here, where], self.gain[here, where] = mask(kept), mask(gained)
        else:
            self.current[here, where] = CURRENT_SCALE * mask(value.astype(jnp.float32))

    def magnetic(self, e, count):
        ext, rows = self.ext, self.rows
        here, above = pl.ds(e, count), pl.ds(e + 1, count)
        ex, ey, es = ext[EX][here], ext[EY][here], ext[ES][here]
        bx = ext[BX][here] - (rows[4] * (next_y(es) - es) - rows[5] * (ext[EY][above] - ey))
        by = ext[BY][here] - rows[6] * ((ext[EX][above] - ex) - (next_x(rows[0] * es) - rows[0] * es))
        bs = ext[BS][here] - rows[4] * ((next_x(ey) - ey) - (next_y(ex) - ex))
        ext[BX][here], ext[BY][here], ext[BS][here] = bx, by, bs

    def electric(self, e, count, moved_now):
        ext, rows = self.ext, self.rows
        here, below, cells = pl.ds(e, count), pl.ds(e - 1, count), pl.ds(e - moved_now, count)
        bx, by, bs = ext[BX][here], ext[BY][here], ext[BS][here]
        kept, gained = self.keep[cells], self.gain[cells]
        ex = kept * ext[EX][here] + gained * ((bs - last_y(bs)) - rows[3] * (by - ext[BY][below]))
        ey = kept * ext[EY][here] + gained * (
            rows[2] * ((bx - ext[BX][below]) - (rows[1] * bs - last_x(rows[1] * bs)))
        )
        es = kept * ext[ES][here] + gained * (
            (by - last_x(by)) - (bx - last_y(bx)) - self.current[cells]
        )
        ext[EX][here], ext[EY][here], ext[ES][here] = ex, ey, es

    def leave(self, plane):
        for a in (BX, BY):
            self.ext[a][plane] = jnp.zeros((self.tall, self.depth), jnp.float32)


def in_groups(start, count, body):
    whole = max(count, 0) // GROUP
    if whole:

        @pl.loop(0, whole)
        def _(i):
            body(start + i * GROUP, GROUP)

    if count > 0 and count % GROUP:
        body(start + whole * GROUP, count % GROUP)


def prepare_kernel(moves, n_sides, moved, *refs):
    own, beside = refs[:8], refs[8 : 8 + n_sides]
    planes, width, depth = own[0].shape
    cells = Cells(refs[8 + n_sides :], width)
    tall, rows = cells.tall, cells.rows
    base = 3 - moves
    top = base + planes - 1
    total = width * lax.axis_size("gx")

    row = lax.broadcasted_iota(jnp.int32, (tall, depth), 0)
    place = lax.axis_index("gx") * width + jnp.where(row < width + HALF, row, row - tall)
    inside = (place >= 0) & (place < total)
    whole, half = column_scales(place, total)
    step = jnp.where(inside, TIME_STEP, 0.0)
    for n, value in enumerate((whole, half, 1.0 / whole, 1.0 / half, step, step / whole, step / half)):
        rows[n] = value
    for a in range(8):
        cells.put(a, base, planes, own[a][...], False)
        tiles = [side[pl.ds(a % 4 * planes, planes)] for side in beside]
        cells.put(a, base, planes, spread_tiles(tiles, a >= 4), True)
    for a in (EX, EY):
        cells.ext[a][0] = jnp.zeros((tall, depth), jnp.float32)
        cells.ext[a][planes + 3] = jnp.zeros((tall, depth), jnp.float32)

    moved_now = 0
    for t in range(STEPS):
        moved_now = moved_now + moved[t]
        in_groups(base + t, planes - 1 - 2 * t, cells.magnetic)

        @pl.when((lax.axis_index("gz") == 0) & (moved_now == t + 1))
        def _():
            cells.leave(base + t)

        in_groups(base + t + 1, planes - 2 - 2 * t, lambda e, n: cells.electric(e, n, moved_now))


def prepare(moves, moved, own, beside):
    planes, width, depth = own[0].shape
    tall = width + TILE
    vmem = lambda *shape: pltpu.VMEM(shape, jnp.float32)
    shapes = [vmem(planes + 4, tall, depth)] * 9
    shapes += [vmem(7, tall, depth)]
    return pl.pallas_call(
        functools.partial(prepare_kernel, moves, len(beside)),
        out_shape=shapes,
        in_specs=[SMEM] + [VMEM] * (8 + len(beside)),
        out_specs=[VMEM] * len(shapes),
        compiler_params=pltpu.CompilerParams(vmem_limit_bytes=32 * 2**20),
        cost_estimate=pl.CostEstimate(flops=22 * 10**8, bytes_accessed=10**7, transcendentals=0),
        name="prepare",
    )(moved, *own, *beside)


def steps_kernel(case, n_sides, planes, width, moved, *refs):
    rows, down, up, on, off = refs[9:14]
    outs = refs[14:20]
    cells = Cells((*refs[20:29], rows), width)
    sems = refs[29]
    ext = cells.ext
    moves = case[0]
    base = 3 - moves
    top = base + planes - 1
    far = planes + 3
    first = lax.axis_index("gz") == 0
    last = lax.axis_index("gz") == lax.axis_size("gz") - 1
    even = lax.axis_index("gz") % 2 == 0
    downs, ups = down_counts(case), up_counts(case)
    at, up_at = offsets(downs[:6]), [up_traces(case) + n for n in offsets(ups)]
    far_at = at[-1]
    at = at[:6] + [far_at + 4, far_at + 4 + downs[CODES]]
    copies = []

    def send(a, start, end):
        if end > start:
            item = pltpu.make_async_copy(
                ext[a].at[pl.ds(start, end - start), pl.ds(0, width)],
                outs[a].at[pl.ds(start - 3, end - start)],
                sems.at[len(copies)],
            )
            item.start()
            copies.append(item)

    for a in range(6):
        send(a, base + (2 if a >= BX else 3), top - 2)

    starts = corner_starts(case)

    def came(span, above):
        if above:
            return jnp.where(even, on[span], off[span])
        return jnp.where(even, off[span], on[span])

    def corner_above(a, count):
        at = [8 + n * starts[-1] + starts[a % 4] for n in range(n_sides)]
        return spread_tiles([came(pl.ds(n, count), True) for n in at], a >= 4)

    def corner_below(a, count):
        at = [2 * up_traces(case) + (2 * n + a % 4 - 1) * base - count for n in range(n_sides)]
        return spread_tiles([came(pl.ds(n, count), False) for n in at], a >= 4)

    for a in range(8):
        if downs[a]:
            cells.put(a, top + 1, downs[a], down[pl.ds(at[a], downs[a])], False)
            cells.put(a, top + 1, downs[a], corner_above(a, downs[a]), True)
        if ups[a]:
            cells.put(a, base - ups[a], ups[a], up[pl.ds(up_at[a], ups[a])], False)
            cells.put(a, base - ups[a], ups[a], corner_below(a, ups[a]), True)

    low = low_half(cells.depth)
    tile_row = lax.broadcasted_iota(jnp.int32, (TILE, cells.depth), 0)

    def trace(value, n, above):
        right_block, left_block = came(2 * n, above), came(2 * n + 1, above)
        at_right = jnp.where(tile_row >= TILE - 2, turned(right_block), value[width - TILE :])
        at_left = jnp.where(tile_row < 2, turned(left_block), value[:TILE])
        beyond = turned(jnp.where(low, left_block, right_block))
        return jnp.concatenate([at_left, value[TILE : width - TILE], at_right, beyond], 0)

    def far_first():
        for a in (EX, EY):
            ext[a][far] = jnp.where(last, 0.0, trace(down[far_at + a], a, True))

    def far_second(moved_now):
        gained = cells.gain[far - moved_now]
        ex = trace(down[far_at + 2], 2, True) + gained * (rows[3] * ext[BY][far - 1])
        ey = trace(down[far_at + 3], 3, True) - gained * (rows[2] * ext[BX][far - 1])
        ext[EX][far], ext[EY][far] = jnp.where(last, 0.0, ex), jnp.where(last, 0.0, ey)

    def below_first(moved_now):
        bx, by = rows[5] * ext[EY][base], -rows[6] * ext[EX][base]
        ext[BX][base - 1] = trace(up[0], 0, False) + bx
        ext[BY][base - 1] = trace(up[1], 1, False) + by
        if moves == 2:
            return None
        gained = cells.gain[1 - moved_now]
        ex, ey = -gained * (rows[3] * by), gained * (rows[2] * bx)
        es = gained * ((by - last_x(by)) - (bx - last_y(bx)))
        weighted = rows[0] * es
        bx = bx - rows[4] * (next_y(es) - es) - rows[5] * ey
        by = by + rows[6] * (ex + next_x(weighted) - weighted)
        return trace(up[2], 2, False) + bx, trace(up[3], 3, False) + by

    def below_second(state):
        ext[BX][1] = state[0] + rows[5] * ext[EY][base]
        ext[BY][1] = state[1] - rows[6] * ext[EX][base]

    moved_now = 0
    for t in range(STEPS):
        moved_now = moved_now + moved[t]
        above = moves + 1 + t
        lowest, lowest_e = max(t, base), max(t + 1, base)
        if t == 0:
            below_state = below_first(moved_now)
        if base + t > lowest:
            cells.magnetic(lowest, base + t - lowest)
        cells.magnetic(top - t, above)
        if moves == 1 and t == 1:
            below_second(below_state)

        @pl.when(first)
        def _():
            cells.leave(base + moved_now - 1)

        if t == STEPS - 1:
            for a in (BX, BY, BS):
                send(a, 3, base + 2)
                send(a, top - 2, planes + 3)
        low_part = lowest_e, base + t + 1 - lowest_e
        if t < STEPS - 1:
            cells.electric(*low_part, moved_now)
            cells.electric(top - t, above, moved_now)
        else:
            cut = above // 2
            for start, count in ((top - 2, cut), (top - 2 + cut, above - cut), low_part):
                cells.electric(start, count, moved_now)
                for a in (EX, EY, ES):
                    send(a, start, start + count)
        if t == 0:
            far_first()
        elif t == 1:
            far_second(moved_now)
        if t < STEPS - 1:

            @pl.when(last)
            def _():
                for a in (EX, EY, ES):
                    ext[a][top + 1 + moved_now] = jnp.zeros((cells.tall, cells.depth), jnp.float32)

    for item in copies:
        item.wait()


def advance(case, n_sides, moved, shape, ready, ghosts):
    planes, width, depth = shape
    block = jax.ShapeDtypeStruct(shape, jnp.float32)
    n_in = 11 + len(ghosts)
    found = pl.pallas_call(
        functools.partial(steps_kernel, case, n_sides, planes, width),
        out_shape=[block] * 6 + [pltpu.VMEM(x.shape, x.dtype) for x in ready[:9]],
        in_specs=[SMEM] + [VMEM] * (n_in - 1),
        out_specs=[ANY] * 6 + [VMEM] * 9,
        input_output_aliases={1 + n: 6 + n for n in range(9)},
        scratch_shapes=[pltpu.SemaphoreType.DMA((21,))],
        compiler_params=pltpu.CompilerParams(vmem_limit_bytes=32 * 2**20),
        name="steps",
    )(moved, *ready, *ghosts)
    return tuple(found[:6])


def passed(block, to, sides=(0,)):
    size_z, size_x = lax.axis_size("gz"), lax.axis_size("gx")
    route = [
        (z * size_x + x, to(z) * size_x + x + dx)
        for z in range(size_z)
        for x in range(size_x)
        for dx in sides
        if 0 <= to(z) < size_z and 0 <= x + dx < size_x
    ]
    return lax.ppermute(block, ("gz", "gx"), route)


def on_device(*args):
    arrays, moved = args[:8], args[8]
    arrays = arrays[:6] + (arrays[7], arrays[6])
    sides = ("swap",) if lax.axis_size("gx") == 2 else ("right", "left")
    which, moved, sent = pack(arrays, moved)

    def run(c, own, sent, moved):
        case = CASES[c]
        down = passed(sent[c], lambda z: z - 1)
        across = edges(sides, own)
        ways = {"swap": (1, -1), "right": (1,), "left": (-1,)}
        beside = [passed(block, lambda z: z, ways[side]) for block, side in zip(across, sides)]
        up = passed(lift(case, own, across), lambda z: z + 1)
        on, off = relay(case, moved, own, beside)
        off = passed(off, lambda z: z + 1 if z % 2 else z - 1)
        on = passed(on, lambda z: z ^ 1)
        ready = prepare(case[0], moved, own, beside)
        return advance(case, len(sides), moved, own[0].shape, ready, [down, up, on, off])

    return lax.switch(
        which[0],
        [functools.partial(run, c) for c in range(len(CASES))],
        arrays,
        sent,
        moved,
    )


def solution(mesh):
    block = P("gz", "gx", None)
    return jax.shard_map(
        on_device,
        mesh=mesh,
        in_specs=(block,) * 8 + (P(),),
        out_specs=(block,) * 6,
        check_vma=False,
    )
```

time: 20.7 us -> 20.8 us (level)
    pallas_call x1, Pallas kernels: 0.04 us -> 0.33 us  [relay(): pl.pallas_call(functools.partial(relay_kernel, case, len(beside)), out_sh...]
  transfers between devices with their start and end apart: 5 -> 5, of which waited for: 1 -> 1; matrix products, arithmetic and copies ran while one was open for 0% -> 0% of each run, Pallas kernels for 9% -> 10%
where the time goes in v9:
time: 20.8 us
  starting transfers between devices  11.6 us (56%)
  Pallas kernels  6.18 us (30%)
  waiting for transfers between devices  1.54 us (7%)
  between operations  0.96 us (5%)
  loops' own time  0.5 us (2%)
    ppermute x5, starting transfers between devices, passed(): return lax.ppermute(block, ('gz', 'gx'), route)  11.6 us
    pallas_call x1, Pallas kernels, advance(): pl.pallas_call(functools.partial(steps_kernel, case, n_sides, planes, wid...  2.33 us
    pallas_call x1, Pallas kernels, pack(): pl.pallas_call(pack_kernel, out_shape=shapes, in_specs=[ANY] * 9, out_spe...  1.85 us
    ppermute x5, waiting for transfers between devices, passed(): return lax.ppermute(block, ('gz', 'gx'), route)  1.54 us
    pallas_call x1, Pallas kernels, prepare(): pl.pallas_call(functools.partial(prepare_kernel, moves, len(beside)), out...  1.53 us
    another operation x1, loops' own time, on_device(): lax.switch(which[0], [functools.partial(run, c) for c in range(len(CASES)...  0.5 us
  transfers between devices with their start and end apart: 5, of which 1 were waited for; matrix products, arithmetic and copies ran while one was open for 0% of the time, Pallas kernels for 10%

profile of v9, /device:TPU:5, one launch (start us, length us, event | category | flops | bytes accessed | tf_op | source)
XLA Modules:
  0.0 20.8 jit_solution(2238081460772181266)
XLA Ops:
  0.6 0.0 copy-start.6
  0.6 0.0 copy-start.7
  0.7 0.0 copy-start.5
  0.7 0.0 copy-start.4
  0.7 0.0 copy-start.3
  0.7 0.0 copy-start.2
  0.7 0.0 copy-start.1
  0.7 0.0 copy-start
  0.7 1.9 %pack.1 = (s32[1]{0:T(128)S(4)}, s32[3]{0:T(128)S(4)}, f32[11,64,128]{2,1,0:T(8,128)S(1)}, f32[13,64,128]{2,1,0:T(8,128)S(1)}, f32[19,64,128]{2,1,0:T(8,128)S(1)}, /*index=5*/f32[21,64,128]{2,1,0:T(8,128)S(1)}) custom-call(f32[8,64,128]{2,1,0:T(8,128)} %refs_0_.1, f32[8,64,128]{2,1,0:T(8,128)} %refs_1_.1, f32[8,64,128]{2,1,0:T(8,128)} %refs_2_.1, ...), custom_call_target="tpu_custom_call" | custom-call | tf_op jit(solution)/shard_map/pack/pallas_call | solution.py:226
  2.7 17.9 %conditional.1 = (f32[8,64,128]{2,1,0:T(8,128)}, f32[8,64,128]{2,1,0:T(8,128)}, f32[8,64,128]{2,1,0:T(8,128)}, f32[8,64,128]{2,1,0:T(8,128)}, f32[8,64,128]{2,1,0:T(8,128)}, /*index=5*/f32[8,64,128]{2,1,0:T(8,128)}) conditional(s32[]{:T(128)} %bitcast, (f32[8,64,128]{2,1,0:T(8,128)S(1)}, f32[8,64,128]{2,1,0:T(8,128)S(1)}, ...), branch_computations={%region_0.0_spmd, %region_1.0_spmd, %region_2.0_spmd, %region_3.0_... | conditional | flops 2209999872 | bytes 24112632 | solution.py:736
  2.7 2.6 %collective-permute-start.11 = (f32[19,64,128]{2,1,0:T(8,128)S(1)}, f32[19,64,128]{2,1,0:T(8,128)S(1)}, u32[]{:S(2)}, u32[]{:S(2)}) collective-permute-start(f32[19,64,128]{2,1,0:T(8,128)S(1)} %get-tuple-element.155), channel_id=1, source_target_pairs={{2,0},{3,1},{4,2},{5,3},{6,4},{7,5},{8,6},{9,7},{10,8},{11,9},{12,... | collective-permute-start | bytes 1867784 | tf_op jit(solution)/shard_map/cond/branch_2_fun/ppermute | solution.py:714
  5.3 1.3 %collective-permute-start.10 = (f32[32,8,128]{2,1,0:T(8,128)S(1)}, f32[32,8,128]{2,1,0:T(8,128)S(1)}, u32[]{:S(2)}, u32[]{:S(2)}) collective-permute-start(f32[32,8,128]{2,1,0:T(8,128)S(1)} %edges.6.refs_8_), channel_id=1, source_target_pairs={{0,1},{1,0},{2,3},{3,2},{4,5},{5,4},{6,7},{7,6},{8,9},{9,8},{10,11... | collective-permute-start | bytes 393224 | tf_op jit(solution)/shard_map/cond/branch_2_fun/ppermute | solution.py:714
  6.6 0.1 lift.6
  6.7 4.2 %collective-permute-start.12 = (f32[4,64,128]{2,1,0:T(8,128)S(1)}, f32[4,64,128]{2,1,0:T(8,128)S(1)}, u32[]{:S(2)}, u32[]{:S(2)}) collective-permute-start(f32[4,64,128]{2,1,0:T(8,128)S(1)} %lift.6), channel_id=1, source_target_pairs={{0,2},{1,3},{2,4},{3,5},{4,6},{5,7},{6,8},{7,9},{8,10},{9,11},{10,... | collective-permute-start | bytes 393224 | tf_op jit(solution)/shard_map/cond/branch_2_fun/ppermute | solution.py:714
  10.9 0.0 collective-permute-done.10.refs_8_
  10.9 0.3 %relay.6 = (f32[18,8,128]{2,1,0:T(8,128)S(1)}, f32[17,8,128]{2,1,0:T(8,128)S(1)}) custom-call(s32[3]{0:T(128)S(4)} %get-tuple-element.136.moved, f32[8,64,128]{2,1,0:T(8,128)S(1)} %get-tuple-element.137.refs_0_, f32[8,64,128]{2,1,0:T(8,128)S(1)} %get-tuple-element.138.refs_1_, f32[8,64,128]{2,1,0:T(8,128)S(1)} %get-tuple-element.139.refs_2_, ...), custom_call_target="tpu_custom_call" | custom-call | tf_op jit(solution)/shard_map/cond/branch_2_fun/relay/pallas_call | solution.py:395
  11.2 3.5 %collective-permute-start.14 = (f32[17,8,128]{2,1,0:T(8,128)S(1)}, f32[17,8,128]{2,1,0:T(8,128)S(1)}, u32[]{:S(2)}, u32[]{:S(2)}) collective-permute-start(f32[17,8,128]{2,1,0:T(8,128)S(1)} %get-tuple-element.157), channel_id=1, source_target_pairs={{2,4},{3,5},{4,2},{5,3},{6,8},{7,9},{8,6},{9,7},{10,12},{11,13},{1... | collective-permute-start | bytes 208904 | tf_op jit(solution)/shard_map/cond/branch_2_fun/ppermute | solution.py:714
  14.7 0.1 collective-permute-start.13
  14.8 1.5 %prepare.6 = (f32[12,72,128]{2,1,0:T(8,128)S(1)}, f32[12,72,128]{2,1,0:T(8,128)S(1)}, f32[12,72,128]{2,1,0:T(8,128)S(1)}, f32[12,72,128]{2,1,0:T(8,128)S(1)}, f3...) custom-call(s32[3]{0:T(128)S(4)} %get-tuple-element.136.moved, ...), custom_call_target="tpu_custom_call" | custom-call | flops 2200000000 | bytes 10000000 | tf_op jit(solution)/shard_map/cond/branch_2_fun/prepare/pallas_call | solution.py:538
  16.3 0.0 collective-permute-done.12.refs_11_
  16.3 1.5 %collective-permute-done.14.refs_13_ = f32[17,8,128]{2,1,0:T(8,128)S(1)} collective-permute-done((f32[17,8,128]{2,1,0:T(8,128)S(1)}, f32[17,8,128]{2,1,0:T(8,128)S(1)}, u32[]{:S(2)}, u32[]{:S(2)}) %collective-permute-start.14) | collective-permute-done | bytes 69664 | tf_op jit(solution)/shard_map/cond/branch_2_fun/ppermute | solution.py:714
  17.8 0.0 collective-permute-done.13.refs_12_
  17.8 0.0 collective-permute-done.11.refs_10_
  17.9 2.3 %steps.6 = (f32[8,64,128]{2,1,0:T(8,128)}, f32[8,64,128]{2,1,0:T(8,128)}, f32[8,64,128]{2,1,0:T(8,128)}, f32[8,64,128]{2,1,0:T(8,128)}, f32[8,64,128]{2,1,0:T(8,...) custom-call(s32[3]{0:T(128)S(4)} %get-tuple-element.136.moved, ...), custom_call_target="tpu_custom_call", output_to_operand_aliasing={{6}: (1, {}), {7}: (2, {}), {8}: (3, {}), {9}: (4, {}), {10... | custom-call | tf_op jit(solution)/shard_map/cond/branch_2_fun/steps/pallas_call | solution.py:692
  (9 shorter events, 0.1 us)
Async XLA Ops:
  0.6 1.9 %copy-start.6 = (s32[8,64,128]{2,1,0:T(8,128)S(1)}, s32[8,64,128]{2,1,0:T(8,128)}, u32[]{:S(2)}) copy-start(s32[8,64,128]{2,1,0:T(8,128)} %refs_6_.1) | copy-start | bytes 786436
  0.6 1.9 %copy-start.7 = (s32[8,64,128]{2,1,0:T(8,128)S(1)}, s32[8,64,128]{2,1,0:T(8,128)}, u32[]{:S(2)}) copy-start(s32[8,64,128]{2,1,0:T(8,128)} %refs_7_.1) | copy-start | bytes 786436
  0.7 1.9 %copy-start.5 = (f32[8,64,128]{2,1,0:T(8,128)S(1)}, f32[8,64,128]{2,1,0:T(8,128)}, u32[]{:S(2)}) copy-start(f32[8,64,128]{2,1,0:T(8,128)} %refs_5_.1) | copy-start | bytes 786436
  0.7 1.9 %copy-start.4 = (f32[8,64,128]{2,1,0:T(8,128)S(1)}, f32[8,64,128]{2,1,0:T(8,128)}, u32[]{:S(2)}) copy-start(f32[8,64,128]{2,1,0:T(8,128)} %refs_4_.1) | copy-start | bytes 786436
  0.7 1.9 %copy-start.3 = (f32[8,64,128]{2,1,0:T(8,128)S(1)}, f32[8,64,128]{2,1,0:T(8,128)}, u32[]{:S(2)}) copy-start(f32[8,64,128]{2,1,0:T(8,128)} %refs_3_.1) | copy-start | bytes 786436
  0.7 1.9 %copy-start.2 = (f32[8,64,128]{2,1,0:T(8,128)S(1)}, f32[8,64,128]{2,1,0:T(8,128)}, u32[]{:S(2)}) copy-start(f32[8,64,128]{2,1,0:T(8,128)} %refs_2_.1) | copy-start | bytes 786436
  0.7 1.9 %copy-start.1 = (f32[8,64,128]{2,1,0:T(8,128)S(1)}, f32[8,64,128]{2,1,0:T(8,128)}, u32[]{:S(2)}) copy-start(f32[8,64,128]{2,1,0:T(8,128)} %refs_1_.1) | copy-start | bytes 786436
  0.7 1.9 %copy-start = (f32[8,64,128]{2,1,0:T(8,128)S(1)}, f32[8,64,128]{2,1,0:T(8,128)}, u32[]{:S(2)}) copy-start(f32[8,64,128]{2,1,0:T(8,128)} %refs_0_.1) | copy-start | bytes 786436
  2.7 15.2 %collective-permute-start.11 = (f32[19,64,128]{2,1,0:T(8,128)S(1)}, f32[19,64,128]{2,1,0:T(8,128)S(1)}, u32[]{:S(2)}, u32[]{:S(2)}) collective-permute-start(f32[19,64,128]{2,1,0:T(8,128)S(1)} %get-tuple-element.155), channel_id=1, source_target_pairs={{2,0},{3,1},{4,2},{5,3},{6,4},{7,5},{8,6},{9,7},{10,8},{11,9},{12,... | collective-permute-start | bytes 1867784 | tf_op jit(solution)/shard_map/cond/branch_2_fun/ppermute | solution.py:714
  5.3 5.5 %collective-permute-start.10 = (f32[32,8,128]{2,1,0:T(8,128)S(1)}, f32[32,8,128]{2,1,0:T(8,128)S(1)}, u32[]{:S(2)}, u32[]{:S(2)}) collective-permute-start(f32[32,8,128]{2,1,0:T(8,128)S(1)} %edges.6.refs_8_), channel_id=1, source_target_pairs={{0,1},{1,0},{2,3},{3,2},{4,5},{5,4},{6,7},{7,6},{8,9},{9,8},{10,11... | collective-permute-start | bytes 393224 | tf_op jit(solution)/shard_map/cond/branch_2_fun/ppermute | solution.py:714
  6.7 9.6 %collective-permute-start.12 = (f32[4,64,128]{2,1,0:T(8,128)S(1)}, f32[4,64,128]{2,1,0:T(8,128)S(1)}, u32[]{:S(2)}, u32[]{:S(2)}) collective-permute-start(f32[4,64,128]{2,1,0:T(8,128)S(1)} %lift.6), channel_id=1, source_target_pairs={{0,2},{1,3},{2,4},{3,5},{4,6},{5,7},{6,8},{7,9},{8,10},{9,11},{10,... | collective-permute-start | bytes 393224 | tf_op jit(solution)/shard_map/cond/branch_2_fun/ppermute | solution.py:714
  11.2 6.6 %collective-permute-start.14 = (f32[17,8,128]{2,1,0:T(8,128)S(1)}, f32[17,8,128]{2,1,0:T(8,128)S(1)}, u32[]{:S(2)}, u32[]{:S(2)}) collective-permute-start(f32[17,8,128]{2,1,0:T(8,128)S(1)} %get-tuple-element.157), channel_id=1, source_target_pairs={{2,4},{3,5},{4,2},{5,3},{6,8},{7,9},{8,6},{9,7},{10,12},{11,13},{1... | collective-permute-start | bytes 208904 | tf_op jit(solution)/shard_map/cond/branch_2_fun/ppermute | solution.py:714
  14.7 3.2 %collective-permute-start.13 = (f32[18,8,128]{2,1,0:T(8,128)S(1)}, f32[18,8,128]{2,1,0:T(8,128)S(1)}, u32[]{:S(2)}, u32[]{:S(2)}) collective-permute-start(f32[18,8,128]{2,1,0:T(8,128)S(1)} %get-tuple-element.156), channel_id=1, source_target_pairs={{0,2},{1,3},{2,0},{3,1},{4,6},{5,7},{6,4},{7,5},{8,10},{9,11},{10,... | collective-permute-start | bytes 221192 | tf_op jit(solution)/shard_map/cond/branch_2_fun/ppermute | solution.py:714

commit v10 on v9

--- a/solution.py
+++ b/solution.py
@@ -23,7 +23,7 @@
 def down_counts(case):
     moves, now = case
     later = moves - now
-    return (moves,) * 6 + (later + 1, later)
+    return (moves,) * 6 + (later + (moves == 1), later)
 
 
 def up_counts(case):
@@ -117,27 +117,36 @@
 
 def far_traces(flat, case, second_move, field, code, bunch, codes_ready=lambda: None):
     far, first_move = case
+    lowest = far - 1 if far == 1 else far - 2
     folded, now_b = {}, {}
-    for plane in range(far - 1, far + 2):
+    for plane in range(lowest, far + 2):
         above = field(EX, plane + 1), field(EY, plane + 1)
         folded[plane] = flat.add_above(field(BX, plane), field(BY, plane), *above)
         fields = field(EX, plane), field(EY, plane), field(ES, plane)
         now_b[plane] = flat.radial_vertical(*folded[plane], *fields)
     codes_ready()
-    now_e, now_s = {}, {}
-    for plane in (far, far + 1):
+    now_e, now_es, now_bs = {}, {}, {}
+    for plane in range(lowest + 1, far + 2):
         ex, ey = field(EX, plane), field(EY, plane)
-        now_s[plane] = flat.longitudinal(field(BS, plane), ex, ey)
+        now_bs[plane] = flat.longitudinal(field(BS, plane), ex, ey)
         factors = coefficients(code(plane - first_move))
         over = [up - under for up, under in zip(now_b[plane], now_b[plane - 1])]
-        now_e[plane] = flat.electric(ex, ey, now_s[plane], *over, factors)
-        if plane == far:
-            es = flat.electric_s(field(ES, far), *now_b[far], bunch(far - first_move), factors)
-    bx, by = flat.add_above(*now_b[far], *now_e[far + 1])
-    bx, by = flat.radial_vertical(bx, by, *now_e[far], es)
-    bs = flat.longitudinal(now_s[far], *now_e[far])
+        now_e[plane] = flat.electric(ex, ey, now_bs[plane], *over, factors)
+        if plane <= far:
+            now_es[plane] = flat.electric_s(
+                field(ES, plane), *now_b[plane], bunch(plane - first_move), factors
+            )
+
+    def second(plane):
+        next_b = flat.add_above(*now_b[plane], *now_e[plane + 1])
+        return flat.radial_vertical(*next_b, *now_e[plane], now_es[plane])
+
+    over = second(far)
+    if far == 2:
+        over = [up - under for up, under in zip(over, second(far - 1))]
+    bs = flat.longitudinal(now_bs[far], *now_e[far])
     factors = coefficients(code(far - first_move - second_move))
-    return folded[far - 1], (*now_e[far], *flat.electric(*now_e[far], bs, bx, by, factors))
+    return folded[far - 1], (*now_e[far], *flat.electric(*now_e[far], bs, *over, factors))
 
 
 def near_traces(flat, case, planes, field, code, bunch):
@@ -318,7 +327,7 @@
 
 def corner_starts(case):
     moves = case[0]
-    return offsets((moves, moves, moves + 1, moves))
+    return offsets((moves, moves, moves + (moves == 1), moves))
 
 
 def relay_kernel(case, n_sides, moved, *refs):
@@ -616,9 +625,11 @@
             ext[a][far] = jnp.where(last, 0.0, trace(down[far_at + a], a, True))
 
     def far_second(moved_now):
-        gained = cells.gain[far - moved_now]
-        ex = trace(down[far_at + 2], 2, True) + gained * (rows[3] * ext[BY][far - 1])
-        ey = trace(down[far_at + 3], 3, True) - gained * (rows[2] * ext[BX][far - 1])
+        ex, ey = trace(down[far_at + 2], 2, True), trace(down[far_at + 3], 3, True)
+        if moves == 1:
+            gained = cells.gain[far - moved_now]
+            ex = ex + gained * (rows[3] * ext[BY][far - 1])
+            ey = ey - gained * (rows[2] * ext[BX][far - 1])
         ext[EX][far], ext[EY][far] = jnp.where(last, 0.0, ex), jnp.where(last, 0.0, ey)
 
     def below_first(moved_now):

time: 20.8 us -> 20.8 us (level)
  no operation moved by 1% of the time
where the time goes in v10:
time: 20.8 us; the launch traced here: 20.6 us
  starting transfers between devices  11.6 us (56%)
  Pallas kernels  6.19 us (30%)
  waiting for transfers between devices  1.39 us (7%)
  between operations  0.96 us (5%)
  loops' own time  0.51 us (2%)
    ppermute x5, starting transfers between devices, passed(): return lax.ppermute(block, ('gz', 'gx'), route)  11.6 us
    pallas_call x1, Pallas kernels, advance(): pl.pallas_call(functools.partial(steps_kernel, case, n_sides, planes, wid...  2.3 us
    pallas_call x1, Pallas kernels, pack(): pl.pallas_call(pack_kernel, out_shape=shapes, in_specs=[ANY] * 9, out_spe...  1.91 us
    pallas_call x1, Pallas kernels, prepare(): pl.pallas_call(functools.partial(prepare_kernel, moves, len(beside)), out...  1.53 us
    ppermute x5, waiting for transfers between devices, passed(): return lax.ppermute(block, ('gz', 'gx'), route)  1.39 us
    another operation x1, loops' own time, on_device(): lax.switch(which[0], [functools.partial(run, c) for c in range(len(CASES)...  0.51 us
  transfers between devices with their start and end apart: 5, of which 1 were waited for; matrix products, arithmetic and copies ran while one was open for 0% of the time, Pallas kernels for 10%

profile of v10, /device:TPU:5, one launch (start us, length us, event | category | flops | bytes accessed | tf_op | source)
XLA Modules:
  0.0 20.6 jit_solution(13358178160974991473)
XLA Ops:
  0.6 0.0 copy-start.6
  0.6 0.0 copy-start.7
  0.7 0.0 copy-start.5
  0.7 0.0 copy-start.4
  0.7 0.0 copy-start.3
  0.7 0.0 copy-start.2
  0.7 0.0 copy-start.1
  0.7 0.0 copy-start
  0.7 1.9 %pack.1 = (s32[1]{0:T(128)S(4)}, s32[3]{0:T(128)S(4)}, f32[11,64,128]{2,1,0:T(8,128)S(1)}, f32[13,64,128]{2,1,0:T(8,128)S(1)}, f32[18,64,128]{2,1,0:T(8,128)S(1)}, /*index=5*/f32[20,64,128]{2,1,0:T(8,128)S(1)}) custom-call(f32[8,64,128]{2,1,0:T(8,128)} %refs_0_.1, f32[8,64,128]{2,1,0:T(8,128)} %refs_1_.1, f32[8,64,128]{2,1,0:T(8,128)} %refs_2_.1, ...), custom_call_target="tpu_custom_call" | custom-call | tf_op jit(solution)/shard_map/pack/pallas_call | solution.py:235
  2.7 17.7 %conditional.1 = (f32[8,64,128]{2,1,0:T(8,128)}, f32[8,64,128]{2,1,0:T(8,128)}, f32[8,64,128]{2,1,0:T(8,128)}, f32[8,64,128]{2,1,0:T(8,128)}, f32[8,64,128]{2,1,0:T(8,128)}, /*index=5*/f32[8,64,128]{2,1,0:T(8,128)}) conditional(s32[]{:T(128)} %bitcast, (f32[8,64,128]{2,1,0:T(8,128)S(1)}, f32[8,64,128]{2,1,0:T(8,128)S(1)}, ...), branch_computations={%region_0.0_spmd, %region_1.0_spmd, %region_2.0_spmd, %region_3.0_... | conditional | flops 2209999872 | bytes 23948792 | solution.py:747
  2.9 2.6 %collective-permute-start.16 = (f32[20,64,128]{2,1,0:T(8,128)S(1)}, f32[20,64,128]{2,1,0:T(8,128)S(1)}, u32[]{:S(2)}, u32[]{:S(2)}) collective-permute-start(f32[20,64,128]{2,1,0:T(8,128)S(1)} %get-tuple-element.183), channel_id=1, source_target_pairs={{2,0},{3,1},{4,2},{5,3},{6,4},{7,5},{8,6},{9,7},{10,8},{11,9},{12,... | collective-permute-start | bytes 1966088 | tf_op jit(solution)/shard_map/cond/branch_3_fun/ppermute | solution.py:725
  5.6 1.3 %collective-permute-start.15 = (f32[32,8,128]{2,1,0:T(8,128)S(1)}, f32[32,8,128]{2,1,0:T(8,128)S(1)}, u32[]{:S(2)}, u32[]{:S(2)}) collective-permute-start(f32[32,8,128]{2,1,0:T(8,128)S(1)} %edges.7.refs_8_), channel_id=1, source_target_pairs={{0,1},{1,0},{2,3},{3,2},{4,5},{5,4},{6,7},{7,6},{8,9},{9,8},{10,11... | collective-permute-start | bytes 393224 | tf_op jit(solution)/shard_map/cond/branch_3_fun/ppermute | solution.py:725
  6.9 0.1 lift.7
  6.9 4.2 %collective-permute-start.17 = (f32[2,64,128]{2,1,0:T(8,128)S(1)}, f32[2,64,128]{2,1,0:T(8,128)S(1)}, u32[]{:S(2)}, u32[]{:S(2)}) collective-permute-start(f32[2,64,128]{2,1,0:T(8,128)S(1)} %lift.7), channel_id=1, source_target_pairs={{0,2},{1,3},{2,4},{3,5},{4,6},{5,7},{6,8},{7,9},{8,10},{9,11},{10,... | collective-permute-start | bytes 196616 | tf_op jit(solution)/shard_map/cond/branch_3_fun/ppermute | solution.py:725
  11.1 0.0 collective-permute-done.15.refs_8_
  11.1 0.3 %relay.7 = (f32[17,8,128]{2,1,0:T(8,128)S(1)}, f32[16,8,128]{2,1,0:T(8,128)S(1)}) custom-call(s32[3]{0:T(128)S(4)} %get-tuple-element.164.moved, f32[8,64,128]{2,1,0:T(8,128)S(1)} %get-tuple-element.165.refs_0_, f32[8,64,128]{2,1,0:T(8,128)S(1)} %get-tuple-element.166.refs_1_, f32[8,64,128]{2,1,0:T(8,128)S(1)} %get-tuple-element.167.refs_2_, ...), custom_call_target="tpu_custom_call" | custom-call | tf_op jit(solution)/shard_map/cond/branch_3_fun/relay/pallas_call | solution.py:404
  11.4 3.5 %collective-permute-start.19 = (f32[16,8,128]{2,1,0:T(8,128)S(1)}, f32[16,8,128]{2,1,0:T(8,128)S(1)}, u32[]{:S(2)}, u32[]{:S(2)}) collective-permute-start(f32[16,8,128]{2,1,0:T(8,128)S(1)} %get-tuple-element.185), channel_id=1, source_target_pairs={{2,4},{3,5},{4,2},{5,3},{6,8},{7,9},{8,6},{9,7},{10,12},{11,13},{1... | collective-permute-start | bytes 196616 | tf_op jit(solution)/shard_map/cond/branch_3_fun/ppermute | solution.py:725
  14.9 0.1 collective-permute-start.18
  15.0 1.5 %prepare.7 = (f32[12,72,128]{2,1,0:T(8,128)S(1)}, f32[12,72,128]{2,1,0:T(8,128)S(1)}, f32[12,72,128]{2,1,0:T(8,128)S(1)}, f32[12,72,128]{2,1,0:T(8,128)S(1)}, f3...) custom-call(s32[3]{0:T(128)S(4)} %get-tuple-element.164.moved, ...), custom_call_target="tpu_custom_call" | custom-call | flops 2200000000 | bytes 10000000 | tf_op jit(solution)/shard_map/cond/branch_3_fun/prepare/pallas_call | solution.py:547
  16.5 0.0 collective-permute-done.17.refs_11_
  16.5 1.4 %collective-permute-done.19.refs_13_ = f32[16,8,128]{2,1,0:T(8,128)S(1)} collective-permute-done((f32[16,8,128]{2,1,0:T(8,128)S(1)}, f32[16,8,128]{2,1,0:T(8,128)S(1)}, u32[]{:S(2)}, u32[]{:S(2)}) %collective-permute-start.19) | collective-permute-done | bytes 65568 | tf_op jit(solution)/shard_map/cond/branch_3_fun/ppermute | solution.py:725
  17.9 0.0 collective-permute-done.18.refs_12_
  17.9 0.0 collective-permute-done.16.refs_10_
  17.9 2.3 %steps.7 = (f32[8,64,128]{2,1,0:T(8,128)}, f32[8,64,128]{2,1,0:T(8,128)}, f32[8,64,128]{2,1,0:T(8,128)}, f32[8,64,128]{2,1,0:T(8,128)}, f32[8,64,128]{2,1,0:T(8,...) custom-call(s32[3]{0:T(128)S(4)} %get-tuple-element.164.moved, ...), custom_call_target="tpu_custom_call", output_to_operand_aliasing={{6}: (1, {}), {7}: (2, {}), {8}: (3, {}), {9}: (4, {}), {10... | custom-call | tf_op jit(solution)/shard_map/cond/branch_3_fun/steps/pallas_call | solution.py:703
  (9 shorter events, 0.1 us)
Async XLA Ops:
  0.6 2.0 %copy-start.6 = (s32[8,64,128]{2,1,0:T(8,128)S(1)}, s32[8,64,128]{2,1,0:T(8,128)}, u32[]{:S(2)}) copy-start(s32[8,64,128]{2,1,0:T(8,128)} %refs_6_.1) | copy-start | bytes 786436
  0.6 2.0 %copy-start.7 = (s32[8,64,128]{2,1,0:T(8,128)S(1)}, s32[8,64,128]{2,1,0:T(8,128)}, u32[]{:S(2)}) copy-start(s32[8,64,128]{2,1,0:T(8,128)} %refs_7_.1) | copy-start | bytes 786436
  0.7 2.0 %copy-start.5 = (f32[8,64,128]{2,1,0:T(8,128)S(1)}, f32[8,64,128]{2,1,0:T(8,128)}, u32[]{:S(2)}) copy-start(f32[8,64,128]{2,1,0:T(8,128)} %refs_5_.1) | copy-start | bytes 786436
  0.7 2.0 %copy-start.4 = (f32[8,64,128]{2,1,0:T(8,128)S(1)}, f32[8,64,128]{2,1,0:T(8,128)}, u32[]{:S(2)}) copy-start(f32[8,64,128]{2,1,0:T(8,128)} %refs_4_.1) | copy-start | bytes 786436
  0.7 2.0 %copy-start.3 = (f32[8,64,128]{2,1,0:T(8,128)S(1)}, f32[8,64,128]{2,1,0:T(8,128)}, u32[]{:S(2)}) copy-start(f32[8,64,128]{2,1,0:T(8,128)} %refs_3_.1) | copy-start | bytes 786436
  0.7 2.0 %copy-start.2 = (f32[8,64,128]{2,1,0:T(8,128)S(1)}, f32[8,64,128]{2,1,0:T(8,128)}, u32[]{:S(2)}) copy-start(f32[8,64,128]{2,1,0:T(8,128)} %refs_2_.1) | copy-start | bytes 786436
  0.7 2.0 %copy-start.1 = (f32[8,64,128]{2,1,0:T(8,128)S(1)}, f32[8,64,128]{2,1,0:T(8,128)}, u32[]{:S(2)}) copy-start(f32[8,64,128]{2,1,0:T(8,128)} %refs_1_.1) | copy-start | bytes 786436
  0.7 2.0 %copy-start = (f32[8,64,128]{2,1,0:T(8,128)S(1)}, f32[8,64,128]{2,1,0:T(8,128)}, u32[]{:S(2)}) copy-start(f32[8,64,128]{2,1,0:T(8,128)} %refs_0_.1) | copy-start | bytes 786436
  2.9 15.0 %collective-permute-start.16 = (f32[20,64,128]{2,1,0:T(8,128)S(1)}, f32[20,64,128]{2,1,0:T(8,128)S(1)}, u32[]{:S(2)}, u32[]{:S(2)}) collective-permute-start(f32[20,64,128]{2,1,0:T(8,128)S(1)} %get-tuple-element.183), channel_id=1, source_target_pairs={{2,0},{3,1},{4,2},{5,3},{6,4},{7,5},{8,6},{9,7},{10,8},{11,9},{12,... | collective-permute-start | bytes 1966088 | tf_op jit(solution)/shard_map/cond/branch_3_fun/ppermute | solution.py:725
  5.6 5.5 %collective-permute-start.15 = (f32[32,8,128]{2,1,0:T(8,128)S(1)}, f32[32,8,128]{2,1,0:T(8,128)S(1)}, u32[]{:S(2)}, u32[]{:S(2)}) collective-permute-start(f32[32,8,128]{2,1,0:T(8,128)S(1)} %edges.7.refs_8_), channel_id=1, source_target_pairs={{0,1},{1,0},{2,3},{3,2},{4,5},{5,4},{6,7},{7,6},{8,9},{9,8},{10,11... | collective-permute-start | bytes 393224 | tf_op jit(solution)/shard_map/cond/branch_3_fun/ppermute | solution.py:725
  6.9 9.6 %collective-permute-start.17 = (f32[2,64,128]{2,1,0:T(8,128)S(1)}, f32[2,64,128]{2,1,0:T(8,128)S(1)}, u32[]{:S(2)}, u32[]{:S(2)}) collective-permute-start(f32[2,64,128]{2,1,0:T(8,128)S(1)} %lift.7), channel_id=1, source_target_pairs={{0,2},{1,3},{2,4},{3,5},{4,6},{5,7},{6,8},{7,9},{8,10},{9,11},{10,... | collective-permute-start | bytes 196616 | tf_op jit(solution)/shard_map/cond/branch_3_fun/ppermute | solution.py:725
  11.4 6.5 %collective-permute-start.19 = (f32[16,8,128]{2,1,0:T(8,128)S(1)}, f32[16,8,128]{2,1,0:T(8,128)S(1)}, u32[]{:S(2)}, u32[]{:S(2)}) collective-permute-start(f32[16,8,128]{2,1,0:T(8,128)S(1)} %get-tuple-element.185), channel_id=1, source_target_pairs={{2,4},{3,5},{4,2},{5,3},{6,8},{7,9},{8,6},{9,7},{10,12},{11,13},{1... | collective-permute-start | bytes 196616 | tf_op jit(solution)/shard_map/cond/branch_3_fun/ppermute | solution.py:725
  14.9 3.0 %collective-permute-start.18 = (f32[17,8,128]{2,1,0:T(8,128)S(1)}, f32[17,8,128]{2,1,0:T(8,128)S(1)}, u32[]{:S(2)}, u32[]{:S(2)}) collective-permute-start(f32[17,8,128]{2,1,0:T(8,128)S(1)} %get-tuple-element.184), channel_id=1, source_target_pairs={{0,2},{1,3},{2,0},{3,1},{4,6},{5,7},{6,4},{7,5},{8,10},{9,11},{10,... | collective-permute-start | bytes 208904 | tf_op jit(solution)/shard_map/cond/branch_3_fun/ppermute | solution.py:725

commit v11 on v10

--- a/solution.py
+++ b/solution.py
@@ -115,20 +115,27 @@
         return self.kept(es)[0]
 
 
-def far_traces(flat, case, second_move, field, code, bunch, codes_ready=lambda: None):
+def far_traces(flat, case, second_move, field, code, bunch, ready=lambda arrays: None):
     far, first_move = case
     lowest = far - 1 if far == 1 else far - 2
-    folded, now_b = {}, {}
+    ready((EX, EY, ES))
+    zeros, above_terms, own_terms, spin = (0.0, 0.0), {}, {}, {}
     for plane in range(lowest, far + 2):
-        above = field(EX, plane + 1), field(EY, plane + 1)
-        folded[plane] = flat.add_above(field(BX, plane), field(BY, plane), *above)
-        fields = field(EX, plane), field(EY, plane), field(ES, plane)
-        now_b[plane] = flat.radial_vertical(*folded[plane], *fields)
-    codes_ready()
+        ex, ey = field(EX, plane), field(EY, plane)
+        above_terms[plane] = flat.add_above(*zeros, field(EX, plane + 1), field(EY, plane + 1))
+        own_terms[plane] = flat.radial_vertical(*above_terms[plane], ex, ey, field(ES, plane))
+        if plane > lowest:
+            spin[plane] = flat.longitudinal(0.0, ex, ey)
+    ready((BX, BY, BS))
+    now_b = {}
+    for plane in range(lowest, far + 2):
+        now_b[plane] = [field(a, plane) + v for a, v in zip((BX, BY), own_terms[plane])]
+    folded = [field(a, far - 1) + v for a, v in zip((BX, BY), above_terms[far - 1])]
+    ready((CODES, BUNCH))
     now_e, now_es, now_bs = {}, {}, {}
     for plane in range(lowest + 1, far + 2):
         ex, ey = field(EX, plane), field(EY, plane)
-        now_bs[plane] = flat.longitudinal(field(BS, plane), ex, ey)
+        now_bs[plane] = field(BS, plane) + spin[plane]
         factors = coefficients(code(plane - first_move))
         over = [up - under for up, under in zip(now_b[plane], now_b[plane - 1])]
         now_e[plane] = flat.electric(ex, ey, now_bs[plane], *over, factors)
@@ -146,7 +153,7 @@
         over = [up - under for up, under in zip(over, second(far - 1))]
     bs = flat.longitudinal(now_bs[far], *now_e[far])
     factors = coefficients(code(far - first_move - second_move))
-    return folded[far - 1], (*now_e[far], *flat.electric(*now_e[far], bs, *over, factors))
+    return folded, (*now_e[far], *flat.electric(*now_e[far], bs, *over, factors))
 
 
 def near_traces(flat, case, planes, field, code, bunch):
@@ -190,9 +197,6 @@
     which[0] = case_index
 
     flat = Plane(gx * width, width, depth, total)
-    for item in copies[:6]:
-        item.wait()
-
     for c, case in enumerate(CASES):
         down = sent[c]
         downs = down_counts(case)
@@ -202,8 +206,6 @@
         @pl.when(case_index == c)
         def _():
             field = lambda a, plane: near[a, plane]
-            for a in range(6):
-                down[pl.ds(at[a], far)] = near[a, :far]
 
             folded, traces = far_traces(
                 flat,
@@ -212,8 +214,10 @@
                 field,
                 lambda plane: near_int[0, plane],
                 lambda plane: near_int[1, plane],
-                lambda: [item.wait() for item in copies[6:]],
+                lambda arrays: [copies[a].wait() for a in arrays],
             )
+            for a in range(6):
+                down[pl.ds(at[a], far)] = near[a, :far]
             down[at[BX] + far - 1], down[at[BY] + far - 1] = folded
             place = at[-1]
             for v in traces:

time: 20.8 us -> 20.6 us (level)
  the two profiles are of different devices: /device:TPU:5 before, /device:TPU:1 now
where the time goes in v11:
time: 20.6 us; the launch traced here: 20.3 us
  starting transfers between devices  12.4 us (60%)
  Pallas kernels  6.08 us (30%)
  between operations  0.96 us (5%)
  loops' own time  0.51 us (2%)
  waiting for transfers between devices  0.32 us (2%)
    ppermute x5, starting transfers between devices, passed(): return lax.ppermute(block, ('gz', 'gx'), route)  12.4 us
    pallas_call x1, Pallas kernels, advance(): pl.pallas_call(functools.partial(steps_kernel, case, n_sides, planes, wid...  2.3 us
    pallas_call x1, Pallas kernels, pack(): pl.pallas_call(pack_kernel, out_shape=shapes, in_specs=[ANY] * 9, out_spe...  1.78 us
    pallas_call x1, Pallas kernels, prepare(): pl.pallas_call(functools.partial(prepare_kernel, moves, len(beside)), out...  1.53 us
    another operation x1, loops' own time, on_device(): lax.switch(which[0], [functools.partial(run, c) for c in range(len(CASES)...  0.51 us
  transfers between devices with their start and end apart: 5, of which 1 were waited for; matrix products, arithmetic and copies ran while one was open for 0% of the time, Pallas kernels for 10%

profile of v11, /device:TPU:1, one launch (start us, length us, event | category | flops | bytes accessed | tf_op | source)
XLA Modules:
  0.0 20.3 jit_solution(1188133165017681677)
XLA Ops:
  0.6 0.0 copy-start.6
  0.6 0.0 copy-start.7
  0.7 0.0 copy-start.5
  0.7 0.0 copy-start.4
  0.7 0.0 copy-start.3
  0.7 0.0 copy-start.2
  0.7 0.0 copy-start.1
  0.7 0.0 copy-start
  0.7 1.8 %pack.1 = (s32[1]{0:T(128)S(4)}, s32[3]{0:T(128)S(4)}, f32[11,64,128]{2,1,0:T(8,128)S(1)}, f32[13,64,128]{2,1,0:T(8,128)S(1)}, f32[18,64,128]{2,1,0:T(8,128)S(1)}, /*index=5*/f32[20,64,128]{2,1,0:T(8,128)S(1)}) custom-call(f32[8,64,128]{2,1,0:T(8,128)} %refs_0_.1, f32[8,64,128]{2,1,0:T(8,128)} %refs_1_.1, f32[8,64,128]{2,1,0:T(8,128)} %refs_2_.1, ...), custom_call_target="tpu_custom_call" | custom-call | tf_op jit(solution)/shard_map/pack/pallas_call | solution.py:239
  2.6 17.5 %conditional.1 = (f32[8,64,128]{2,1,0:T(8,128)}, f32[8,64,128]{2,1,0:T(8,128)}, f32[8,64,128]{2,1,0:T(8,128)}, f32[8,64,128]{2,1,0:T(8,128)}, f32[8,64,128]{2,1,0:T(8,128)}, /*index=5*/f32[8,64,128]{2,1,0:T(8,128)}) conditional(s32[]{:T(128)} %bitcast, (f32[8,64,128]{2,1,0:T(8,128)S(1)}, f32[8,64,128]{2,1,0:T(8,128)S(1)}, ...), branch_computations={%region_0.0_spmd, %region_1.0_spmd, %region_2.0_spmd, %region_3.0_... | conditional | flops 2209999872 | bytes 23948792 | solution.py:751
  2.6 2.0 %collective-permute-start.11 = (f32[18,64,128]{2,1,0:T(8,128)S(1)}, f32[18,64,128]{2,1,0:T(8,128)S(1)}, u32[]{:S(2)}, u32[]{:S(2)}) collective-permute-start(f32[18,64,128]{2,1,0:T(8,128)S(1)} %get-tuple-element.155), channel_id=1, source_target_pairs={{2,0},{3,1},{4,2},{5,3},{6,4},{7,5},{8,6},{9,7},{10,8},{11,9},{12,... | collective-permute-start | bytes 1769480 | tf_op jit(solution)/shard_map/cond/branch_2_fun/ppermute | solution.py:729
  4.6 2.7 %collective-permute-start.10 = (f32[32,8,128]{2,1,0:T(8,128)S(1)}, f32[32,8,128]{2,1,0:T(8,128)S(1)}, u32[]{:S(2)}, u32[]{:S(2)}) collective-permute-start(f32[32,8,128]{2,1,0:T(8,128)S(1)} %edges.6.refs_8_), channel_id=1, source_target_pairs={{0,1},{1,0},{2,3},{3,2},{4,5},{5,4},{6,7},{7,6},{8,9},{9,8},{10,11... | collective-permute-start | bytes 393224 | tf_op jit(solution)/shard_map/cond/branch_2_fun/ppermute | solution.py:729
  7.4 0.1 lift.6
  7.5 3.3 %collective-permute-start.12 = (f32[4,64,128]{2,1,0:T(8,128)S(1)}, f32[4,64,128]{2,1,0:T(8,128)S(1)}, u32[]{:S(2)}, u32[]{:S(2)}) collective-permute-start(f32[4,64,128]{2,1,0:T(8,128)S(1)} %lift.6), channel_id=1, source_target_pairs={{0,2},{1,3},{2,4},{3,5},{4,6},{5,7},{6,8},{7,9},{8,10},{9,11},{10,... | collective-permute-start | bytes 393224 | tf_op jit(solution)/shard_map/cond/branch_2_fun/ppermute | solution.py:729
  10.8 0.0 collective-permute-done.10.refs_8_
  10.8 0.3 %relay.6 = (f32[17,8,128]{2,1,0:T(8,128)S(1)}, f32[16,8,128]{2,1,0:T(8,128)S(1)}) custom-call(s32[3]{0:T(128)S(4)} %get-tuple-element.136.moved, f32[8,64,128]{2,1,0:T(8,128)S(1)} %get-tuple-element.137.refs_0_, f32[8,64,128]{2,1,0:T(8,128)S(1)} %get-tuple-element.138.refs_1_, f32[8,64,128]{2,1,0:T(8,128)S(1)} %get-tuple-element.139.refs_2_, ...), custom_call_target="tpu_custom_call" | custom-call | tf_op jit(solution)/shard_map/cond/branch_2_fun/relay/pallas_call | solution.py:408
  11.1 4.3 %collective-permute-start.14 = (f32[16,8,128]{2,1,0:T(8,128)S(1)}, f32[16,8,128]{2,1,0:T(8,128)S(1)}, u32[]{:S(2)}, u32[]{:S(2)}) collective-permute-start(f32[16,8,128]{2,1,0:T(8,128)S(1)} %get-tuple-element.157), channel_id=1, source_target_pairs={{2,4},{3,5},{4,2},{5,3},{6,8},{7,9},{8,6},{9,7},{10,12},{11,13},{1... | collective-permute-start | bytes 196616 | tf_op jit(solution)/shard_map/cond/branch_2_fun/ppermute | solution.py:729
  15.4 0.1 collective-permute-start.13
  15.5 1.5 %prepare.6 = (f32[12,72,128]{2,1,0:T(8,128)S(1)}, f32[12,72,128]{2,1,0:T(8,128)S(1)}, f32[12,72,128]{2,1,0:T(8,128)S(1)}, f32[12,72,128]{2,1,0:T(8,128)S(1)}, f3...) custom-call(s32[3]{0:T(128)S(4)} %get-tuple-element.136.moved, ...), custom_call_target="tpu_custom_call" | custom-call | flops 2200000000 | bytes 10000000 | tf_op jit(solution)/shard_map/cond/branch_2_fun/prepare/pallas_call | solution.py:551
  17.1 0.0 collective-permute-done.12.refs_11_
  17.1 0.3 %collective-permute-done.14.refs_13_ = f32[16,8,128]{2,1,0:T(8,128)S(1)} collective-permute-done((f32[16,8,128]{2,1,0:T(8,128)S(1)}, f32[16,8,128]{2,1,0:T(8,128)S(1)}, u32[]{:S(2)}, u32[]{:S(2)}) %collective-permute-start.14) | collective-permute-done | bytes 65568 | tf_op jit(solution)/shard_map/cond/branch_2_fun/ppermute | solution.py:729
  17.4 0.0 collective-permute-done.13.refs_12_
  17.4 0.0 collective-permute-done.11.refs_10_
  17.4 2.3 %steps.6 = (f32[8,64,128]{2,1,0:T(8,128)}, f32[8,64,128]{2,1,0:T(8,128)}, f32[8,64,128]{2,1,0:T(8,128)}, f32[8,64,128]{2,1,0:T(8,128)}, f32[8,64,128]{2,1,0:T(8,...) custom-call(s32[3]{0:T(128)S(4)} %get-tuple-element.136.moved, ...), custom_call_target="tpu_custom_call", output_to_operand_aliasing={{6}: (1, {}), {7}: (2, {}), {8}: (3, {}), {9}: (4, {}), {10... | custom-call | tf_op jit(solution)/shard_map/cond/branch_2_fun/steps/pallas_call | solution.py:707
  (9 shorter events, 0.1 us)
Async XLA Ops:
  0.6 1.9 %copy-start.6 = (s32[8,64,128]{2,1,0:T(8,128)S(1)}, s32[8,64,128]{2,1,0:T(8,128)}, u32[]{:S(2)}) copy-start(s32[8,64,128]{2,1,0:T(8,128)} %refs_6_.1) | copy-start | bytes 786436
  0.6 1.9 %copy-start.7 = (s32[8,64,128]{2,1,0:T(8,128)S(1)}, s32[8,64,128]{2,1,0:T(8,128)}, u32[]{:S(2)}) copy-start(s32[8,64,128]{2,1,0:T(8,128)} %refs_7_.1) | copy-start | bytes 786436
  0.7 1.9 %copy-start.5 = (f32[8,64,128]{2,1,0:T(8,128)S(1)}, f32[8,64,128]{2,1,0:T(8,128)}, u32[]{:S(2)}) copy-start(f32[8,64,128]{2,1,0:T(8,128)} %refs_5_.1) | copy-start | bytes 786436
  0.7 1.9 %copy-start.4 = (f32[8,64,128]{2,1,0:T(8,128)S(1)}, f32[8,64,128]{2,1,0:T(8,128)}, u32[]{:S(2)}) copy-start(f32[8,64,128]{2,1,0:T(8,128)} %refs_4_.1) | copy-start | bytes 786436
  0.7 1.9 %copy-start.3 = (f32[8,64,128]{2,1,0:T(8,128)S(1)}, f32[8,64,128]{2,1,0:T(8,128)}, u32[]{:S(2)}) copy-start(f32[8,64,128]{2,1,0:T(8,128)} %refs_3_.1) | copy-start | bytes 786436
  0.7 1.9 %copy-start.2 = (f32[8,64,128]{2,1,0:T(8,128)S(1)}, f32[8,64,128]{2,1,0:T(8,128)}, u32[]{:S(2)}) copy-start(f32[8,64,128]{2,1,0:T(8,128)} %refs_2_.1) | copy-start | bytes 786436
  0.7 1.9 %copy-start.1 = (f32[8,64,128]{2,1,0:T(8,128)S(1)}, f32[8,64,128]{2,1,0:T(8,128)}, u32[]{:S(2)}) copy-start(f32[8,64,128]{2,1,0:T(8,128)} %refs_1_.1) | copy-start | bytes 786436
  0.7 1.9 %copy-start = (f32[8,64,128]{2,1,0:T(8,128)S(1)}, f32[8,64,128]{2,1,0:T(8,128)}, u32[]{:S(2)}) copy-start(f32[8,64,128]{2,1,0:T(8,128)} %refs_0_.1) | copy-start | bytes 786436
  2.6 14.8 %collective-permute-start.11 = (f32[18,64,128]{2,1,0:T(8,128)S(1)}, f32[18,64,128]{2,1,0:T(8,128)S(1)}, u32[]{:S(2)}, u32[]{:S(2)}) collective-permute-start(f32[18,64,128]{2,1,0:T(8,128)S(1)} %get-tuple-element.155), channel_id=1, source_target_pairs={{2,0},{3,1},{4,2},{5,3},{6,4},{7,5},{8,6},{9,7},{10,8},{11,9},{12,... | collective-permute-start | bytes 1769480 | tf_op jit(solution)/shard_map/cond/branch_2_fun/ppermute | solution.py:729
  4.6 6.1 %collective-permute-start.10 = (f32[32,8,128]{2,1,0:T(8,128)S(1)}, f32[32,8,128]{2,1,0:T(8,128)S(1)}, u32[]{:S(2)}, u32[]{:S(2)}) collective-permute-start(f32[32,8,128]{2,1,0:T(8,128)S(1)} %edges.6.refs_8_), channel_id=1, source_target_pairs={{0,1},{1,0},{2,3},{3,2},{4,5},{5,4},{6,7},{7,6},{8,9},{9,8},{10,11... | collective-permute-start | bytes 393224 | tf_op jit(solution)/shard_map/cond/branch_2_fun/ppermute | solution.py:729
  7.5 9.6 %collective-permute-start.12 = (f32[4,64,128]{2,1,0:T(8,128)S(1)}, f32[4,64,128]{2,1,0:T(8,128)S(1)}, u32[]{:S(2)}, u32[]{:S(2)}) collective-permute-start(f32[4,64,128]{2,1,0:T(8,128)S(1)} %lift.6), channel_id=1, source_target_pairs={{0,2},{1,3},{2,4},{3,5},{4,6},{5,7},{6,8},{7,9},{8,10},{9,11},{10,... | collective-permute-start | bytes 393224 | tf_op jit(solution)/shard_map/cond/branch_2_fun/ppermute | solution.py:729
  11.1 6.2 %collective-permute-start.14 = (f32[16,8,128]{2,1,0:T(8,128)S(1)}, f32[16,8,128]{2,1,0:T(8,128)S(1)}, u32[]{:S(2)}, u32[]{:S(2)}) collective-permute-start(f32[16,8,128]{2,1,0:T(8,128)S(1)} %get-tuple-element.157), channel_id=1, source_target_pairs={{2,4},{3,5},{4,2},{5,3},{6,8},{7,9},{8,6},{9,7},{10,12},{11,13},{1... | collective-permute-start | bytes 196616 | tf_op jit(solution)/shard_map/cond/branch_2_fun/ppermute | solution.py:729
  15.4 1.9 %collective-permute-start.13 = (f32[17,8,128]{2,1,0:T(8,128)S(1)}, f32[17,8,128]{2,1,0:T(8,128)S(1)}, u32[]{:S(2)}, u32[]{:S(2)}) collective-permute-start(f32[17,8,128]{2,1,0:T(8,128)S(1)} %get-tuple-element.156), channel_id=1, source_target_pairs={{0,2},{1,3},{2,0},{3,1},{4,6},{5,7},{6,4},{7,5},{8,10},{9,11},{10,... | collective-permute-start | bytes 208904 | tf_op jit(solution)/shard_map/cond/branch_2_fun/ppermute | solution.py:729

commit v12 on v11

--- a/solution.py
+++ b/solution.py
@@ -680,7 +680,7 @@
             cells.electric(*low_part, moved_now)
             cells.electric(top - t, above, moved_now)
         else:
-            cut = above // 2
+            cut = (2 * above + 2) // 3
             for start, count in ((top - 2, cut), (top - 2 + cut, above - cut), low_part):
                 cells.electric(start, count, moved_now)
                 for a in (EX, EY, ES):

time: 20.6 us -> 20.4 us (level)
  the two profiles are of different devices: /device:TPU:1 before, /device:TPU:5 now
where the time goes in v12:
time: 20.4 us; the launch traced here: 20.2 us
  starting transfers between devices  11.4 us (56%)
  Pallas kernels  6.06 us (30%)
  waiting for transfers between devices  1.44 us (7%)
  between operations  0.95 us (5%)
  loops' own time  0.3 us (1%)
    ppermute x5, starting transfers between devices, passed(): return lax.ppermute(block, ('gz', 'gx'), route)  11.4 us
    pallas_call x1, Pallas kernels, advance(): pl.pallas_call(functools.partial(steps_kernel, case, n_sides, planes, wid...  2.19 us
    pallas_call x1, Pallas kernels, pack(): pl.pallas_call(pack_kernel, out_shape=shapes, in_specs=[ANY] * 9, out_spe...  1.75 us
    pallas_call x1, Pallas kernels, prepare(): pl.pallas_call(functools.partial(prepare_kernel, moves, len(beside)), out...  1.51 us
    ppermute x5, waiting for transfers between devices, passed(): return lax.ppermute(block, ('gz', 'gx'), route)  1.44 us
  transfers between devices with their start and end apart: 5, of which 1 were waited for; matrix products, arithmetic and copies ran while one was open for 0% of the time, Pallas kernels for 10%

profile of v12, /device:TPU:5, one launch (start us, length us, event | category | flops | bytes accessed | tf_op | source)
XLA Modules:
  0.0 20.2 jit_solution(14430536775465019396)
XLA Ops:
  0.7 1.8 %pack.1 = (s32[1]{0:T(128)S(4)}, s32[3]{0:T(128)S(4)}, f32[11,64,128]{2,1,0:T(8,128)S(1)}, f32[13,64,128]{2,1,0:T(8,128)S(1)}, f32[18,64,128]{2,1,0:T(8,128)S(1)}, /*index=5*/f32[20,64,128]{2,1,0:T(8,128)S(1)}) custom-call(f32[8,64,128]{2,1,0:T(8,128)} %refs_0_.1, f32[8,64,128]{2,1,0:T(8,128)} %refs_1_.1, f32[8,64,128]{2,1,0:T(8,128)} %refs_2_.1, ...), custom_call_target="tpu_custom_call" | custom-call | tf_op jit(solution)/shard_map/pack/pallas_call | solution.py:239
  2.5 0.0 copy-done.6
  2.5 0.0 copy-done.7
  2.5 0.0 copy-done.5
  2.5 0.0 copy-done.4
  2.5 0.0 copy-done.3
  2.5 0.0 copy-done.2
  2.5 0.0 copy-done.1
  2.6 0.0 copy-done
  2.6 17.5 %conditional.1 = (f32[8,64,128]{2,1,0:T(8,128)}, f32[8,64,128]{2,1,0:T(8,128)}, f32[8,64,128]{2,1,0:T(8,128)}, f32[8,64,128]{2,1,0:T(8,128)}, f32[8,64,128]{2,1,0:T(8,128)}, /*index=5*/f32[8,64,128]{2,1,0:T(8,128)}) conditional(s32[]{:T(128)} %bitcast, (f32[8,64,128]{2,1,0:T(8,128)S(1)}, f32[8,64,128]{2,1,0:T(8,128)S(1)}, ...), branch_computations={%region_0.0_spmd, %region_1.0_spmd, %region_2.0_spmd, %region_3.0_... | conditional | flops 2209999872 | bytes 23948792 | solution.py:751
  2.6 2.6 %collective-permute-start.6 = (f32[13,64,128]{2,1,0:T(8,128)S(1)}, f32[13,64,128]{2,1,0:T(8,128)S(1)}, u32[]{:S(2)}, u32[]{:S(2)}) collective-permute-start(f32[13,64,128]{2,1,0:T(8,128)S(1)} %get-tuple-element.127), channel_id=1, source_target_pairs={{2,0},{3,1},{4,2},{5,3},{6,4},{7,5},{8,6},{9,7},{10,8},{11,9},{12,... | collective-permute-start | bytes 1277960 | tf_op jit(solution)/shard_map/cond/branch_1_fun/ppermute | solution.py:729
  5.2 1.3 %collective-permute-start.5 = (f32[32,8,128]{2,1,0:T(8,128)S(1)}, f32[32,8,128]{2,1,0:T(8,128)S(1)}, u32[]{:S(2)}, u32[]{:S(2)}) collective-permute-start(f32[32,8,128]{2,1,0:T(8,128)S(1)} %edges.5.refs_8_), channel_id=1, source_target_pairs={{0,1},{1,0},{2,3},{3,2},{4,5},{5,4},{6,7},{7,6},{8,9},{9,8},{10,11... | collective-permute-start | bytes 393224 | tf_op jit(solution)/shard_map/cond/branch_1_fun/ppermute | solution.py:729
  6.5 0.2 %lift.5 = f32[6,64,128]{2,1,0:T(8,128)S(1)} custom-call(f32[8,64,128]{2,1,0:T(8,128)S(1)} %get-tuple-element.109.refs_0_, f32[8,64,128]{2,1,0:T(8,128)S(1)} %get-tuple-element.110.refs_1_, f32[8,64,128]{2,1,0:T(8,128)S(1)} %get-tuple-element.111.refs_2_, f32[8,64,128]{2,1,0:T(8,128)S(1)} %get-tuple-element.112.refs_3_, ...), custom_call_target="tpu_custom_call" | custom-call | flops 10000000 | bytes 10000000 | tf_op jit(solution)/shard_map/cond/branch_1_fun/lift/pallas_call | solution.py:315
  6.7 4.2 %collective-permute-start.7 = (f32[6,64,128]{2,1,0:T(8,128)S(1)}, f32[6,64,128]{2,1,0:T(8,128)S(1)}, u32[]{:S(2)}, u32[]{:S(2)}) collective-permute-start(f32[6,64,128]{2,1,0:T(8,128)S(1)} %lift.5), channel_id=1, source_target_pairs={{0,2},{1,3},{2,4},{3,5},{4,6},{5,7},{6,8},{7,9},{8,10},{9,11},{10,... | collective-permute-start | bytes 589832 | tf_op jit(solution)/shard_map/cond/branch_1_fun/ppermute | solution.py:729
  10.9 0.0 collective-permute-done.5.refs_8_
  10.9 0.3 %relay.5 = (f32[14,8,128]{2,1,0:T(8,128)S(1)}, f32[13,8,128]{2,1,0:T(8,128)S(1)}) custom-call(s32[3]{0:T(128)S(4)} %get-tuple-element.108.moved, f32[8,64,128]{2,1,0:T(8,128)S(1)} %get-tuple-element.109.refs_0_, f32[8,64,128]{2,1,0:T(8,128)S(1)} %get-tuple-element.110.refs_1_, f32[8,64,128]{2,1,0:T(8,128)S(1)} %get-tuple-element.111.refs_2_, ...), custom_call_target="tpu_custom_call" | custom-call | tf_op jit(solution)/shard_map/cond/branch_1_fun/relay/pallas_call | solution.py:408
  11.3 3.3 %collective-permute-start.9 = (f32[13,8,128]{2,1,0:T(8,128)S(1)}, f32[13,8,128]{2,1,0:T(8,128)S(1)}, u32[]{:S(2)}, u32[]{:S(2)}) collective-permute-start(f32[13,8,128]{2,1,0:T(8,128)S(1)} %get-tuple-element.129), channel_id=1, source_target_pairs={{2,4},{3,5},{4,2},{5,3},{6,8},{7,9},{8,6},{9,7},{10,12},{11,13},{1... | collective-permute-start | bytes 159752 | tf_op jit(solution)/shard_map/cond/branch_1_fun/ppermute | solution.py:729
  14.6 0.1 collective-permute-start.8
  14.7 1.5 %prepare.5 = (f32[12,72,128]{2,1,0:T(8,128)S(1)}, f32[12,72,128]{2,1,0:T(8,128)S(1)}, f32[12,72,128]{2,1,0:T(8,128)S(1)}, f32[12,72,128]{2,1,0:T(8,128)S(1)}, f3...) custom-call(s32[3]{0:T(128)S(4)} %get-tuple-element.108.moved, ...), custom_call_target="tpu_custom_call" | custom-call | flops 2200000000 | bytes 10000000 | tf_op jit(solution)/shard_map/cond/branch_1_fun/prepare/pallas_call | solution.py:551
  16.2 1.4 %collective-permute-done.9.refs_13_ = f32[13,8,128]{2,1,0:T(8,128)S(1)} collective-permute-done((f32[13,8,128]{2,1,0:T(8,128)S(1)}, f32[13,8,128]{2,1,0:T(8,128)S(1)}, u32[]{:S(2)}, u32[]{:S(2)}) %collective-permute-start.9) | collective-permute-done | bytes 53280 | tf_op jit(solution)/shard_map/cond/branch_1_fun/ppermute | solution.py:729
  17.6 0.0 collective-permute-done.8.refs_12_
  17.6 0.0 collective-permute-done.7.refs_11_
  17.6 0.0 collective-permute-done.6.refs_10_
  17.6 2.2 %steps.5 = (f32[8,64,128]{2,1,0:T(8,128)}, f32[8,64,128]{2,1,0:T(8,128)}, f32[8,64,128]{2,1,0:T(8,128)}, f32[8,64,128]{2,1,0:T(8,128)}, f32[8,64,128]{2,1,0:T(8,...) custom-call(s32[3]{0:T(128)S(4)} %get-tuple-element.108.moved, ...), custom_call_target="tpu_custom_call", output_to_operand_aliasing={{6}: (1, {}), {7}: (2, {}), {8}: (3, {}), {9}: (4, {}), {10... | custom-call | tf_op jit(solution)/shard_map/cond/branch_1_fun/steps/pallas_call | solution.py:707
  (9 shorter events, 0.1 us)
Async XLA Ops:
  0.6 1.8 %copy-start.6 = (s32[8,64,128]{2,1,0:T(8,128)S(1)}, s32[8,64,128]{2,1,0:T(8,128)}, u32[]{:S(2)}) copy-start(s32[8,64,128]{2,1,0:T(8,128)} %refs_6_.1) | copy-start | bytes 786436
  0.6 1.8 %copy-start.7 = (s32[8,64,128]{2,1,0:T(8,128)S(1)}, s32[8,64,128]{2,1,0:T(8,128)}, u32[]{:S(2)}) copy-start(s32[8,64,128]{2,1,0:T(8,128)} %refs_7_.1) | copy-start | bytes 786436
  0.7 1.8 %copy-start.5 = (f32[8,64,128]{2,1,0:T(8,128)S(1)}, f32[8,64,128]{2,1,0:T(8,128)}, u32[]{:S(2)}) copy-start(f32[8,64,128]{2,1,0:T(8,128)} %refs_5_.1) | copy-start | bytes 786436
  0.7 1.8 %copy-start.4 = (f32[8,64,128]{2,1,0:T(8,128)S(1)}, f32[8,64,128]{2,1,0:T(8,128)}, u32[]{:S(2)}) copy-start(f32[8,64,128]{2,1,0:T(8,128)} %refs_4_.1) | copy-start | bytes 786436
  0.7 1.8 %copy-start.3 = (f32[8,64,128]{2,1,0:T(8,128)S(1)}, f32[8,64,128]{2,1,0:T(8,128)}, u32[]{:S(2)}) copy-start(f32[8,64,128]{2,1,0:T(8,128)} %refs_3_.1) | copy-start | bytes 786436
  0.7 1.8 %copy-start.2 = (f32[8,64,128]{2,1,0:T(8,128)S(1)}, f32[8,64,128]{2,1,0:T(8,128)}, u32[]{:S(2)}) copy-start(f32[8,64,128]{2,1,0:T(8,128)} %refs_2_.1) | copy-start | bytes 786436
  0.7 1.8 %copy-start.1 = (f32[8,64,128]{2,1,0:T(8,128)S(1)}, f32[8,64,128]{2,1,0:T(8,128)}, u32[]{:S(2)}) copy-start(f32[8,64,128]{2,1,0:T(8,128)} %refs_1_.1) | copy-start | bytes 786436
  0.7 1.9 %copy-start = (f32[8,64,128]{2,1,0:T(8,128)S(1)}, f32[8,64,128]{2,1,0:T(8,128)}, u32[]{:S(2)}) copy-start(f32[8,64,128]{2,1,0:T(8,128)} %refs_0_.1) | copy-start | bytes 786436
  2.6 15.0 %collective-permute-start.6 = (f32[13,64,128]{2,1,0:T(8,128)S(1)}, f32[13,64,128]{2,1,0:T(8,128)S(1)}, u32[]{:S(2)}, u32[]{:S(2)}) collective-permute-start(f32[13,64,128]{2,1,0:T(8,128)S(1)} %get-tuple-element.127), channel_id=1, source_target_pairs={{2,0},{3,1},{4,2},{5,3},{6,4},{7,5},{8,6},{9,7},{10,8},{11,9},{12,... | collective-permute-start | bytes 1277960 | tf_op jit(solution)/shard_map/cond/branch_1_fun/ppermute | solution.py:729
  5.2 5.7 %collective-permute-start.5 = (f32[32,8,128]{2,1,0:T(8,128)S(1)}, f32[32,8,128]{2,1,0:T(8,128)S(1)}, u32[]{:S(2)}, u32[]{:S(2)}) collective-permute-start(f32[32,8,128]{2,1,0:T(8,128)S(1)} %edges.5.refs_8_), channel_id=1, source_target_pairs={{0,1},{1,0},{2,3},{3,2},{4,5},{5,4},{6,7},{7,6},{8,9},{9,8},{10,11... | collective-permute-start | bytes 393224 | tf_op jit(solution)/shard_map/cond/branch_1_fun/ppermute | solution.py:729
  6.7 10.9 %collective-permute-start.7 = (f32[6,64,128]{2,1,0:T(8,128)S(1)}, f32[6,64,128]{2,1,0:T(8,128)S(1)}, u32[]{:S(2)}, u32[]{:S(2)}) collective-permute-start(f32[6,64,128]{2,1,0:T(8,128)S(1)} %lift.5), channel_id=1, source_target_pairs={{0,2},{1,3},{2,4},{3,5},{4,6},{5,7},{6,8},{7,9},{8,10},{9,11},{10,... | collective-permute-start | bytes 589832 | tf_op jit(solution)/shard_map/cond/branch_1_fun/ppermute | solution.py:729
  11.3 6.4 %collective-permute-start.9 = (f32[13,8,128]{2,1,0:T(8,128)S(1)}, f32[13,8,128]{2,1,0:T(8,128)S(1)}, u32[]{:S(2)}, u32[]{:S(2)}) collective-permute-start(f32[13,8,128]{2,1,0:T(8,128)S(1)} %get-tuple-element.129), channel_id=1, source_target_pairs={{2,4},{3,5},{4,2},{5,3},{6,8},{7,9},{8,6},{9,7},{10,12},{11,13},{1... | collective-permute-start | bytes 159752 | tf_op jit(solution)/shard_map/cond/branch_1_fun/ppermute | solution.py:729
  14.6 3.0 %collective-permute-start.8 = (f32[14,8,128]{2,1,0:T(8,128)S(1)}, f32[14,8,128]{2,1,0:T(8,128)S(1)}, u32[]{:S(2)}, u32[]{:S(2)}) collective-permute-start(f32[14,8,128]{2,1,0:T(8,128)S(1)} %get-tuple-element.128), channel_id=1, source_target_pairs={{0,2},{1,3},{2,0},{3,1},{4,6},{5,7},{6,4},{7,5},{8,10},{9,11},{10,... | collective-permute-start | bytes 172040 | tf_op jit(solution)/shard_map/cond/branch_1_fun/ppermute | solution.py:729
